TPU v7x, 256 devices: a whole 4x4x8 slice. The times are simulated.
256 devices in a mesh: row: 8 (over z_hi, y), col: 32 (over x, z_lo, core).
Axes of the slice: x: 4, y: 4, z: 8 (z_hi: 2, z_lo: 4; z = z_hi * 4 + z_lo), core: 2. Of those that a mesh axis runs over, the one named last changes fastest.
Arguments:
- patches: bfloat16 [32768, 768], P(('row', 'col')), may hold values from -4 to 4
- tile_slot: int32 [32768], P(('row', 'col')), may hold values from 0 to 127, as said below
- w_embed: bfloat16 [768, 1024], replicated, may hold values from -0.21875 to 0.21875
- w_query: bfloat16 [1024, 1024], replicated, may hold values from -0.1875 to 0.1875
- w_keyval: bfloat16 [1024, 2048], replicated, may hold values from -0.1875 to 0.1875
- w_out: bfloat16 [1024, 1024], replicated, may hold values from -0.1875 to 0.1875
- cotangent: bfloat16 [128, 256, 1024], P('row', 'col'), may hold values from -6 to 6
Outputs:
- final_tokens: bfloat16 [128, 256, 1024], P('row', 'col')
- input_grad: bfloat16 [128, 256, 1024], P('row', 'col')
Inputs may be any that keep to these rules, and one draw needn't show every extreme that they name: `tile_slot`: row i of the 128 embedding rows held by the device at (row r, col c) goes to the core tile in grid tile row i // 16 and tile column c; for every core tile the slots named by its 8 sources are together each position 0 to 127 exactly once.
All inputs are finite; a program needn't handle non-finite values.
Results may differ from a plain program's by a relative error of at most 0.014.
Values may be sent and summed in bfloat16 or wider, within the bound.
No kernel may reach another device: no remote copies, remote signals or barrier semaphores. Data moves between devices by JAX's collectives and lax.ppermute only.
A program may use at most 192 MiB of HBM per device.

v0:
```python
import jax
import jax.numpy as jnp
from jax import lax
from jax.sharding import PartitionSpec as P

D = 1024
HEADS = 16


EPSILON = 1e-06


def extended_2(x, sides, width):
    for axis, dim in sides:
        peers, length = (lax.axis_size(axis), x.shape[dim])
        up = [(i, (i + 1) % peers) for i in range(peers - 1)]
        down = [(j, i) for i, j in up]
        last = lax.slice_in_dim(x, length - width, length, axis=dim)
        first = lax.slice_in_dim(x, 0, width, axis=dim)
        before = lax.ppermute(last, axis, up)
        after = lax.ppermute(first, axis, down)
        x = jnp.concatenate([before, x, after], axis=dim)
    return x


def rms_scale(values):
    return values * lax.rsqrt(jnp.mean(values * values, axis=-1, keepdims=True) + EPSILON)


def head_scale(values):
    shaped = values.reshape(values.shape[:-1] + (HEADS, D // HEADS))
    return rms_scale(shaped).reshape(values.shape)


def project_query(normed, w_query):
    flattened = normed.reshape(-1, D)
    projected = jnp.dot(flattened, w_query, preferred_element_type=jnp.float32)
    return head_scale(projected).astype(jnp.bfloat16).reshape(normed.shape)


def project_keyval(normed, w_keyval):
    flattened = normed.reshape(-1, D)
    projected = jnp.dot(flattened, w_keyval, preferred_element_type=jnp.float32)
    key_part = head_scale(projected[:, :D]).astype(jnp.bfloat16)
    value_part = projected[:, D:].astype(jnp.bfloat16)
    joined = jnp.concatenate([key_part, value_part], axis=1)
    return joined.reshape(normed.shape[:-1] + (2 * D,))


def prepare(residual, w_query):
    normed = rms_scale(residual).astype(jnp.bfloat16)
    return (normed, project_query(normed, w_query))


def split_pair(values):
    high_part = values.astype(jnp.bfloat16)
    low_part = (values - high_part.astype(jnp.float32)).astype(jnp.bfloat16)
    return (high_part, low_part)


def mixed_product(form, floats, halves):
    high_part, low_part = split_pair(floats)
    first = jnp.einsum(form, high_part, halves, preferred_element_type=jnp.float32)
    return first + jnp.einsum(form, low_part, halves, preferred_element_type=jnp.float32)


def offset_views(padded, offset, tile_rows):
    head_size = D // HEADS
    padded_cols = padded.shape[1]
    rows = padded[offset : offset + tile_rows]
    key_view = rows[..., :D].reshape(tile_rows, padded_cols, HEADS, head_size)
    value_view = rows[..., D:].reshape(tile_rows, padded_cols, HEADS, head_size)
    return (key_view, value_view)


def attend(queries, padded, window_mask):
    tile_rows, tile_cols = (queries.shape[0], queries.shape[1])
    head_size = D // HEADS
    padded_cols = padded.shape[1]
    query_heads = queries.reshape(tile_rows, tile_cols, HEADS, head_size)
    score_parts = []
    for offset in range(7):
        key_view, value_view = offset_views(padded, offset, tile_rows)
        score_parts.append(
            jnp.einsum("ijhe,ikhe->ijhk", query_heads, key_view, preferred_element_type=jnp.float32)
        )
    scores = jnp.concatenate(score_parts, axis=-1) * head_size ** (-0.5)
    weight = jnp.exp(scores) * window_mask[:, :, None, :]
    probs = weight / jnp.sum(weight, axis=-1, keepdims=True)
    output = jnp.zeros((tile_rows, tile_cols, HEADS, head_size), jnp.float32)
    for offset in range(7):
        key_view, value_view = offset_views(padded, offset, tile_rows)
        probs_part = probs[..., offset * padded_cols : (offset + 1) * padded_cols]
        output = output + mixed_product("ijhk,ikhe->ijhe", probs_part, value_view)
    return (output.reshape(tile_rows, tile_cols, D), probs)


def attend_back(queries, padded, probs, attended_back):
    tile_rows, tile_cols = (queries.shape[0], queries.shape[1])
    head_size = D // HEADS
    padded_cols = padded.shape[1]
    query_heads = queries.reshape(tile_rows, tile_cols, HEADS, head_size)
    output_back = attended_back.reshape(tile_rows, tile_cols, HEADS, head_size)
    back_parts = []
    for offset in range(7):
        key_view, value_view = offset_views(padded, offset, tile_rows)
        back_parts.append(
            jnp.einsum(
                "ijhe,ikhe->ijhk", output_back, value_view, preferred_element_type=jnp.float32
            )
        )
    probs_back = jnp.concatenate(back_parts, axis=-1)
    centred = probs_back - jnp.sum(probs_back * probs, axis=-1, keepdims=True)
    scores_back = probs * centred * head_size ** (-0.5)
    queries_back = jnp.zeros((tile_rows, tile_cols, HEADS, head_size), jnp.float32)
    key_total = jnp.zeros((tile_rows + 6, padded_cols, D), jnp.float32)
    value_total = jnp.zeros((tile_rows + 6, padded_cols, D), jnp.float32)
    for offset in range(7):
        key_view, value_view = offset_views(padded, offset, tile_rows)
        part_slice = slice(offset * padded_cols, (offset + 1) * padded_cols)
        scores_part = scores_back[..., part_slice]
        probs_part = probs[..., part_slice]
        queries_back = queries_back + mixed_product("ijhk,ikhe->ijhe", scores_part, key_view)
        key_part = mixed_product("ijhk,ijhe->ikhe", scores_part, query_heads).reshape(
            tile_rows, padded_cols, D
        )
        value_part = mixed_product("ijhk,ijhe->ikhe", probs_part, output_back).reshape(
            tile_rows, padded_cols, D
        )
        key_total = key_total.at[offset : offset + tile_rows].add(key_part)
        value_total = value_total.at[offset : offset + tile_rows].add(value_part)
    padded_back = jnp.concatenate([key_total, value_total], axis=-1)
    return (queries_back.reshape(tile_rows, tile_cols, D).astype(jnp.bfloat16), padded_back)


def project_out(residual, attended, w_out):
    update = jnp.dot(attended.reshape(-1, D), w_out, preferred_element_type=jnp.float32).reshape(
        residual.shape
    )
    return (residual + update).astype(jnp.bfloat16)


def finish(residual, queries, padded, w_out, window_mask):
    output, probs = attend(queries, padded, window_mask)
    return project_out(residual, output.astype(jnp.bfloat16), w_out)


def fold_rim(extended, along):
    interior = extended.shape[along] - 12
    leading = (slice(None),) * along
    middle = lax.slice_in_dim(extended, 6, interior + 6, axis=along)
    middle = middle.at[leading + (slice(0, 3),)].add(lax.slice_in_dim(extended, 0, 3, axis=along))
    return middle.at[leading + (slice(interior - 3, interior),)].add(
        lax.slice_in_dim(extended, interior + 9, interior + 12, axis=along)
    )


def on_device(patches, tile_slot, w_embed, w_query, w_keyval, w_out, cotangent):
    tile_rows, tile_cols = (cotangent.shape[0], cotangent.shape[1])
    row_count = lax.axis_size("row")
    col_count = lax.axis_size("col")
    tile_size = tile_rows * tile_cols
    per_source = tile_size // row_count
    slot_blocks = tile_slot.reshape(row_count, per_source)
    embedded = jnp.dot(patches, w_embed, preferred_element_type=jnp.float32).astype(jnp.bfloat16)
    arrived, slot_ids = (
        lax.all_to_all(
            embedded.reshape(row_count, per_source, D),
            "row",
            split_axis=0,
            concat_axis=0,
            tiled=True,
        ),
        lax.all_to_all(slot_blocks, "row", split_axis=0, concat_axis=0, tiled=True),
    )
    arrived = arrived.reshape(tile_size, D)
    current = jnp.zeros((tile_size, D), jnp.bfloat16).at[slot_ids.reshape(-1)].set(arrived)
    current = current.reshape(tile_rows, tile_cols, D)
    row_position = (
        lax.axis_index("row") * tile_rows - 3 + jnp.arange(tile_rows + 6, dtype=jnp.int32)
    )
    row_valid = ((row_position >= 0) & (row_position < tile_rows * row_count)).astype(jnp.float32)
    col_position = (
        lax.axis_index("col") * tile_cols - 3 + jnp.arange(tile_cols + 6, dtype=jnp.int32)
    )
    col_valid = ((col_position >= 0) & (col_position < tile_cols * col_count)).astype(jnp.float32)
    row_windows = jnp.stack([row_valid[offset : offset + tile_rows] for offset in range(7)], axis=1)
    query_col = jnp.arange(tile_cols, dtype=jnp.int32)[:, None]
    key_col = jnp.arange(tile_cols + 6, dtype=jnp.int32)[None, :]
    col_band = ((key_col >= query_col) & (key_col <= query_col + 6)).astype(
        jnp.float32
    ) * col_valid[None, :]
    window_mask = (row_windows[:, None, :, None] * col_band[None, :, None, :]).reshape(
        tile_rows, tile_cols, 7 * (tile_cols + 6)
    )

    def padded_keyval(interior_fn):
        return extended_2(interior_fn(), (("row", 0), ("col", 1)), 3)

    residual = current.astype(jnp.float32)
    normed, queries = prepare(residual, w_query)
    padded = padded_keyval(lambda: project_keyval(normed, w_keyval))
    current = finish(residual, queries, padded, w_out, window_mask)
    residual = current.astype(jnp.float32)
    (normed, queries), pull_prepare = jax.vjp(lambda values: prepare(values, w_query), residual)
    keyval, pull_keyval = jax.vjp(lambda values: project_keyval(values, w_keyval), normed)
    padded = padded_keyval(lambda: keyval)
    output, probs = attend(queries, padded, window_mask)
    attended = output.astype(jnp.bfloat16)
    final_tokens, pull_out = jax.vjp(
        lambda residual_in, attended_in: project_out(residual_in, attended_in, w_out),
        residual,
        attended,
    )
    residual_back, attended_back = pull_out(cotangent)
    queries_back, padded_back = attend_back(queries, padded, probs, attended_back)
    extended = extended_2(padded_back.astype(jnp.bfloat16), (("row", 0), ("col", 1)), 3).astype(
        padded_back.dtype
    )
    keyval_back = fold_rim(fold_rim(extended, 0), 1).astype(jnp.bfloat16)
    (normed_back,) = pull_keyval(keyval_back)
    (prepare_back,) = pull_prepare((normed_back, queries_back))
    input_grad = (residual_back + prepare_back).astype(jnp.bfloat16)
    return (final_tokens, input_grad)


def solution(mesh):
    in_specs = (
        P(("row", "col"), None),
        P(("row", "col")),
        P(),
        P(),
        P(),
        P(),
        P("row", "col", None),
    )
    out_specs = (P("row", "col", None), P("row", "col", None))
    return jax.shard_map(
        on_device, mesh=mesh, in_specs=in_specs, out_specs=out_specs, check_vma=False
    )
```

profile of v0, /device:TPU:30, one launch (start us, length us, event | category | flops | bytes accessed | tf_op | source)
XLA Modules:
  0.0 673.1 jit_solution(12114396999701982469)
XLA Ops:
  2.1 11.3 %all-to-all-start = ((s32[8,1,16]{2,1,0:T(1,128)}), s32[8,1,16]{2,1,0:T(1,128)S(1)}, u32[]{:S(2)}, u32[]{:S(2)}) async-start(s32[8,1,16]{2,1,0:T(1,128)} %bitcast), calls=%async_computation | async-start | bytes 8192 | tf_op jit(solution)/shard_map/all_to_all | solution.py:174
  17.0 4.4 all-to-all-done
  21.4 5.4 all-to-all-start.1
  26.8 3.9 copy.220
  52.5 9.3 %collective-permute-start = (bf16[3,8,2048]{2,0,1:T(4,128)(2,1)S(1)}, bf16[3,8,2048]{2,0,1:T(4,128)(2,1)S(1)}, u32[]{:S(2)}, u32[]{:S(2)}) collective-permute-start(bf16[3,8,2048]{2,0,1:T(4,128)(2,1)S(1)} %copy.217), channel_id=1, source_target_pairs={{0,32},{32,64},{64,96},{96,128},{128,160},{160,192},{192,224},{1,3... | collective-permute-start | bytes 294920 | tf_op jit(solution)/shard_map/ppermute | solution.py:20
  71.9 6.6 collective-permute-done.2
  80.0 3.4 fusion.244
  121.6 5.1 concatenate.76
  173.1 3.1 fusion.155
  188.8 10.4 %collective-permute-start.4 = (bf16[3,8,2048]{2,0,1:T(4,128)(2,1)S(1)}, bf16[3,8,2048]{2,0,1:T(4,128)(2,1)S(1)}, u32[]{:S(2)}, u32[]{:S(2)}) collective-permute-start(bf16[3,8,2048]{2,0,1:T(4,128)(2,1)S(1)} %copy.254), channel_id=1, source_target_pairs={{0,32},{32,64},{64,96},{96,128},{128,160},{160,192},{192,224},{1,3... | collective-permute-start | bytes 294920 | tf_op jit(solution)/shard_map/ppermute | solution.py:20
  209.2 6.7 collective-permute-done.6
  217.4 3.6 fusion.243
  224.4 3.2 convolution_bitcast_fusion.13
  246.5 5.8 concatenate.80
  281.0 3.1 fusion.104
  288.3 3.0 fusion.100
  295.7 3.0 fusion.96
  317.2 3.0 fusion.84
  321.9 5.5 concatenate.81
  361.4 3.1 add.563
  364.5 3.2 add_bitcast_fusion.5
  383.4 3.2 add_bitcast_fusion.3
  391.2 3.2 add_bitcast_fusion.2
  398.9 3.2 add_bitcast_fusion.1
  406.8 3.2 add_bitcast_fusion
  414.5 5.9 scatter-add.74
  423.2 5.9 scatter-add.75
  431.9 5.9 scatter-add.76
  440.6 5.9 scatter-add.79
  449.3 5.9 scatter-add.80
  458.0 5.9 scatter-add.81
  475.4 3.0 add_bitcast_fusion.12
  485.7 3.0 add_bitcast_fusion.11
  493.3 5.9 scatter-add.61
  501.9 6.0 scatter-add.64
  508.0 3.5 add_bitcast_fusion.10
  518.9 5.9 scatter-add.65
  524.8 3.5 add_bitcast_fusion.9
  535.6 5.9 scatter-add.66
  541.5 3.5 add_bitcast_fusion.8
  552.4 5.9 scatter-add.69
  558.3 3.5 add_bitcast_fusion.7
  569.1 5.9 scatter-add.70
  579.6 11.0 %collective-permute-start.8 = (bf16[3,14,2048]{2,0,1:T(4,128)(2,1)}, bf16[3,14,2048]{2,0,1:T(4,128)(2,1)}, u32[]{:S(2)}, u32[]{:S(2)}) collective-permute-start(bf16[3,14,2048]{2,0,1:T(4,128)(2,1)} %get-tuple-element.220), channel_id=1, source_target_pairs={{0,32},{32,64},{64,96},{96,128},{128,160},{160,192},{192,224},{1,3... | collective-permute-start | bytes 516104 | tf_op jit(solution)/shard_map/ppermute | solution.py:20
  627.4 3.3 collective-permute-done.10
  637.9 7.4 %scatter-add.84 = f32[16,20,2048]{2,0,1:T(8,128)} dynamic-update-slice(f32[16,20,2048]{2,0,1:T(8,128)} %slice.936, f32[3,20,2048]{2,0,1:T(4,128)} %convert_add_fusion.1, s32[]{:T(128)} %constant.467.clone.1, s32[]{:T(128)} %constant.467.clone.1, s32[]{:T(128)} %constant.467.clone.1) | dynamic-update-slice | bytes 983044 | tf_op jit(solution)/shard_map/scatter-add | solution.py:152
  647.9 6.7 scatter-add.85
  667.2 3.9 convolution_convert_fusion.3
  (502 shorter events, 429.1 us)
Async XLA Ops:
  0.6 15.5 %copy-start = (bf16[1024,1024]{1,0:T(8,128)(2,1)S(1)}, bf16[1024,1024]{1,0:T(8,128)(2,1)}, u32[]{:S(2)}) copy-start(bf16[1024,1024]{1,0:T(8,128)(2,1)} %param.48) | copy-start | bytes 6291460
  0.6 15.5 %copy-start.107 = (bf16[16,8,1024]{2,1,0:T(8,128)(2,1)S(1)}, bf16[16,8,1024]{2,1,0:T(8,128)(2,1)}, u32[]{:S(2)}) copy-start(bf16[16,8,1024]{2,1,0:T(8,128)(2,1)} %param.49) | copy-start | bytes 786436
  2.1 19.2 %all-to-all-start = ((s32[8,1,16]{2,1,0:T(1,128)}), s32[8,1,16]{2,1,0:T(1,128)S(1)}, u32[]{:S(2)}, u32[]{:S(2)}) async-start(s32[8,1,16]{2,1,0:T(1,128)} %bitcast), calls=%async_computation | async-start | bytes 8192 | tf_op jit(solution)/shard_map/all_to_all | solution.py:174
  21.4 14.3 %all-to-all-start.1 = ((bf16[8,16,1024]{2,1,0:T(8,128)(2,1)}), bf16[8,16,1024]{2,1,0:T(8,128)(2,1)S(1)}, u32[]{:S(2)}, u32[]{:S(2)}) async-start(bf16[8,16,1024]{2,1,0:T(8,128)(2,1)} %bitcast.2), calls=%async_computation.1 | async-start | bytes 524288 | tf_op jit(solution)/shard_map/all_to_all | solution.py:167
  32.3 95.8 %copy-start.104 = (f32[16,8,98]{2,1,0:T(8,128)}, f32[16,8,98]{2,1,0:T(8,128)S(1)}, u32[]{:S(2)}) copy-start(f32[16,8,98]{2,1,0:T(8,128)S(1)} %broadcast_multiply_fusion) | copy-start | bytes 150532
  47.6 14.2 %copy-start.27 = (bf16[1024,1024]{0,1:T(8,128)(2,1)S(1)}, bf16[1024,1024]{0,1:T(8,128)(2,1)}, u32[]{:S(2)}) copy-start(bf16[1024,1024]{0,1:T(8,128)(2,1)} %copy.220) | copy-start | bytes 6291460
  48.9 13.8 %copy-start.103 = (bf16[128,1024]{1,0:T(8,128)(2,1)S(1)}, bf16[128,1024]{1,0:T(8,128)(2,1)}, u32[]{:S(2)}) copy-start(bf16[128,1024]{1,0:T(8,128)(2,1)} %slice.1173) | copy-start | bytes 786436
  49.8 13.1 %collective-permute-start.1 = (bf16[3,8,2048]{2,0,1:T(4,128)(2,1)S(1)}, bf16[3,8,2048]{2,0,1:T(4,128)(2,1)S(1)}, u32[]{:S(2)}, u32[]{:S(2)}) collective-permute-start(bf16[3,8,2048]{2,0,1:T(4,128)(2,1)S(1)} %copy.218), channel_id=1, source_target_pairs={{32,0},{64,32},{96,64},{128,96},{160,128},{192,160},{224,192},{33,... | collective-permute-start | bytes 294920 | tf_op jit(solution)/shard_map/ppermute | solution.py:21
  52.5 11.8 %collective-permute-start = (bf16[3,8,2048]{2,0,1:T(4,128)(2,1)S(1)}, bf16[3,8,2048]{2,0,1:T(4,128)(2,1)S(1)}, u32[]{:S(2)}, u32[]{:S(2)}) collective-permute-start(bf16[3,8,2048]{2,0,1:T(4,128)(2,1)S(1)} %copy.217), channel_id=1, source_target_pairs={{0,32},{32,64},{64,96},{96,128},{128,160},{160,192},{192,224},{1,3... | collective-permute-start | bytes 294920 | tf_op jit(solution)/shard_map/ppermute | solution.py:20
  63.0 6.7 copy-start.109
  64.3 5.4 copy-start.110
  65.4 6.5 collective-permute-start.3
  67.3 11.2 %collective-permute-start.2 = (bf16[22,3,2048]{2,0,1:T(8,128)(2,1)}, bf16[22,3,2048]{2,0,1:T(8,128)(2,1)}, u32[]{:S(2)}, u32[]{:S(2)}) collective-permute-start(bf16[22,3,2048]{2,0,1:T(8,128)(2,1)} %get-tuple-element.252), channel_id=1, source_target_pairs={{0,1},{1,2},{2,3},{3,4},{4,5},{5,6},{6,7},{7,8},{8,9},{9,10},{10,1... | collective-permute-start | bytes 811016 | tf_op jit(solution)/shard_map/ppermute | solution.py:20
  172.5 4.7 copy-start.29
  173.1 4.1 copy-start.112
  173.1 4.1 copy-start.28
  176.2 9.2 %copy-start.64 = (f32[128,2048]{1,0:T(8,128)}, f32[128,2048]{1,0:T(8,128)S(1)}, u32[]{:S(2)}) copy-start(f32[128,2048]{1,0:T(8,128)S(1)} %fusion.155) | copy-start | bytes 3145732
  186.5 20.6 %copy-start.77 = (f32[128,16,64]{0,2,1:T(8,128)S(1)}, f32[128,16,64]{0,2,1:T(8,128)}, u32[]{:S(2)}) copy-start(f32[128,16,64]{0,2,1:T(8,128)} %get-tuple-element.270) | copy-start | bytes 1572868
  186.6 13.6 %collective-permute-start.5 = (bf16[3,8,2048]{2,0,1:T(4,128)(2,1)S(1)}, bf16[3,8,2048]{2,0,1:T(4,128)(2,1)S(1)}, u32[]{:S(2)}, u32[]{:S(2)}) collective-permute-start(bf16[3,8,2048]{2,0,1:T(4,128)(2,1)S(1)} %copy.255), channel_id=1, source_target_pairs={{32,0},{64,32},{96,64},{128,96},{160,128},{192,160},{224,192},{33,... | collective-permute-start | bytes 294920 | tf_op jit(solution)/shard_map/ppermute | solution.py:21
  188.8 12.9 %collective-permute-start.4 = (bf16[3,8,2048]{2,0,1:T(4,128)(2,1)S(1)}, bf16[3,8,2048]{2,0,1:T(4,128)(2,1)S(1)}, u32[]{:S(2)}, u32[]{:S(2)}) collective-permute-start(bf16[3,8,2048]{2,0,1:T(4,128)(2,1)S(1)} %copy.254), channel_id=1, source_target_pairs={{0,32},{32,64},{64,96},{96,128},{128,160},{160,192},{192,224},{1,3... | collective-permute-start | bytes 294920 | tf_op jit(solution)/shard_map/ppermute | solution.py:20
  201.7 5.4 copy-start.111
  202.8 6.5 collective-permute-start.7
  204.7 11.2 %collective-permute-start.6 = (bf16[22,3,2048]{2,0,1:T(8,128)(2,1)}, bf16[22,3,2048]{2,0,1:T(8,128)(2,1)}, u32[]{:S(2)}, u32[]{:S(2)}) collective-permute-start(bf16[22,3,2048]{2,0,1:T(8,128)(2,1)} %get-tuple-element.250), channel_id=1, source_target_pairs={{0,1},{1,2},{2,3},{3,4},{4,5},{5,6},{6,7},{7,8},{8,9},{9,10},{10,1... | collective-permute-start | bytes 811016 | tf_op jit(solution)/shard_map/ppermute | solution.py:20
  207.7 37.1 %copy-start.16 = (bf16[128,16,64]{2,1,0:T(8,128)(2,1)}, bf16[128,16,64]{2,1,0:T(8,128)(2,1)S(1)}, u32[]{:S(2)}) copy-start(bf16[128,16,64]{2,1,0:T(8,128)(2,1)S(1)} %copy.257) | copy-start | bytes 786436
  224.4 4.9 copy-start.43
  244.8 7.5 %copy-start.31 = (bf16[16,14,16,64]{3,2,0,1:T(8,128)(2,1)}, bf16[16,14,16,64]{3,2,0,1:T(8,128)(2,1)S(1)}, u32[]{:S(2)}) copy-start(bf16[16,14,16,64]{3,2,0,1:T(8,128)(2,1)S(1)} %reshape.944) | copy-start | bytes 1376260
  246.5 5.8 copy-start.105
  329.4 26.0 %copy-start.1 = (f32[16,8,16,98]{3,1,2,0:T(8,128)}, f32[16,8,16,98]{3,1,2,0:T(8,128)S(1)}, u32[]{:S(2)}) copy-start(f32[16,8,16,98]{3,1,2,0:T(8,128)S(1)} %fusion.7) | copy-start | bytes 2408452
  372.2 5.2 copy-start.15
  372.3 5.2 copy-start.75
  575.0 15.6 %copy-start.5 = (f32[16,8,16,98]{3,1,2,0:T(8,128)S(1)}, f32[16,8,16,98]{3,1,2,0:T(8,128)}, u32[]{:S(2)}) copy-start(f32[16,8,16,98]{3,1,2,0:T(8,128)} %copy-done.1) | copy-start | bytes 2408452
  575.0 15.7 %copy-start.59 = (bf16[16,14,16,64]{3,2,0,1:T(8,128)(2,1)S(1)}, bf16[16,14,16,64]{3,2,0,1:T(8,128)(2,1)}, u32[]{:S(2)}) copy-start(bf16[16,14,16,64]{3,2,0,1:T(8,128)(2,1)} %reshape.938) | copy-start | bytes 1376260
  575.0 15.7 %copy-start.97 = (f32[16,16,64,8]{2,3,1,0:T(8,128)S(1)}, f32[16,16,64,8]{2,3,1,0:T(8,128)}, u32[]{:S(2)}) copy-start(f32[16,16,64,8]{2,3,1,0:T(8,128)} %fusion.135) | copy-start | bytes 1572868
  577.7 36.4 %collective-permute-start.9 = (bf16[3,14,2048]{2,0,1:T(4,128)(2,1)}, bf16[3,14,2048]{2,0,1:T(4,128)(2,1)S(1)}, u32[]{:S(2)}, u32[]{:S(2)}) collective-permute-start(bf16[3,14,2048]{2,0,1:T(4,128)(2,1)} %get-tuple-element.221), channel_id=1, source_target_pairs={{32,0},{64,32},{96,64},{128,96},{160,128},{192,160},{224,192},{33,... | collective-permute-start | bytes 516104 | tf_op jit(solution)/shard_map/ppermute | solution.py:21
  579.6 11.7 %copy-start.45 = (bf16[16,14,16,64]{3,2,0,1:T(8,128)(2,1)S(1)}, bf16[16,14,16,64]{3,2,0,1:T(8,128)(2,1)}, u32[]{:S(2)}) copy-start(bf16[16,14,16,64]{3,2,0,1:T(8,128)(2,1)} %copy-done.43) | copy-start | bytes 1376260
  579.6 11.7 %copy-start.90 = (f32[16,16,64,8]{2,3,1,0:T(8,128)S(1)}, f32[16,16,64,8]{2,3,1,0:T(8,128)}, u32[]{:S(2)}) copy-start(f32[16,16,64,8]{2,3,1,0:T(8,128)} %fusion.131) | copy-start | bytes 1572868
  579.6 34.5 %collective-permute-start.8 = (bf16[3,14,2048]{2,0,1:T(4,128)(2,1)}, bf16[3,14,2048]{2,0,1:T(4,128)(2,1)}, u32[]{:S(2)}, u32[]{:S(2)}) collective-permute-start(bf16[3,14,2048]{2,0,1:T(4,128)(2,1)} %get-tuple-element.220), channel_id=1, source_target_pairs={{0,32},{32,64},{64,96},{96,128},{128,160},{160,192},{192,224},{1,3... | collective-permute-start | bytes 516104 | tf_op jit(solution)/shard_map/ppermute | solution.py:20
  614.0 7.0 %copy-start.78 = (f32[128,16,64]{0,2,1:T(8,128)S(1)}, f32[128,16,64]{0,2,1:T(8,128)}, u32[]{:S(2)}) copy-start(f32[128,16,64]{0,2,1:T(8,128)} %get-tuple-element.270) | copy-start | bytes 1572868
  614.0 7.0 %copy-start.79 = (f32[128,16,64]{0,2,1:T(8,128)S(1)}, f32[128,16,64]{0,2,1:T(8,128)}, u32[]{:S(2)}) copy-start(f32[128,16,64]{0,2,1:T(8,128)} %copy.362) | copy-start | bytes 1572868
  614.1 7.8 %copy-start.100 = (bf16[3,14,2048]{2,0,1:T(4,128)(2,1)}, bf16[3,14,2048]{2,0,1:T(4,128)(2,1)S(1)}, u32[]{:S(2)}) copy-start(bf16[3,14,2048]{2,0,1:T(4,128)(2,1)S(1)} %collective-permute-done.9) | copy-start | bytes 516100
  616.5 10.8 %collective-permute-start.11 = (bf16[28,3,2048]{2,0,1:T(8,128)(2,1)}, bf16[28,3,2048]{2,0,1:T(8,128)(2,1)}, u32[]{:S(2)}, u32[]{:S(2)}) collective-permute-start(bf16[28,3,2048]{2,0,1:T(8,128)(2,1)} %get-tuple-element.219), channel_id=1, source_target_pairs={{1,0},{2,1},{3,2},{4,3},{5,4},{6,5},{7,6},{8,7},{9,8},{10,9},{11,1... | collective-permute-start | bytes 1032200 | tf_op jit(solution)/shard_map/ppermute | solution.py:21
  618.4 12.2 %collective-permute-start.10 = (bf16[28,3,2048]{2,0,1:T(8,128)(2,1)}, bf16[28,3,2048]{2,0,1:T(8,128)(2,1)}, u32[]{:S(2)}, u32[]{:S(2)}) collective-permute-start(bf16[28,3,2048]{2,0,1:T(8,128)(2,1)} %get-tuple-element.218), channel_id=1, source_target_pairs={{0,1},{1,2},{2,3},{3,4},{4,5},{5,6},{6,7},{7,8},{8,9},{9,10},{10,1... | collective-permute-start | bytes 1032200 | tf_op jit(solution)/shard_map/ppermute | solution.py:20
  622.8 7.9 %copy-start.23 = (bf16[22,14,1024]{2,0,1:T(8,128)(2,1)S(1)}, bf16[22,14,1024]{2,0,1:T(8,128)(2,1)}, u32[]{:S(2)}) copy-start(bf16[22,14,1024]{2,0,1:T(8,128)(2,1)} %convert.20) | copy-start | bytes 1892356
  622.8 7.9 %copy-start.26 = (bf16[22,14,1024]{2,0,1:T(8,128)(2,1)S(1)}, bf16[22,14,1024]{2,0,1:T(8,128)(2,1)}, u32[]{:S(2)}) copy-start(bf16[22,14,1024]{2,0,1:T(8,128)(2,1)} %copy-done.24) | copy-start | bytes 1892356
  625.1 5.6 copy-start.101
  658.4 4.5 copy-start.117
  667.2 3.9 copy-start.30
  667.2 3.9 copy-start.74
  (84 other events, 158.3 us)
where the time goes:
time: 687 us; the launch traced here: 673 us
  local copies, waits for them, and re-layouts  291 us (42%)
  matrix products  206 us (30%)
  other arithmetic  78.7 us (11%)
  starting transfers between devices  67.1 us (10%)
  waiting for transfers between devices  28.1 us (4%)
    dot_general x35, matrix products, mixed_product(): jnp.einsum(form, low_part, halves, preferred_element_type=jnp.float32)  90.2 us
    dot_general x35, matrix products, mixed_product(): jnp.einsum(form, high_part, halves, preferred_element_type=jnp.float32)  51.8 us
    ppermute x6, starting transfers between devices, extended_2(): before = lax.ppermute(last, axis, up)  38.1 us
    scatter-add x7, local copies, waits for them, and re-layouts, attend_back(): key_total = key_total.at[offset:offset + tile_rows].add(key_part)  37.8 us
    scatter-add x7, local copies, waits for them, and re-layouts, attend_back(): value_total = value_total.at[offset:offset + tile_rows].add(value_part)  37.7 us
    reshape x14, local copies, waits for them, and re-layouts, offset_views(): value_view = rows[..., D:].reshape(tile_rows, padded_cols, HEADS, head_size)  34.8 us
    dot_general x14, matrix products, attend(): jnp.einsum('ijhe,ikhe->ijhk', query_heads, key_view, preferred_element_ty...  32.8 us
    another operation x12, local copies, waits for them, and re-layouts  32.8 us
  transfers between devices with their start and end apart: 14, of which 9 were waited for; matrix products, arithmetic and copies ran while one was open for 6% of the time, Pallas kernels for 0%

commit v1 on v0

v1 whole, which is shorter than its diff:
```python
import functools

import jax
import jax.numpy as jnp
from jax import lax
from jax.experimental import pallas as pl
from jax.experimental.pallas import tpu as pltpu
from jax.sharding import PartitionSpec as P

D = 1024
PIX = 768
EPSILON = 1e-06
F32 = jnp.float32
BF = jnp.bfloat16
LANES = 256
GROUPS = D // LANES
NT = (((1,), (1,)), ((), ()))
NN = (((1,), (0,)), ((), ()))
TN = (((0,), (0,)), ((), ()))


def dot(a, b, dims=NN):
    return lax.dot_general(a, b, dims, preferred_element_type=F32)


def iota(shape, axis):
    return lax.broadcasted_iota(jnp.int32, shape, axis)


def group_mean_matrix():
    same = (iota((LANES, LANES), 0) >> 6) == (iota((LANES, LANES), 1) >> 6)
    return jnp.where(same, 1.0 / 64, 0.0).astype(BF)


def group_mean(values, means):
    return dot(values.astype(BF), means)


def row_scale(residual):
    return lax.rsqrt(jnp.mean(residual * residual, axis=-1, keepdims=True) + EPSILON)


def cols(index):
    return pl.ds(pl.multiple_of(index * LANES, LANES), LANES)


def head_masks():
    lane = iota((1, LANES), 1) >> 6
    return [jnp.where(lane == h, 1.0, 0.0).astype(BF) for h in range(4)]


def stack_heads(values, masks):
    return jnp.concatenate([values * mask for mask in masks], axis=0)


def unstack_heads(stacked):
    lane = iota((64, LANES), 1) >> 6
    parts = [stacked[64 * h : 64 * h + 64] for h in range(4)]
    low = jnp.where(lane == 0, parts[0], parts[1])
    high = jnp.where(lane == 2, parts[2], parts[3])
    return jnp.where(lane < 2, low, high)


def block_mask(first_row, col_index, grid_rows, grid_cols):
    shape = (64, 256)
    token, key = iota(shape, 0), iota(shape, 1)
    query_row, query_col = token >> 3, token & 7
    side = key - 128
    left = key < 192
    rim = side & 63
    key_row = jnp.where(key < 128, key >> 3, rim >> 2)
    rim_col = jnp.where(left, (rim & 3) - 4, (rim & 3) + 8)
    key_col = jnp.where(key < 128, key & 7, rim_col)
    row_gap = key_row - query_row - 4
    col_gap = key_col - query_col
    near = (row_gap >= -3) & (row_gap <= 3) & (col_gap >= -3) & (col_gap <= 3)
    row = first_row + key_row
    col = col_index * 8 + key_col
    inside = (row >= 0) & (row < grid_rows) & (col >= 0) & (col < grid_cols)
    mask = jnp.where(near & inside, 1.0, 0.0)
    return jnp.concatenate([mask] * 4, axis=0)


def softmax_parts(scores, mask):
    weight = jnp.exp(scores) * mask
    total = jnp.sum(weight, axis=-1, keepdims=True)
    return weight, 1.0 / jnp.where(total > 0, total, 1.0)


def place_kernel(recv_ref, own_ref, left_ref, right_ref):
    sources, slots = [], []
    for tile in range(3):
        part = recv_ref[:, 16 * tile : 16 * tile + 16, :].reshape(128, PIX + 128)
        sources.append(part[:, :PIX])
        slot = part[:, PIX:].astype(F32).T + 128.0 * tile
        slots.append(slot[:8])
    source = jnp.concatenate(sources, axis=0)
    slot = jnp.concatenate(slots, axis=1)

    def pick(position):
        hot = jnp.where(position == slot[:1], 1.0, 0.0).astype(BF)
        return dot(hot, source).astype(BF)

    own_ref[...] = pick((iota((320, 384), 0) + 32).astype(F32))
    n = iota((144, 384), 0)
    edge = ((n >> 2) + 6) * 8 + (n & 3)
    left_ref[...] = pick(edge.astype(F32))
    right_ref[...] = pick((edge + 4).astype(F32))


def own_first_kernel(own_ref, we_ref, wq_ref, wkv_ref, x0_ref, q_ref, kv_ref, x_s, n_s):
    means = group_mean_matrix()

    @pl.loop(0, GROUPS)
    def _(g):
        x_s[:, cols(g)] = dot(own_ref[...], we_ref[:, cols(g)]).astype(BF).astype(F32)

    residual = x_s[...]
    n_s[...] = (residual * row_scale(residual)).astype(BF)
    x0_ref[...] = residual[32:288].astype(BF)

    @pl.loop(0, GROUPS)
    def _(g):
        query = dot(n_s[32:288, :], wq_ref[:, cols(g)])
        query = query * lax.rsqrt(group_mean(query * query, means) + EPSILON)
        q_ref[:, cols(g)] = (query.astype(BF) * 0.125).astype(BF)
        key = dot(n_s[...], wkv_ref[:, cols(g)])
        key = key * lax.rsqrt(group_mean(key * key, means) + EPSILON)
        kv_ref[:, cols(g)] = key.astype(BF)
        kv_ref[:, cols(g + GROUPS)] = dot(n_s[...], wkv_ref[:, cols(g + GROUPS)]).astype(BF)


def keys_of(kv_ref, rim_ref, block, group):
    rim = rim_ref.shape[0] // 2
    lanes = cols(group)
    return jnp.concatenate(
        [
            kv_ref[64 * block : 64 * block + 128, lanes],
            rim_ref[32 * block : 32 * block + 64, lanes],
            rim_ref[rim + 32 * block : rim + 32 * block + 64, lanes],
        ],
        axis=0,
    )


def padded_rim(values):
    half = values.shape[0] // 2
    pad = jnp.zeros((8, values.shape[1]), F32)
    return jnp.concatenate([pad, values[:half], pad, pad, values[half:], pad], axis=0)


def first_core_kernel(
    grid_rows, grid_cols,
    place_ref, left_ref, right_ref, we_ref, wkv_ref, wo_ref, x0_ref, q_ref, kv_ref,
    x1_ref, go_left_ref, go_right_ref,
    p_s, x_s, n_s, rim_s, o_s, mask_s,
):
    means = group_mean_matrix()
    p_s[0:144, :] = left_ref[...]
    p_s[144:288, :] = right_ref[...]

    @pl.loop(0, GROUPS)
    def _(g):
        x_s[:, cols(g)] = dot(p_s[...], we_ref[:, cols(g)]).astype(BF).astype(F32)

    residual = x_s[...]
    n_s[...] = (residual * row_scale(residual)).astype(BF)

    @pl.loop(0, GROUPS)
    def _(g):
        key = dot(n_s[...], wkv_ref[:, cols(g)])
        key = key * lax.rsqrt(group_mean(key * key, means) + EPSILON)
        rim_s[:, cols(g)] = padded_rim(key).astype(BF)
        value = dot(n_s[...], wkv_ref[:, cols(g + GROUPS)])
        rim_s[:, cols(g + GROUPS)] = padded_rim(value).astype(BF)

    first_row = place_ref[0] * 16 - 12
    for block in range(4):
        mask_s[block] = block_mask(first_row + 8 * block, place_ref[1], grid_rows, grid_cols)
    masks = head_masks()

    @pl.loop(0, GROUPS)
    def _(g):
        for block in range(4):
            query = stack_heads(q_ref[64 * block : 64 * block + 64, cols(g)], masks)
            key = keys_of(kv_ref, rim_s, block, g)
            value = keys_of(kv_ref, rim_s, block, g + GROUPS)
            weight, inverse = softmax_parts(dot(query, key, NT), mask_s[block])
            mixed = dot(weight.astype(BF), value) * inverse
            o_s[64 * block : 64 * block + 64, cols(g)] = unstack_heads(mixed).astype(BF)

    n = iota((112, 256), 0)
    edge = ((n >> 2) + 2) * 8 + (n & 3)
    source = iota((112, 256), 1)
    pick_left = jnp.where(edge == source, 1.0, 0.0).astype(BF)
    pick_right = jnp.where(edge + 4 == source, 1.0, 0.0).astype(BF)

    @pl.loop(0, GROUPS)
    def _(g):
        total = x0_ref[:, cols(g)].astype(F32) + dot(o_s[...], wo_ref[:, cols(g)])
        total = total.astype(BF)
        x1_ref[:, cols(g)] = total
        go_left_ref[:, cols(g)] = dot(pick_left, total).astype(BF)
        go_right_ref[:, cols(g)] = dot(pick_right, total).astype(BF)


def own_second_kernel(
    x1_ref, cot_ref, above_ref, below_ref, wq_ref, wkv_ref, wo_ref,
    q_ref, kv_ref, do_ref, rsq_ref, rsk_ref,
    n_s, c_s,
):
    means = group_mean_matrix()
    residual = x1_ref[...].astype(F32)
    n_s[...] = (residual * row_scale(residual)).astype(BF)
    c_s[0:32, :] = above_ref[...]
    c_s[32:160, :] = cot_ref[...]
    c_s[160:192, :] = below_ref[...]

    @pl.loop(0, GROUPS)
    def _(g):
        query = dot(n_s[32:224, :], wq_ref[:, cols(g)])
        scale = lax.rsqrt(group_mean(query * query, means) + EPSILON)
        q_ref[:, cols(g)] = ((query * scale).astype(BF) * 0.125).astype(BF)
        rsq_ref[:, cols(g)] = scale[32:160]
        key = dot(n_s[...], wkv_ref[:, cols(g)])
        scale = lax.rsqrt(group_mean(key * key, means) + EPSILON)
        kv_ref[:, cols(g)] = (key * scale).astype(BF)
        rsk_ref[:, cols(g)] = scale[64:192]
        kv_ref[:, cols(g + GROUPS)] = dot(n_s[...], wkv_ref[:, cols(g + GROUPS)]).astype(BF)
        do_ref[:, cols(g)] = dot(c_s[...], wo_ref[cols(g), :], NT).astype(BF)


def head_scale_back(back, normed, scale, means):
    return scale * (back - normed * group_mean(back * normed, means))


def second_core_kernel(
    grid_rows, grid_cols,
    place_ref, left_ref, right_ref, wkv_ref, q_ref, kv_ref, do_ref,
    o_ref, dq_ref, dkv_ref, go_left_ref, go_right_ref,
    n_s, rim_s, rs_s, db_s, mask_s,
):
    means = group_mean_matrix()
    residual = jnp.concatenate([left_ref[...].astype(F32), right_ref[...].astype(F32)], axis=0)
    residual = padded_rim(residual)
    n_s[...] = (residual * row_scale(residual)).astype(BF)

    @pl.loop(0, GROUPS)
    def _(g):
        key = dot(n_s[...], wkv_ref[:, cols(g)])
        scale = lax.rsqrt(group_mean(key * key, means) + EPSILON)
        rim_s[:, cols(g)] = (key * scale).astype(BF)
        rs_s[0:64, cols(g)] = scale[32:96]
        rs_s[64:128, cols(g)] = scale[160:224]
        rim_s[:, cols(g + GROUPS)] = dot(n_s[...], wkv_ref[:, cols(g + GROUPS)]).astype(BF)

    first_row = place_ref[0] * 16 - 8
    for block in range(3):
        mask_s[block] = block_mask(first_row + 8 * block, place_ref[1], grid_rows, grid_cols)
    masks = head_masks()

    @pl.loop(0, GROUPS)
    def _(g):
        key_backs, value_backs = [], []
        for block in range(3):
            query = stack_heads(q_ref[64 * block : 64 * block + 64, cols(g)], masks)
            key = keys_of(kv_ref, rim_s, block, g)
            value = keys_of(kv_ref, rim_s, block, g + GROUPS)
            weight, inverse = softmax_parts(dot(query, key, NT), mask_s[block])
            probs = weight * inverse
            probs_low = probs.astype(BF)
            out_back = stack_heads(do_ref[64 * block : 64 * block + 64, cols(g)], masks)
            probs_back = dot(out_back, value, NT)
            centre = jnp.sum(probs_back * probs, axis=-1, keepdims=True)
            scores_back = (probs * (probs_back - centre)).astype(BF)
            o_ref[64 * block : 64 * block + 64, cols(g)] = unstack_heads(
                dot(probs_low, value)
            ).astype(BF)
            dq_ref[64 * block : 64 * block + 64, cols(g)] = unstack_heads(
                dot(scores_back, key)
            ).astype(BF)
            key_backs.append(dot(scores_back, query, TN))
            value_backs.append(dot(probs_low, out_back, TN))

        def fold(parts):
            def piece(start, half):
                return jnp.concatenate(
                    [
                        parts[0][start + half : start + 2 * half] + parts[1][start : start + half],
                        parts[1][start + half : start + 2 * half] + parts[2][start : start + half],
                    ],
                    axis=0,
                )

            return piece(0, 64), jnp.concatenate([piece(128, 32), piece(192, 32)], axis=0)

        own, rim = fold(key_backs)
        dkv_ref[:, cols(g)] = own.astype(BF)
        normed = jnp.concatenate([rim_s[32:96, cols(g)], rim_s[160:224, cols(g)]], axis=0)
        rim = head_scale_back(rim, normed.astype(F32), rs_s[:, cols(g)], means)
        db_s[:, cols(g)] = rim.astype(BF)
        own, rim = fold(value_backs)
        dkv_ref[:, cols(g + GROUPS)] = own.astype(BF)
        db_s[:, cols(g + GROUPS)] = rim.astype(BF)

    @pl.loop(0, GROUPS)
    def _(g):
        back = dot(db_s[...], wkv_ref[cols(g), :], NT).astype(BF)
        go_left_ref[:, cols(g)] = back[:64]
        go_right_ref[:, cols(g)] = back[64:]


def own_back_kernel(
    x1_ref, o_ref, dq_ref, dkv_ref, q_ref, kv_ref, rsq_ref, rsk_ref, wq_ref, wkv_ref, wo_ref,
    out_ref, dn_ref,
    a_s, b_s,
):
    means = group_mean_matrix()

    @pl.loop(0, GROUPS)
    def _(g):
        total = x1_ref[64:192, cols(g)].astype(F32) + dot(o_ref[32:160, :], wo_ref[:, cols(g)])
        out_ref[:, cols(g)] = total.astype(BF)
        back = dq_ref[32:160, cols(g)].astype(F32) * 0.125
        normed = q_ref[32:160, cols(g)].astype(F32) * 8.0
        a_s[:, cols(g)] = head_scale_back(back, normed, rsq_ref[:, cols(g)], means).astype(BF)
        back = dkv_ref[:, cols(g)].astype(F32)
        normed = kv_ref[64:192, cols(g)].astype(F32)
        b_s[:, cols(g)] = head_scale_back(back, normed, rsk_ref[:, cols(g)], means).astype(BF)
        b_s[:, cols(g + GROUPS)] = dkv_ref[:, cols(g + GROUPS)]

    @pl.loop(0, GROUPS)
    def _(g):
        back = dot(a_s[...], wq_ref[cols(g), :], NT) + dot(b_s[...], wkv_ref[cols(g), :], NT)
        dn_ref[:, cols(g)] = back


def last_kernel(x1_ref, cot_ref, dn_ref, left_ref, right_ref, out_ref):
    n, source = iota((128, 64), 0), iota((128, 64), 1)
    column = n & 7
    place = (n >> 3) * 4 + (column & 3)
    from_left = jnp.where((place == source) & (column < 4), 1.0, 0.0).astype(BF)
    from_right = jnp.where((place == source) & (column >= 4), 1.0, 0.0).astype(BF)
    pick = jnp.concatenate([from_left, from_right], axis=1)
    arrived = jnp.concatenate([left_ref[...], right_ref[...]], axis=0)
    back = dn_ref[...] + dot(pick, arrived)
    residual = x1_ref[64:192, :].astype(F32)
    scale = row_scale(residual)
    normed = residual * scale
    mean = jnp.mean(back * normed, axis=-1, keepdims=True)
    out_ref[...] = (cot_ref[...].astype(F32) + scale * (back - normed * mean)).astype(BF)


def call(kernel, out_shapes, *operands, scratch=(), flops=0, moved=0, small=None):
    vmem = pl.BlockSpec(memory_space=pltpu.VMEM)
    in_specs = [vmem] * len(operands)
    if small is not None:
        operands = (small,) + operands
        in_specs = [pl.BlockSpec(memory_space=pltpu.SMEM)] + in_specs
    shapes = tuple(jax.ShapeDtypeStruct(s, d) for s, d in out_shapes)
    return pl.pallas_call(
        kernel,
        out_shape=shapes,
        in_specs=in_specs,
        out_specs=tuple(vmem for _ in shapes),
        scratch_shapes=[pltpu.VMEM(s, d) for s, d in scratch],
        compiler_params=pltpu.CompilerParams(vmem_limit_bytes=40 * 1024 * 1024),
        cost_estimate=pl.CostEstimate(flops=flops, bytes_accessed=moved, transcendentals=0),
    )(*operands)


def shift(values, axis, step):
    peers = lax.axis_size(axis)
    return lax.ppermute(
        values, axis, [(i, i + step) for i in range(peers) if 0 <= i + step < peers]
    )


def on_device(patches, tile_slot, w_embed, w_query, w_keyval, w_out, cotangent):
    rows, columns = lax.axis_size("row"), lax.axis_size("col")
    grid_rows, grid_cols = rows * 16, columns * 8
    place = jnp.stack([lax.axis_index("row"), lax.axis_index("col")]).astype(jnp.int32)
    cot = cotangent.reshape(128, D)

    slot = jnp.broadcast_to(tile_slot.astype(BF)[:, None], (128, 128))
    block = jnp.concatenate([patches, slot], axis=1).reshape(rows, 16, PIX + 128)
    wide = jnp.pad(block, ((1, 1), (0, 0), (0, 0)))
    block = jnp.concatenate([wide[:-2], wide[1:-1], wide[2:]], axis=1)
    arrived = lax.all_to_all(block, "row", split_axis=0, concat_axis=0, tiled=True)

    above = shift(cot[96:], "row", 1)
    below = shift(cot[:32], "row", -1)

    own, go_left, go_right = call(
        place_kernel, (((320, PIX), BF), ((144, PIX), BF), ((144, PIX), BF)), arrived
    )
    left = shift(go_right, "col", 1)
    right = shift(go_left, "col", -1)
    x0, queries, keyval = call(
        own_first_kernel,
        (((256, D), BF), ((256, D), BF), ((320, 2 * D), BF)),
        own, w_embed, w_query, w_keyval,
        scratch=(((320, D), F32), ((320, D), BF)),
        flops=8 * 10**9, moved=8 * 10**6,
    )
    x1, go_left, go_right = call(
        functools.partial(first_core_kernel, grid_rows, grid_cols),
        (((256, D), BF), ((112, D), BF), ((112, D), BF)),
        left, right, w_embed, w_keyval, w_out, x0, queries, keyval,
        small=place,
        scratch=(
            ((288, PIX), BF), ((288, D), F32), ((288, D), BF), ((320, 2 * D), BF), ((256, D), BF),
            ((4, 256, 256), F32),
        ),
        flops=8 * 10**9, moved=8 * 10**6,
    )
    left = shift(go_right, "col", 1)
    right = shift(go_left, "col", -1)
    queries, keyval, out_back, query_scale, key_scale = call(
        own_second_kernel,
        (((192, D), BF), ((256, 2 * D), BF), ((192, D), BF), ((128, D), F32), ((128, D), F32)),
        x1, cot, above, below, w_query, w_keyval, w_out,
        scratch=(((256, D), BF), ((192, D), BF)),
        flops=8 * 10**9, moved=8 * 10**6,
    )
    attended, dq, dkv, go_left, go_right = call(
        functools.partial(second_core_kernel, grid_rows, grid_cols),
        (((192, D), BF), ((192, D), BF), ((128, 2 * D), BF), ((64, D), BF), ((64, D), BF)),
        left, right, w_keyval, queries, keyval, out_back,
        small=place,
        scratch=(
            ((256, D), BF), ((256, 2 * D), BF), ((128, D), F32), ((128, 2 * D), BF),
            ((3, 256, 256), F32),
        ),
        flops=8 * 10**9, moved=8 * 10**6,
    )
    left = shift(go_right, "col", 1)
    right = shift(go_left, "col", -1)
    final_tokens, back = call(
        own_back_kernel,
        (((128, D), BF), ((128, D), F32)),
        x1, attended, dq, dkv, queries, keyval, query_scale, key_scale, w_query, w_keyval, w_out,
        scratch=(((128, D), BF), ((128, 2 * D), BF)),
        flops=8 * 10**9, moved=8 * 10**6,
    )
    (input_grad,) = call(last_kernel, (((128, D), BF),), x1, cot, back, left, right)
    return final_tokens.reshape(16, 8, D), input_grad.reshape(16, 8, D)


def solution(mesh):
    in_specs = (
        P(("row", "col"), None),
        P(("row", "col")),
        P(),
        P(),
        P(),
        P(),
        P("row", "col", None),
    )
    out_specs = (P("row", "col", None), P("row", "col", None))
    return jax.shard_map(
        on_device, mesh=mesh, in_specs=in_specs, out_specs=out_specs, check_vma=False
    )
```

time: 687 us -> 105 us (0.15)
  the two profiles are of different devices: /device:TPU:30 before, /device:TPU:2 now
where the time goes in v1:
time: 105 us; the launch traced here: 104 us
  starting transfers between devices  41.8 us (40%)
  Pallas kernels  40.1 us (38%)
  waiting for transfers between devices  15 us (14%)
  local copies, waits for them, and re-layouts  3.74 us (4%)
  other arithmetic  2.61 us (2%)
    pallas_call x7, Pallas kernels, call(): pl.pallas_call(kernel, out_shape=shapes, in_specs=in_specs, out_specs=tup...  40.1 us
    ppermute x8, starting transfers between devices, shift(): lax.ppermute(values, axis, [(i, i + step) for i in range(peers) if 0 <= i...  30.6 us
    all_to_all x1, waiting for transfers between devices, on_device(): lax.all_to_all(block, 'row', split_axis=0, concat_axis=0, tiled=True)  14.9 us
    all_to_all x1, starting transfers between devices, on_device(): lax.all_to_all(block, 'row', split_axis=0, concat_axis=0, tiled=True)  11.2 us
    unnamed x12, local copies, waits for them, and re-layouts  3.61 us
  transfers between devices with their start and end apart: 9, of which 1 were waited for; matrix products, arithmetic and copies ran while one was open for 0% of the time, Pallas kernels for 25%

profile of v1, /device:TPU:2, one launch (start us, length us, event | category | flops | bytes accessed | tf_op | source)
XLA Modules:
  0.0 104.1 jit_solution(13146647102768286512)
XLA Ops:
  0.6 0.7 convert_element_type.5
  1.3 0.1 broadcast_in_dim.2
  1.4 0.9 pad_maximum_fusion.1
  2.4 0.0 copy-start
  2.4 0.9 pad_maximum_fusion
  3.3 0.0 copy-start.4
  3.3 11.2 %all-to-all-start = ((bf16[8,48,896]{2,1,0:T(8,128)(2,1)}), bf16[8,48,896]{2,1,0:T(8,128)(2,1)S(1)}, u32[]{:S(2)}, u32[]{:S(2)}) async-start(bf16[8,48,896]{2,1,0:T(8,128)(2,1)} %pad_maximum_fusion), calls=%async_computation | async-start | bytes 1376256 | tf_op jit(solution)/shard_map/all_to_all | solution.py:389
  14.5 0.0 copy-done
  14.6 1.3 %collective-permute-start.5 = (bf16[32,1024]{1,0:T(8,128)(2,1)S(1)}, bf16[32,1024]{1,0:T(8,128)(2,1)S(1)}, u32[]{:S(2)}, u32[]{:S(2)}) collective-permute-start(bf16[32,1024]{1,0:T(8,128)(2,1)S(1)} %get-tuple-element.44), channel_id=1, source_target_pairs={{32,0},{64,32},{96,64},{128,96},{160,128},{192,160},{224,192},{33,... | collective-permute-start | bytes 196616 | tf_op jit(solution)/shard_map/ppermute | solution.py:374
  15.9 4.5 %collective-permute-start.4 = (bf16[32,1024]{1,0:T(8,128)(2,1)S(1)}, bf16[32,1024]{1,0:T(8,128)(2,1)S(1)}, u32[]{:S(2)}, u32[]{:S(2)}) collective-permute-start(bf16[32,1024]{1,0:T(8,128)(2,1)S(1)} %get-tuple-element.45), channel_id=1, source_target_pairs={{0,32},{32,64},{64,96},{96,128},{128,160},{160,192},{192,224},{1,3... | collective-permute-start | bytes 196616 | tf_op jit(solution)/shard_map/ppermute | solution.py:374
  20.4 0.1 pad_add_fusion.place_ref
  20.5 14.9 %all-to-all-done.recv_ref = bf16[8,48,896]{2,1,0:T(8,128)(2,1)S(1)} async-done(((bf16[8,48,896]{2,1,0:T(8,128)(2,1)}), bf16[8,48,896]{2,1,0:T(8,128)(2,1)S(1)}, u32[]{:S(2)}, u32[]{:S(2)}) %all-to-all-start) | async-done | bytes 688160 | tf_op jit(solution)/shard_map/all_to_all | solution.py:389
  35.4 0.7 shard_map.86
  36.1 1.9 %collective-permute-start = (bf16[144,768]{1,0:T(8,128)(2,1)S(1)}, bf16[144,768]{1,0:T(8,128)(2,1)S(1)}, u32[]{:S(2)}, u32[]{:S(2)}) collective-permute-start(bf16[144,768]{1,0:T(8,128)(2,1)S(1)} %get-tuple-element.23), channel_id=1, source_target_pairs={{0,1},{1,2},{2,3},{3,4},{4,5},{5,6},{6,7},{7,8},{8,9},{9,10},{10,1... | collective-permute-start | bytes 663560 | tf_op jit(solution)/shard_map/ppermute | solution.py:374
  38.1 6.3 %collective-permute-start.1 = (bf16[144,768]{1,0:T(8,128)(2,1)S(1)}, bf16[144,768]{1,0:T(8,128)(2,1)S(1)}, u32[]{:S(2)}, u32[]{:S(2)}) collective-permute-start(bf16[144,768]{1,0:T(8,128)(2,1)S(1)} %get-tuple-element.24), channel_id=1, source_target_pairs={{1,0},{2,1},{3,2},{4,3},{5,4},{6,5},{7,6},{8,7},{9,8},{10,9},{11,1... | collective-permute-start | bytes 663560 | tf_op jit(solution)/shard_map/ppermute | solution.py:374
  44.4 0.0 copy-done.4
  44.4 0.0 copy-start.1
  44.4 2.2 %copy-done.1 = bf16[1024,2048]{1,0:T(8,128)(2,1)S(1)} copy-done((bf16[1024,2048]{1,0:T(8,128)(2,1)S(1)}, bf16[1024,2048]{1,0:T(8,128)(2,1)}, u32[]{:S(2)}) %copy-start.1) | copy-done | bytes 4194328
  46.6 0.0 copy-start.5
  46.6 1.4 %copy-done.5 = bf16[768,1024]{1,0:T(8,128)(2,1)S(1)} copy-done((bf16[768,1024]{1,0:T(8,128)(2,1)S(1)}, bf16[768,1024]{1,0:T(8,128)(2,1)}, u32[]{:S(2)}) %copy-start.5) | copy-done | bytes 1572888
  48.0 0.0 copy-start.2
  48.0 0.0 copy-start.3
  48.0 5.8 %shard_map.87 = (bf16[256,1024]{1,0:T(8,128)(2,1)S(1)}, bf16[256,1024]{1,0:T(8,128)(2,1)S(1)}, bf16[320,2048]{1,0:T(8,128)(2,1)S(1)}) custom-call(bf16[320,768]{1,0:T(8,128)(2,1)S(1)} %get-tuple-element.25.own_ref, bf16[768,1024]{1,0:T(8,128)(2,1)S(1)} %copy-done.5, bf16[1024,1024]{1,0:T(8,128)(2,1)S(1)} %copy-done.4, bf16[1024,2048]{1,0:T(8,128)(2,1)S(1)} %copy-done.1), custom_call_target="tpu_custom_call" | custom-call | flops 8000000000 | bytes 8000000 | tf_op jit(solution)/shard_map/pallas_call | solution.py:361
  53.9 0.0 collective-permute-done.left_ref
  53.9 0.0 collective-permute-done.1.right_ref
  53.9 0.0 copy-done.2
  53.9 0.0 copy-done.3
  53.9 10.6 %shard_map.88 = (bf16[256,1024]{1,0:T(8,128)(2,1)S(1)}, bf16[112,1024]{1,0:T(8,128)(2,1)S(1)}, bf16[112,1024]{1,0:T(8,128)(2,1)S(1)}) custom-call(s32[2]{0:T(128)S(1)} %pad_add_fusion.place_ref, bf16[144,768]{1,0:T(8,128)(2,1)S(1)} %collective-permute-done.left_ref, bf16[144,768]{1,0:T(8,128)(2,1)S(1)} %collective-permute-done.1.right_ref, ...), custom_call_target="tpu_custom_call" | custom-call | flops 8000000000 | bytes 8000000 | tf_op jit(solution)/shard_map/pallas_call | solution.py:361
  64.5 1.9 %collective-permute-start.2 = (bf16[112,1024]{1,0:T(8,128)(2,1)S(1)}, bf16[112,1024]{1,0:T(8,128)(2,1)S(1)}, u32[]{:S(2)}, u32[]{:S(2)}) collective-permute-start(bf16[112,1024]{1,0:T(8,128)(2,1)S(1)} %get-tuple-element.30), channel_id=1, source_target_pairs={{0,1},{1,2},{2,3},{3,4},{4,5},{5,6},{6,7},{7,8},{8,9},{9,10},{10,1... | collective-permute-start | bytes 688136 | tf_op jit(solution)/shard_map/ppermute | solution.py:374
  66.4 6.3 %collective-permute-start.3 = (bf16[112,1024]{1,0:T(8,128)(2,1)S(1)}, bf16[112,1024]{1,0:T(8,128)(2,1)S(1)}, u32[]{:S(2)}, u32[]{:S(2)}) collective-permute-start(bf16[112,1024]{1,0:T(8,128)(2,1)S(1)} %get-tuple-element.31), channel_id=1, source_target_pairs={{1,0},{2,1},{3,2},{4,3},{5,4},{6,5},{7,6},{8,7},{9,8},{10,9},{11,1... | collective-permute-start | bytes 688136 | tf_op jit(solution)/shard_map/ppermute | solution.py:374
  72.8 0.0 collective-permute-done.5.below_ref
  72.8 0.0 collective-permute-done.4.above_ref
  72.8 4.9 %shard_map.89 = (bf16[192,1024]{1,0:T(8,128)(2,1)S(1)}, bf16[256,2048]{1,0:T(8,128)(2,1)S(1)}, bf16[192,1024]{1,0:T(8,128)(2,1)S(1)}, f32[128,1024]{1,0:T(8,128)S(1)}, f32[128,1024]{1,0:T(8,128)S(1)}) custom-call(bf16[256,1024]{1,0:T(8,128)(2,1)S(1)} %get-tuple-element.29.x1_ref, bf16[128,1024]{1,0:T(8,128)(2,1)S(1)} %bitcast.10, ...), custom_call_target="tpu_custom_call" | custom-call | flops 8000000000 | bytes 8000000 | tf_op jit(solution)/shard_map/pallas_call | solution.py:361
  77.7 0.0 collective-permute-done.2.left_ref
  77.7 0.0 collective-permute-done.3.right_ref
  77.7 13.0 %shard_map.90 = (bf16[192,1024]{1,0:T(8,128)(2,1)S(1)}, bf16[192,1024]{1,0:T(8,128)(2,1)S(1)}, bf16[128,2048]{1,0:T(8,128)(2,1)S(1)}, bf16[64,1024]{1,0:T(8,128)(2,1)S(1)}, bf16[64,1024]{1,0:T(8,128)(2,1)S(1)}) custom-call(s32[2]{0:T(128)S(1)} %pad_add_fusion.place_ref, bf16[112,1024]{1,0:T(8,128)(2,1)S(1)} %collective-permute-done.2.left_ref, ...), custom_call_target="tpu_custom_call" | custom-call | flops 8000000000 | bytes 8000000 | tf_op jit(solution)/shard_map/pallas_call | solution.py:361
  90.8 1.9 %collective-permute-start.6 = (bf16[64,1024]{1,0:T(8,128)(2,1)S(1)}, bf16[64,1024]{1,0:T(8,128)(2,1)S(1)}, u32[]{:S(2)}, u32[]{:S(2)}) collective-permute-start(bf16[64,1024]{1,0:T(8,128)(2,1)S(1)} %get-tuple-element.42), channel_id=1, source_target_pairs={{0,1},{1,2},{2,3},{3,4},{4,5},{5,6},{6,7},{7,8},{8,9},{9,10},{10,1... | collective-permute-start | bytes 393224 | tf_op jit(solution)/shard_map/ppermute | solution.py:374
  92.7 6.3 %collective-permute-start.7 = (bf16[64,1024]{1,0:T(8,128)(2,1)S(1)}, bf16[64,1024]{1,0:T(8,128)(2,1)S(1)}, u32[]{:S(2)}, u32[]{:S(2)}) collective-permute-start(bf16[64,1024]{1,0:T(8,128)(2,1)S(1)} %get-tuple-element.43), channel_id=1, source_target_pairs={{1,0},{2,1},{3,2},{4,3},{5,4},{6,5},{7,6},{8,7},{9,8},{10,9},{11,1... | collective-permute-start | bytes 393224 | tf_op jit(solution)/shard_map/ppermute | solution.py:374
  99.1 3.9 %shard_map.91 = (bf16[128,1024]{1,0:T(8,128)(2,1)}, f32[128,1024]{1,0:T(8,128)S(1)}) custom-call(bf16[256,1024]{1,0:T(8,128)(2,1)S(1)} %get-tuple-element.29.x1_ref, bf16[192,1024]{1,0:T(8,128)(2,1)S(1)} %get-tuple-element.35.o_ref, bf16[192,1024]{1,0:T(8,128)(2,1)S(1)} %get-tuple-element.36.dq_ref, bf16[128,2048]{1,0:T(8,128)(2,1)S(1)} %get-tuple-element.37.dkv_ref, ...), custom_call_target="tpu_custom_call" | custom-call | flops 8000000000 | bytes 8000000 | tf_op jit(solution)/shard_map/pallas_call | solution.py:361
  103.0 0.0 collective-permute-done.6.left_ref
  103.0 0.0 collective-permute-done.7.right_ref
  103.0 1.1 %shard_map.92 = bf16[128,1024]{1,0:T(8,128)(2,1)} custom-call(bf16[256,1024]{1,0:T(8,128)(2,1)S(1)} %get-tuple-element.29.x1_ref, bf16[128,1024]{1,0:T(8,128)(2,1)S(1)} %bitcast.11, f32[128,1024]{1,0:T(8,128)S(1)} %get-tuple-element.41.dn_ref, bf16[64,1024]{1,0:T(8,128)(2,1)S(1)} %collective-permute-done.6.left_ref, ...), custom_call_target="tpu_custom_call" | custom-call | tf_op jit(solution)/shard_map/pallas_call | solution.py:361
  (2 shorter events, 0.0 us)
Async XLA Ops:
  2.4 12.2 %copy-start = (bf16[16,8,1024]{2,1,0:T(8,128)(2,1)S(1)}, bf16[16,8,1024]{2,1,0:T(8,128)(2,1)}, u32[]{:S(2)}) copy-start(bf16[16,8,1024]{2,1,0:T(8,128)(2,1)} %param.13) | copy-start | bytes 786436
  3.3 41.1 %copy-start.4 = (bf16[1024,1024]{1,0:T(8,128)(2,1)S(1)}, bf16[1024,1024]{1,0:T(8,128)(2,1)}, u32[]{:S(2)}) copy-start(bf16[1024,1024]{1,0:T(8,128)(2,1)} %wq_ref.5) | copy-start | bytes 6291460
  3.3 32.1 %all-to-all-start = ((bf16[8,48,896]{2,1,0:T(8,128)(2,1)}), bf16[8,48,896]{2,1,0:T(8,128)(2,1)S(1)}, u32[]{:S(2)}, u32[]{:S(2)}) async-start(bf16[8,48,896]{2,1,0:T(8,128)(2,1)} %pad_maximum_fusion), calls=%async_computation | async-start | bytes 1376256 | tf_op jit(solution)/shard_map/all_to_all | solution.py:389
  14.6 58.2 %collective-permute-start.5 = (bf16[32,1024]{1,0:T(8,128)(2,1)S(1)}, bf16[32,1024]{1,0:T(8,128)(2,1)S(1)}, u32[]{:S(2)}, u32[]{:S(2)}) collective-permute-start(bf16[32,1024]{1,0:T(8,128)(2,1)S(1)} %get-tuple-element.44), channel_id=1, source_target_pairs={{32,0},{64,32},{96,64},{128,96},{160,128},{192,160},{224,192},{33,... | collective-permute-start | bytes 196616 | tf_op jit(solution)/shard_map/ppermute | solution.py:374
  15.9 56.9 %collective-permute-start.4 = (bf16[32,1024]{1,0:T(8,128)(2,1)S(1)}, bf16[32,1024]{1,0:T(8,128)(2,1)S(1)}, u32[]{:S(2)}, u32[]{:S(2)}) collective-permute-start(bf16[32,1024]{1,0:T(8,128)(2,1)S(1)} %get-tuple-element.45), channel_id=1, source_target_pairs={{0,32},{32,64},{64,96},{96,128},{128,160},{160,192},{192,224},{1,3... | collective-permute-start | bytes 196616 | tf_op jit(solution)/shard_map/ppermute | solution.py:374
  36.1 17.7 %collective-permute-start = (bf16[144,768]{1,0:T(8,128)(2,1)S(1)}, bf16[144,768]{1,0:T(8,128)(2,1)S(1)}, u32[]{:S(2)}, u32[]{:S(2)}) collective-permute-start(bf16[144,768]{1,0:T(8,128)(2,1)S(1)} %get-tuple-element.23), channel_id=1, source_target_pairs={{0,1},{1,2},{2,3},{3,4},{4,5},{5,6},{6,7},{7,8},{8,9},{9,10},{10,1... | collective-permute-start | bytes 663560 | tf_op jit(solution)/shard_map/ppermute | solution.py:374
  38.1 15.8 %collective-permute-start.1 = (bf16[144,768]{1,0:T(8,128)(2,1)S(1)}, bf16[144,768]{1,0:T(8,128)(2,1)S(1)}, u32[]{:S(2)}, u32[]{:S(2)}) collective-permute-start(bf16[144,768]{1,0:T(8,128)(2,1)S(1)} %get-tuple-element.24), channel_id=1, source_target_pairs={{1,0},{2,1},{3,2},{4,3},{5,4},{6,5},{7,6},{8,7},{9,8},{10,9},{11,1... | collective-permute-start | bytes 663560 | tf_op jit(solution)/shard_map/ppermute | solution.py:374
  44.4 2.2 %copy-start.1 = (bf16[1024,2048]{1,0:T(8,128)(2,1)S(1)}, bf16[1024,2048]{1,0:T(8,128)(2,1)}, u32[]{:S(2)}) copy-start(bf16[1024,2048]{1,0:T(8,128)(2,1)} %wkv_ref.9) | copy-start | bytes 12582916
  46.6 1.4 %copy-start.5 = (bf16[768,1024]{1,0:T(8,128)(2,1)S(1)}, bf16[768,1024]{1,0:T(8,128)(2,1)}, u32[]{:S(2)}) copy-start(bf16[768,1024]{1,0:T(8,128)(2,1)} %we_ref.3) | copy-start | bytes 4718596
  48.0 5.8 %copy-start.2 = (bf16[1024,2048]{1,0:T(8,128)(2,1)S(1)}, bf16[1024,2048]{1,0:T(8,128)(2,1)}, u32[]{:S(2)}) copy-start(bf16[1024,2048]{1,0:T(8,128)(2,1)} %wkv_ref.9) | copy-start | bytes 12582916
  48.0 5.9 %copy-start.3 = (bf16[1024,1024]{1,0:T(8,128)(2,1)S(1)}, bf16[1024,1024]{1,0:T(8,128)(2,1)}, u32[]{:S(2)}) copy-start(bf16[1024,1024]{1,0:T(8,128)(2,1)} %wo_ref.5) | copy-start | bytes 6291460
  64.5 13.2 %collective-permute-start.2 = (bf16[112,1024]{1,0:T(8,128)(2,1)S(1)}, bf16[112,1024]{1,0:T(8,128)(2,1)S(1)}, u32[]{:S(2)}, u32[]{:S(2)}) collective-permute-start(bf16[112,1024]{1,0:T(8,128)(2,1)S(1)} %get-tuple-element.30), channel_id=1, source_target_pairs={{0,1},{1,2},{2,3},{3,4},{4,5},{5,6},{6,7},{7,8},{8,9},{9,10},{10,1... | collective-permute-start | bytes 688136 | tf_op jit(solution)/shard_map/ppermute | solution.py:374
  66.4 11.3 %collective-permute-start.3 = (bf16[112,1024]{1,0:T(8,128)(2,1)S(1)}, bf16[112,1024]{1,0:T(8,128)(2,1)S(1)}, u32[]{:S(2)}, u32[]{:S(2)}) collective-permute-start(bf16[112,1024]{1,0:T(8,128)(2,1)S(1)} %get-tuple-element.31), channel_id=1, source_target_pairs={{1,0},{2,1},{3,2},{4,3},{5,4},{6,5},{7,6},{8,7},{9,8},{10,9},{11,1... | collective-permute-start | bytes 688136 | tf_op jit(solution)/shard_map/ppermute | solution.py:374
  90.8 12.2 %collective-permute-start.6 = (bf16[64,1024]{1,0:T(8,128)(2,1)S(1)}, bf16[64,1024]{1,0:T(8,128)(2,1)S(1)}, u32[]{:S(2)}, u32[]{:S(2)}) collective-permute-start(bf16[64,1024]{1,0:T(8,128)(2,1)S(1)} %get-tuple-element.42), channel_id=1, source_target_pairs={{0,1},{1,2},{2,3},{3,4},{4,5},{5,6},{6,7},{7,8},{8,9},{9,10},{10,1... | collective-permute-start | bytes 393224 | tf_op jit(solution)/shard_map/ppermute | solution.py:374
  92.7 10.3 %collective-permute-start.7 = (bf16[64,1024]{1,0:T(8,128)(2,1)S(1)}, bf16[64,1024]{1,0:T(8,128)(2,1)S(1)}, u32[]{:S(2)}, u32[]{:S(2)}) collective-permute-start(bf16[64,1024]{1,0:T(8,128)(2,1)S(1)} %get-tuple-element.43), channel_id=1, source_target_pairs={{1,0},{2,1},{3,2},{4,3},{5,4},{6,5},{7,6},{8,7},{9,8},{10,9},{11,1... | collective-permute-start | bytes 393224 | tf_op jit(solution)/shard_map/ppermute | solution.py:374

commit v2 on v1

--- a/solution.py
+++ b/solution.py
@@ -41,7 +41,7 @@
 
 
 def cols(index):
-    return pl.ds(pl.multiple_of(index * LANES, LANES), LANES)
+    return slice(index * LANES, index * LANES + LANES)
 
 
 def head_masks():
@@ -66,10 +66,10 @@
     token, key = iota(shape, 0), iota(shape, 1)
     query_row, query_col = token >> 3, token & 7
     side = key - 128
-    left = key < 192
+    right = (key < 192) == ((col_index & 1) == 0)
     rim = side & 63
     key_row = jnp.where(key < 128, key >> 3, rim >> 2)
-    rim_col = jnp.where(left, (rim & 3) - 4, (rim & 3) + 8)
+    rim_col = jnp.where(right, (rim & 3) + 8, (rim & 3) - 4)
     key_col = jnp.where(key < 128, key & 7, rim_col)
     row_gap = key_row - query_row - 4
     col_gap = key_col - query_col
@@ -87,40 +87,82 @@
     return weight, 1.0 / jnp.where(total > 0, total, 1.0)
 
 
-def place_kernel(recv_ref, own_ref, left_ref, right_ref):
-    sources, slots = [], []
-    for tile in range(3):
-        part = recv_ref[:, 16 * tile : 16 * tile + 16, :].reshape(128, PIX + 128)
-        sources.append(part[:, :PIX])
-        slot = part[:, PIX:].astype(F32).T + 128.0 * tile
-        slots.append(slot[:8])
-    source = jnp.concatenate(sources, axis=0)
-    slot = jnp.concatenate(slots, axis=1)
+def pack_kernel(place_ref, patches_ref, slot_ref, own_ref, far_ref, slot_s, wide_s, sems):
+    half = place_ref[0] >> 2
+    copies = [pltpu.make_async_copy(slot_ref, slot_s, sems.at[0])]
+    for i, (target, side) in enumerate(((own_ref, half), (far_ref, 1 - half))):
+        copies.append(
+            pltpu.make_async_copy(
+                patches_ref.at[pl.ds(pl.multiple_of(48 * side, 16), 80), :],
+                target.at[pl.ds(pl.multiple_of(16 - 16 * side, 16), 80), pl.ds(0, PIX)],
+                sems.at[i + 1],
+            )
+        )
+    for copy in copies:
+        copy.start()
+    for copy in copies:
+        copy.wait()
+    wide_s[...] = jnp.broadcast_to(slot_s[...].astype(F32), (128, 128)).T.astype(BF)
+    for target, side in ((own_ref, half), (far_ref, 1 - half)):
+        target[pl.ds(pl.multiple_of(80 * side, 16), 16), :] = jnp.zeros((16, PIX + 128), BF)
+        target[pl.ds(pl.multiple_of(16 - 16 * side, 16), 80), PIX:] = wide_s[
+            pl.ds(pl.multiple_of(48 * side, 16), 80), :
+        ]
+
+
+def windows(place_ref, own_ref, far_ref, step):
+    start = pl.multiple_of(((place_ref[0] & 3) ^ step) * 16, 16)
+    return own_ref[pl.ds(start, 48), :], far_ref[pl.ds(start, 48), :]
+
+
+def spread_kernel(place_ref, own_ref, far_ref, touched_ref, *out_refs):
+    for step, out_ref in zip((2, 3, 1), out_refs):
+        near, far = windows(place_ref, own_ref, far_ref, step)
+        out_ref[0:48, :] = near
+        out_ref[48:96, :] = far
+
+
+def place_kernel(
+    place_ref, own_in_ref, far_in_ref, in2_ref, in3_ref, in1_ref, own_ref, go_a_ref, go_b_ref
+):
+    near, far = windows(place_ref, own_in_ref, far_in_ref, 0)
+    source = jnp.concatenate([near, far, in2_ref[...], in3_ref[...], in1_ref[...]], axis=0)
+    slots = []
+    for part in range(3):
+        slots.append(source[128 * part : 128 * part + 128, PIX:].astype(F32).T[:8])
+    tile = lax.rem(iota((8, 384), 1) >> 4, 3)
+    slot = jnp.concatenate(slots, axis=1) + 128.0 * tile.astype(F32)
+    source = source[:, :PIX]
+    even = 1 - (place_ref[1] & 1)
 
     def pick(position):
-        hot = jnp.where(position == slot[:1], 1.0, 0.0).astype(BF)
+        hot = jnp.where(position.astype(F32) == slot[:1], 1.0, 0.0).astype(BF)
         return dot(hot, source).astype(BF)
 
-    own_ref[...] = pick((iota((320, 384), 0) + 32).astype(F32))
+    own_ref[...] = pick(iota((320, 384), 0) + 32)
     n = iota((144, 384), 0)
     edge = ((n >> 2) + 6) * 8 + (n & 3)
-    left_ref[...] = pick(edge.astype(F32))
-    right_ref[...] = pick((edge + 4).astype(F32))
+    go_a_ref[...] = pick(edge + 4 * even)
+    go_b_ref[...] = pick(edge + 4 * (1 - even))
+
+
+def touch_kernel(we_ref, wq_ref, wkv_ref, wo_ref, out_ref):
+    total = we_ref[0:16, 0:128].astype(F32) + wq_ref[0:16, 0:128].astype(F32)
+    total = total + wkv_ref[0:16, 0:128].astype(F32) + wo_ref[0:16, 0:128].astype(F32)
+    out_ref[...] = total
 
 
 def own_first_kernel(own_ref, we_ref, wq_ref, wkv_ref, x0_ref, q_ref, kv_ref, x_s, n_s):
     means = group_mean_matrix()
 
-    @pl.loop(0, GROUPS)
-    def _(g):
+    for g in range(GROUPS):
         x_s[:, cols(g)] = dot(own_ref[...], we_ref[:, cols(g)]).astype(BF).astype(F32)
 
     residual = x_s[...]
     n_s[...] = (residual * row_scale(residual)).astype(BF)
     x0_ref[...] = residual[32:288].astype(BF)
 
-    @pl.loop(0, GROUPS)
-    def _(g):
+    for g in range(GROUPS):
         query = dot(n_s[32:288, :], wq_ref[:, cols(g)])
         query = query * lax.rsqrt(group_mean(query * query, means) + EPSILON)
         q_ref[:, cols(g)] = (query.astype(BF) * 0.125).astype(BF)
@@ -151,23 +193,21 @@
 
 def first_core_kernel(
     grid_rows, grid_cols,
-    place_ref, left_ref, right_ref, we_ref, wkv_ref, wo_ref, x0_ref, q_ref, kv_ref,
-    x1_ref, go_left_ref, go_right_ref,
+    place_ref, a_ref, b_ref, we_ref, wkv_ref, wo_ref, x0_ref, q_ref, kv_ref,
+    x1_ref, go_a_ref, go_b_ref,
     p_s, x_s, n_s, rim_s, o_s, mask_s,
 ):
     means = group_mean_matrix()
-    p_s[0:144, :] = left_ref[...]
-    p_s[144:288, :] = right_ref[...]
-
-    @pl.loop(0, GROUPS)
-    def _(g):
+    p_s[0:144, :] = a_ref[...]
+    p_s[144:288, :] = b_ref[...]
+
+    for g in range(GROUPS):
         x_s[:, cols(g)] = dot(p_s[...], we_ref[:, cols(g)]).astype(BF).astype(F32)
 
     residual = x_s[...]
     n_s[...] = (residual * row_scale(residual)).astype(BF)
 
-    @pl.loop(0, GROUPS)
-    def _(g):
+    for g in range(GROUPS):
         key = dot(n_s[...], wkv_ref[:, cols(g)])
         key = key * lax.rsqrt(group_mean(key * key, means) + EPSILON)
         rim_s[:, cols(g)] = padded_rim(key).astype(BF)
@@ -179,8 +219,7 @@
         mask_s[block] = block_mask(first_row + 8 * block, place_ref[1], grid_rows, grid_cols)
     masks = head_masks()
 
-    @pl.loop(0, GROUPS)
-    def _(g):
+    for g in range(GROUPS):
         for block in range(4):
             query = stack_heads(q_ref[64 * block : 64 * block + 64, cols(g)], masks)
             key = keys_of(kv_ref, rim_s, block, g)
@@ -192,16 +231,16 @@
     n = iota((112, 256), 0)
     edge = ((n >> 2) + 2) * 8 + (n & 3)
     source = iota((112, 256), 1)
-    pick_left = jnp.where(edge == source, 1.0, 0.0).astype(BF)
-    pick_right = jnp.where(edge + 4 == source, 1.0, 0.0).astype(BF)
-
-    @pl.loop(0, GROUPS)
-    def _(g):
+    even = 1 - (place_ref[1] & 1)
+    pick_a = jnp.where(edge + 4 * even == source, 1.0, 0.0).astype(BF)
+    pick_b = jnp.where(edge + 4 * (1 - even) == source, 1.0, 0.0).astype(BF)
+
+    for g in range(GROUPS):
         total = x0_ref[:, cols(g)].astype(F32) + dot(o_s[...], wo_ref[:, cols(g)])
         total = total.astype(BF)
         x1_ref[:, cols(g)] = total
-        go_left_ref[:, cols(g)] = dot(pick_left, total).astype(BF)
-        go_right_ref[:, cols(g)] = dot(pick_right, total).astype(BF)
+        go_a_ref[:, cols(g)] = dot(pick_a, total).astype(BF)
+        go_b_ref[:, cols(g)] = dot(pick_b, total).astype(BF)
 
 
 def own_second_kernel(
@@ -216,8 +255,7 @@
     c_s[32:160, :] = cot_ref[...]
     c_s[160:192, :] = below_ref[...]
 
-    @pl.loop(0, GROUPS)
-    def _(g):
+    for g in range(GROUPS):
         query = dot(n_s[32:224, :], wq_ref[:, cols(g)])
         scale = lax.rsqrt(group_mean(query * query, means) + EPSILON)
         q_ref[:, cols(g)] = ((query * scale).astype(BF) * 0.125).astype(BF)
@@ -236,17 +274,16 @@
 
 def second_core_kernel(
     grid_rows, grid_cols,
-    place_ref, left_ref, right_ref, wkv_ref, q_ref, kv_ref, do_ref,
-    o_ref, dq_ref, dkv_ref, go_left_ref, go_right_ref,
+    place_ref, a_ref, b_ref, wkv_ref, q_ref, kv_ref, do_ref,
+    o_ref, dq_ref, dkv_ref, go_a_ref, go_b_ref,
     n_s, rim_s, rs_s, db_s, mask_s,
 ):
     means = group_mean_matrix()
-    residual = jnp.concatenate([left_ref[...].astype(F32), right_ref[...].astype(F32)], axis=0)
+    residual = jnp.concatenate([a_ref[...].astype(F32), b_ref[...].astype(F32)], axis=0)
     residual = padded_rim(residual)
     n_s[...] = (residual * row_scale(residual)).astype(BF)
 
-    @pl.loop(0, GROUPS)
-    def _(g):
+    for g in range(GROUPS):
         key = dot(n_s[...], wkv_ref[:, cols(g)])
         scale = lax.rsqrt(group_mean(key * key, means) + EPSILON)
         rim_s[:, cols(g)] = (key * scale).astype(BF)
@@ -259,8 +296,7 @@
         mask_s[block] = block_mask(first_row + 8 * block, place_ref[1], grid_rows, grid_cols)
     masks = head_masks()
 
-    @pl.loop(0, GROUPS)
-    def _(g):
+    for g in range(GROUPS):
         key_backs, value_backs = [], []
         for block in range(3):
             query = stack_heads(q_ref[64 * block : 64 * block + 64, cols(g)], masks)
@@ -303,11 +339,10 @@
         dkv_ref[:, cols(g + GROUPS)] = own.astype(BF)
         db_s[:, cols(g + GROUPS)] = rim.astype(BF)
 
-    @pl.loop(0, GROUPS)
-    def _(g):
+    for g in range(GROUPS):
         back = dot(db_s[...], wkv_ref[cols(g), :], NT).astype(BF)
-        go_left_ref[:, cols(g)] = back[:64]
-        go_right_ref[:, cols(g)] = back[64:]
+        go_a_ref[:, cols(g)] = back[:64]
+        go_b_ref[:, cols(g)] = back[64:]
 
 
 def own_back_kernel(
@@ -317,8 +352,7 @@
 ):
     means = group_mean_matrix()
 
-    @pl.loop(0, GROUPS)
-    def _(g):
+    for g in range(GROUPS):
         total = x1_ref[64:192, cols(g)].astype(F32) + dot(o_ref[32:160, :], wo_ref[:, cols(g)])
         out_ref[:, cols(g)] = total.astype(BF)
         back = dq_ref[32:160, cols(g)].astype(F32) * 0.125
@@ -329,20 +363,18 @@
         b_s[:, cols(g)] = head_scale_back(back, normed, rsk_ref[:, cols(g)], means).astype(BF)
         b_s[:, cols(g + GROUPS)] = dkv_ref[:, cols(g + GROUPS)]
 
-    @pl.loop(0, GROUPS)
-    def _(g):
+    for g in range(GROUPS):
         back = dot(a_s[...], wq_ref[cols(g), :], NT) + dot(b_s[...], wkv_ref[cols(g), :], NT)
         dn_ref[:, cols(g)] = back
 
 
-def last_kernel(x1_ref, cot_ref, dn_ref, left_ref, right_ref, out_ref):
-    n, source = iota((128, 64), 0), iota((128, 64), 1)
-    column = n & 7
-    place = (n >> 3) * 4 + (column & 3)
-    from_left = jnp.where((place == source) & (column < 4), 1.0, 0.0).astype(BF)
-    from_right = jnp.where((place == source) & (column >= 4), 1.0, 0.0).astype(BF)
-    pick = jnp.concatenate([from_left, from_right], axis=1)
-    arrived = jnp.concatenate([left_ref[...], right_ref[...]], axis=0)
+def last_kernel(place_ref, x1_ref, cot_ref, dn_ref, a_ref, b_ref, out_ref):
+    n, source = iota((128, 128), 0), iota((128, 128), 1)
+    right = (source < 64) == ((place_ref[1] & 1) == 0)
+    column = jnp.where(right, (source & 3) + 4, source & 3)
+    token = ((source & 63) >> 2) * 8 + column
+    pick = jnp.where(n == token, 1.0, 0.0).astype(BF)
+    arrived = jnp.concatenate([a_ref[...], b_ref[...]], axis=0)
     back = dn_ref[...] + dot(pick, arrived)
     residual = x1_ref[64:192, :].astype(F32)
     scale = row_scale(residual)
@@ -351,9 +383,9 @@
     out_ref[...] = (cot_ref[...].astype(F32) + scale * (back - normed * mean)).astype(BF)
 
 
-def call(kernel, out_shapes, *operands, scratch=(), flops=0, moved=0, small=None):
+def call(kernel, out_shapes, *operands, scratch=(), flops=0, moved=0, small=None, hbm=False):
     vmem = pl.BlockSpec(memory_space=pltpu.VMEM)
-    in_specs = [vmem] * len(operands)
+    in_specs = [pl.BlockSpec(memory_space=pltpu.HBM) if hbm else vmem] * len(operands)
     if small is not None:
         operands = (small,) + operands
         in_specs = [pl.BlockSpec(memory_space=pltpu.SMEM)] + in_specs
@@ -363,8 +395,8 @@
         out_shape=shapes,
         in_specs=in_specs,
         out_specs=tuple(vmem for _ in shapes),
-        scratch_shapes=[pltpu.VMEM(s, d) for s, d in scratch],
-        compiler_params=pltpu.CompilerParams(vmem_limit_bytes=40 * 1024 * 1024),
+        scratch_shapes=[s if d is None else pltpu.VMEM(s, d) for s, d in scratch],
+        compiler_params=pltpu.CompilerParams(vmem_limit_bytes=32 * 1024 * 1024),
         cost_estimate=pl.CostEstimate(flops=flops, bytes_accessed=moved, transcendentals=0),
     )(*operands)
 
@@ -374,6 +406,17 @@
     return lax.ppermute(
         values, axis, [(i, i + step) for i in range(peers) if 0 <= i + step < peers]
     )
+
+
+def trade(values, axis, step):
+    return lax.ppermute(values, axis, [(i, i ^ step) for i in range(lax.axis_size(axis))])
+
+
+def trade_sides(go_a, go_b):
+    peers = lax.axis_size("col")
+    across = [(i, ((i + 1) ^ 1) - 1) for i in range(peers)]
+    b = lax.ppermute(go_b, "col", [(i, j) for i, j in across if 0 <= j < peers])
+    return trade(go_a, "col", 1), b
 
 
 def on_device(patches, tile_slot, w_embed, w_query, w_keyval, w_out, cotangent):
@@ -381,21 +424,32 @@
     grid_rows, grid_cols = rows * 16, columns * 8
     place = jnp.stack([lax.axis_index("row"), lax.axis_index("col")]).astype(jnp.int32)
     cot = cotangent.reshape(128, D)
-
-    slot = jnp.broadcast_to(tile_slot.astype(BF)[:, None], (128, 128))
-    block = jnp.concatenate([patches, slot], axis=1).reshape(rows, 16, PIX + 128)
-    wide = jnp.pad(block, ((1, 1), (0, 0), (0, 0)))
-    block = jnp.concatenate([wide[:-2], wide[1:-1], wide[2:]], axis=1)
-    arrived = lax.all_to_all(block, "row", split_axis=0, concat_axis=0, tiled=True)
+    window = ((96, PIX + 128), BF)
+
+    own, far = call(
+        pack_kernel, (window, window), patches, tile_slot.reshape(1, 128),
+        small=place, hbm=True,
+        scratch=(
+            ((1, 128), jnp.int32), ((128, 128), BF), (pltpu.SemaphoreType.DMA((3,)), None)
+        ),
+    )
+    far = trade(far, "row", 4)
+    (touched,) = call(
+        touch_kernel, (((16, 128), F32),), w_embed, w_query, w_keyval, w_out
+    )
+    sends = call(spread_kernel, (window, window, window), own, far, touched, small=place)
+    arrived = [trade(send, "row", step) for send, step in zip(sends, (2, 3, 1))]
 
     above = shift(cot[96:], "row", 1)
     below = shift(cot[:32], "row", -1)
 
-    own, go_left, go_right = call(
-        place_kernel, (((320, PIX), BF), ((144, PIX), BF), ((144, PIX), BF)), arrived
-    )
-    left = shift(go_right, "col", 1)
-    right = shift(go_left, "col", -1)
+    own, go_a, go_b = call(
+        place_kernel,
+        (((320, PIX), BF), ((144, PIX), BF), ((144, PIX), BF)),
+        own, far, *arrived,
+        small=place,
+    )
+    a, b = trade_sides(go_a, go_b)
     x0, queries, keyval = call(
         own_first_kernel,
         (((256, D), BF), ((256, D), BF), ((320, 2 * D), BF)),
@@ -403,10 +457,10 @@
         scratch=(((320, D), F32), ((320, D), BF)),
         flops=8 * 10**9, moved=8 * 10**6,
     )
-    x1, go_left, go_right = call(
+    x1, go_a, go_b = call(
         functools.partial(first_core_kernel, grid_rows, grid_cols),
         (((256, D), BF), ((112, D), BF), ((112, D), BF)),
-        left, right, w_embed, w_keyval, w_out, x0, queries, keyval,
+        a, b, w_embed, w_keyval, w_out, x0, queries, keyval,
         small=place,
         scratch=(
             ((288, PIX), BF), ((288, D), F32), ((288, D), BF), ((320, 2 * D), BF), ((256, D), BF),
@@ -414,8 +468,7 @@
         ),
         flops=8 * 10**9, moved=8 * 10**6,
     )
-    left = shift(go_right, "col", 1)
-    right = shift(go_left, "col", -1)
+    a, b = trade_sides(go_a, go_b)
     queries, keyval, out_back, query_scale, key_scale = call(
         own_second_kernel,
         (((192, D), BF), ((256, 2 * D), BF), ((192, D), BF), ((128, D), F32), ((128, D), F32)),
@@ -423,10 +476,10 @@
         scratch=(((256, D), BF), ((192, D), BF)),
         flops=8 * 10**9, moved=8 * 10**6,
     )
-    attended, dq, dkv, go_left, go_right = call(
+    attended, dq, dkv, go_a, go_b = call(
         functools.partial(second_core_kernel, grid_rows, grid_cols),
         (((192, D), BF), ((192, D), BF), ((128, 2 * D), BF), ((64, D), BF), ((64, D), BF)),
-        left, right, w_keyval, queries, keyval, out_back,
+        a, b, w_keyval, queries, keyval, out_back,
         small=place,
         scratch=(
             ((256, D), BF), ((256, 2 * D), BF), ((128, D), F32), ((128, 2 * D), BF),
@@ -434,8 +487,7 @@
         ),
         flops=8 * 10**9, moved=8 * 10**6,
     )
-    left = shift(go_right, "col", 1)
-    right = shift(go_left, "col", -1)
+    a, b = trade_sides(go_a, go_b)
     final_tokens, back = call(
         own_back_kernel,
         (((128, D), BF), ((128, D), F32)),
@@ -443,7 +495,7 @@
         scratch=(((128, D), BF), ((128, 2 * D), BF)),
         flops=8 * 10**9, moved=8 * 10**6,
     )
-    (input_grad,) = call(last_kernel, (((128, D), BF),), x1, cot, back, left, right)
+    (input_grad,) = call(last_kernel, (((128, D), BF),), x1, cot, back, a, b, small=place)
     return final_tokens.reshape(16, 8, D), input_grad.reshape(16, 8, D)
 
 

time: 105 us -> 84.7 us (0.81)
  the two profiles are of different devices: /device:TPU:2 before, /device:TPU:30 now
where the time goes in v2:
time: 84.7 us; the launch traced here: 84.3 us
  starting transfers between devices  35 us (41%)
  Pallas kernels  31.8 us (38%)
  local copies, waits for them, and re-layouts  8.39 us (10%)
  waiting for transfers between devices  8.14 us (10%)
  between operations  0.87 us (1%)
    pallas_call x10, Pallas kernels, call(): pl.pallas_call(kernel, out_shape=shapes, in_specs=in_specs, out_specs=tup...  31.8 us
    ppermute x3, starting transfers between devices, trade_sides(): b = lax.ppermute(go_b, 'col', [(i, j) for i, j in across if 0 <= j < peers])  11.9 us
    ppermute x2, starting transfers between devices, shift(): lax.ppermute(values, axis, [(i, i + step) for i in range(peers) if 0 <= i...  11.9 us
    ppermute x7, starting transfers between devices, trade(): lax.ppermute(values, axis, [(i, i ^ step) for i in range(lax.axis_size(ax...  11.3 us
    unnamed x22, local copies, waits for them, and re-layouts  8.38 us
    ppermute x3, waiting for transfers between devices, trade_sides(): b = lax.ppermute(go_b, 'col', [(i, j) for i, j in across if 0 <= j < peers])  8.11 us
  transfers between devices with their start and end apart: 12, of which 3 were waited for; matrix products, arithmetic and copies ran while one was open for 0% of the time, Pallas kernels for 23%

profile of v2, /device:TPU:30, one launch (start us, length us, event | category | flops | bytes accessed | tf_op | source)
XLA Modules:
  0.0 84.3 jit_solution(11409102894449264292)
XLA Ops:
  0.6 0.1 pad_add_fusion.place_ref
  0.7 0.0 copy-start.9
  0.7 0.9 %copy-done.9 = bf16[128,768]{1,0:T(8,128)(2,1)S(1)} copy-done((bf16[128,768]{1,0:T(8,128)(2,1)S(1)}, bf16[128,768]{1,0:T(8,128)(2,1)}, u32[]{:S(2)}) %copy-start.9) | copy-done | bytes 196632
  1.6 0.7 copy-done.10
  2.3 0.7 shard_map.86
  3.0 7.3 %collective-permute-start = (bf16[96,896]{1,0:T(8,128)(2,1)S(1)}, bf16[96,896]{1,0:T(8,128)(2,1)S(1)}, u32[]{:S(2)}, u32[]{:S(2)}) collective-permute-start(bf16[96,896]{1,0:T(8,128)(2,1)S(1)} %get-tuple-element.29), channel_id=1, source_target_pairs={{0,128},{32,160},{64,192},{96,224},{128,0},{160,32},{192,64},{224,... | collective-permute-start | bytes 516104 | tf_op jit(solution)/shard_map/ppermute | solution.py:412
  10.3 2.2 %copy-done = bf16[1024,2048]{1,0:T(8,128)(2,1)S(1)} copy-done((bf16[1024,2048]{1,0:T(8,128)(2,1)S(1)}, bf16[1024,2048]{1,0:T(8,128)(2,1)}, u32[]{:S(2)}) %copy-start) | copy-done | bytes 4194328
  12.5 1.6 %copy-done.2 = bf16[1024,1024]{1,0:T(8,128)(2,1)S(1)} copy-done((bf16[1024,1024]{1,0:T(8,128)(2,1)S(1)}, bf16[1024,1024]{1,0:T(8,128)(2,1)}, u32[]{:S(2)}) %copy-start.2) | copy-done | bytes 2097176
  14.1 1.6 %copy-done.4 = bf16[1024,1024]{1,0:T(8,128)(2,1)S(1)} copy-done((bf16[1024,1024]{1,0:T(8,128)(2,1)S(1)}, bf16[1024,1024]{1,0:T(8,128)(2,1)}, u32[]{:S(2)}) %copy-start.4) | copy-done | bytes 2097176
  15.7 1.4 %copy-done.6 = bf16[768,1024]{1,0:T(8,128)(2,1)S(1)} copy-done((bf16[768,1024]{1,0:T(8,128)(2,1)S(1)}, bf16[768,1024]{1,0:T(8,128)(2,1)}, u32[]{:S(2)}) %copy-start.6) | copy-done | bytes 1572888
  17.1 0.0 collective-permute-done.far_ref.far_in_ref
  17.1 0.6 shard_map.88
  17.7 1.3 %collective-permute-start.1 = (bf16[96,896]{1,0:T(8,128)(2,1)S(1)}, bf16[96,896]{1,0:T(8,128)(2,1)S(1)}, u32[]{:S(2)}, u32[]{:S(2)}) collective-permute-start(bf16[96,896]{1,0:T(8,128)(2,1)S(1)} %get-tuple-element.30), channel_id=1, source_target_pairs={{0,64},{32,96},{64,0},{96,32},{128,192},{160,224},{192,128},{224,1... | collective-permute-start | bytes 516104 | tf_op jit(solution)/shard_map/ppermute | solution.py:412
  19.0 2.2 %collective-permute-start.2 = (bf16[96,896]{1,0:T(8,128)(2,1)S(1)}, bf16[96,896]{1,0:T(8,128)(2,1)S(1)}, u32[]{:S(2)}, u32[]{:S(2)}) collective-permute-start(bf16[96,896]{1,0:T(8,128)(2,1)S(1)} %get-tuple-element.31), channel_id=1, source_target_pairs={{0,96},{32,64},{64,32},{96,0},{128,224},{160,192},{192,160},{224,1... | collective-permute-start | bytes 516104 | tf_op jit(solution)/shard_map/ppermute | solution.py:412
  21.2 0.1 collective-permute-start.3
  21.3 0.0 copy-done.8
  21.3 3.9 %collective-permute-start.9 = (bf16[32,1024]{1,0:T(8,128)(2,1)S(1)}, bf16[32,1024]{1,0:T(8,128)(2,1)S(1)}, u32[]{:S(2)}, u32[]{:S(2)}) collective-permute-start(bf16[32,1024]{1,0:T(8,128)(2,1)S(1)} %get-tuple-element.54), channel_id=1, source_target_pairs={{32,0},{64,32},{96,64},{128,96},{160,128},{192,160},{224,192},{33,... | collective-permute-start | bytes 196616 | tf_op jit(solution)/shard_map/ppermute | solution.py:406
  25.2 8.0 %collective-permute-start.8 = (bf16[32,1024]{1,0:T(8,128)(2,1)S(1)}, bf16[32,1024]{1,0:T(8,128)(2,1)S(1)}, u32[]{:S(2)}, u32[]{:S(2)}) collective-permute-start(bf16[32,1024]{1,0:T(8,128)(2,1)S(1)} %get-tuple-element.55), channel_id=1, source_target_pairs={{0,32},{32,64},{64,96},{96,128},{128,160},{160,192},{192,224},{1,3... | collective-permute-start | bytes 196616 | tf_op jit(solution)/shard_map/ppermute | solution.py:406
  33.2 0.0 collective-permute-done.1.in2_ref
  33.2 0.0 collective-permute-done.2.in3_ref
  33.2 0.0 collective-permute-done.3.in1_ref
  33.2 1.2 %shard_map.89 = (bf16[320,768]{1,0:T(8,128)(2,1)S(1)}, bf16[144,768]{1,0:T(8,128)(2,1)S(1)}, bf16[144,768]{1,0:T(8,128)(2,1)S(1)}) custom-call(s32[2]{0:T(128)S(1)} %pad_add_fusion.place_ref, bf16[96,896]{1,0:T(8,128)(2,1)S(1)} %get-tuple-element.28.own_ref.own_in_ref, bf16[96,896]{1,0:T(8,128)(2,1)S(1)} %collective-permute-done.far_ref.far_in_ref, ...), custom_call_target="tpu_custom_call" | custom-call | tf_op jit(solution)/shard_map/pallas_call | solution.py:393
  34.5 0.1 collective-permute-start.4
  34.6 4.9 %collective-permute-start.5 = (bf16[144,768]{1,0:T(8,128)(2,1)S(1)}, bf16[144,768]{1,0:T(8,128)(2,1)S(1)}, u32[]{:S(2)}, u32[]{:S(2)}) collective-permute-start(bf16[144,768]{1,0:T(8,128)(2,1)S(1)} %get-tuple-element.34), channel_id=1, source_target_pairs={{1,2},{2,1},{3,4},{4,3},{5,6},{6,5},{7,8},{8,7},{9,10},{10,9},{11,... | collective-permute-start | bytes 663560 | tf_op jit(solution)/shard_map/ppermute | solution.py:418
  39.5 0.0 copy-done.3
  39.5 0.0 copy-done.7
  39.5 0.0 copy-start.1
  39.5 0.0 copy-start.5
  39.6 4.3 %shard_map.90 = (bf16[256,1024]{1,0:T(8,128)(2,1)S(1)}, bf16[256,1024]{1,0:T(8,128)(2,1)S(1)}, bf16[320,2048]{1,0:T(8,128)(2,1)S(1)}) custom-call(bf16[320,768]{1,0:T(8,128)(2,1)S(1)} %get-tuple-element.35.own_ref, bf16[768,1024]{1,0:T(8,128)(2,1)S(1)} %copy-done.7, bf16[1024,1024]{1,0:T(8,128)(2,1)S(1)} %copy-done.3, bf16[1024,2048]{1,0:T(8,128)(2,1)S(1)} %copy-done), custom_call_target="tpu_custom_call" | custom-call | flops 8000000000 | bytes 8000000 | tf_op jit(solution)/shard_map/pallas_call | solution.py:393
  43.9 0.0 collective-permute-done.4.a_ref
  43.9 2.2 %collective-permute-done.5.b_ref = bf16[144,768]{1,0:T(8,128)(2,1)S(1)} collective-permute-done((bf16[144,768]{1,0:T(8,128)(2,1)S(1)}, bf16[144,768]{1,0:T(8,128)(2,1)S(1)}, u32[]{:S(2)}, u32[]{:S(2)}) %collective-permute-start.5) | collective-permute-done | bytes 221216 | tf_op jit(solution)/shard_map/ppermute | solution.py:418
  46.1 0.0 copy-done.1
  46.1 0.0 copy-done.5
  46.1 6.3 %shard_map.91 = (bf16[256,1024]{1,0:T(8,128)(2,1)S(1)}, bf16[112,1024]{1,0:T(8,128)(2,1)S(1)}, bf16[112,1024]{1,0:T(8,128)(2,1)S(1)}) custom-call(s32[2]{0:T(128)S(1)} %pad_add_fusion.place_ref, bf16[144,768]{1,0:T(8,128)(2,1)S(1)} %collective-permute-done.4.a_ref, bf16[144,768]{1,0:T(8,128)(2,1)S(1)} %collective-permute-done.5.b_ref, ...), custom_call_target="tpu_custom_call" | custom-call | flops 8000000000 | bytes 8000000 | tf_op jit(solution)/shard_map/pallas_call | solution.py:393
  52.5 0.3 collective-permute-start.6
  52.7 4.1 %collective-permute-start.7 = (bf16[112,1024]{1,0:T(8,128)(2,1)S(1)}, bf16[112,1024]{1,0:T(8,128)(2,1)S(1)}, u32[]{:S(2)}, u32[]{:S(2)}) collective-permute-start(bf16[112,1024]{1,0:T(8,128)(2,1)S(1)} %get-tuple-element.41), channel_id=1, source_target_pairs={{1,2},{2,1},{3,4},{4,3},{5,6},{6,5},{7,8},{8,7},{9,10},{10,9},{11,... | collective-permute-start | bytes 688136 | tf_op jit(solution)/shard_map/ppermute | solution.py:418
  56.8 0.0 collective-permute-done.9.below_ref
  56.8 0.0 collective-permute-done.8.above_ref
  56.8 4.2 %shard_map.92 = (bf16[192,1024]{1,0:T(8,128)(2,1)S(1)}, bf16[256,2048]{1,0:T(8,128)(2,1)S(1)}, bf16[192,1024]{1,0:T(8,128)(2,1)S(1)}, f32[128,1024]{1,0:T(8,128)S(1)}, f32[128,1024]{1,0:T(8,128)S(1)}) custom-call(bf16[256,1024]{1,0:T(8,128)(2,1)S(1)} %get-tuple-element.39.x1_ref, bf16[128,1024]{1,0:T(8,128)(2,1)S(1)} %bitcast.10, ...), custom_call_target="tpu_custom_call" | custom-call | flops 8000000000 | bytes 8000000 | tf_op jit(solution)/shard_map/pallas_call | solution.py:393
  61.0 0.0 collective-permute-done.6.a_ref
  61.0 3.1 %collective-permute-done.7.b_ref = bf16[112,1024]{1,0:T(8,128)(2,1)S(1)} collective-permute-done((bf16[112,1024]{1,0:T(8,128)(2,1)S(1)}, bf16[112,1024]{1,0:T(8,128)(2,1)S(1)}, u32[]{:S(2)}, u32[]{:S(2)}) %collective-permute-start.7) | collective-permute-done | bytes 229408 | tf_op jit(solution)/shard_map/ppermute | solution.py:418
  64.1 9.5 %shard_map.93 = (bf16[192,1024]{1,0:T(8,128)(2,1)S(1)}, bf16[192,1024]{1,0:T(8,128)(2,1)S(1)}, bf16[128,2048]{1,0:T(8,128)(2,1)S(1)}, bf16[64,1024]{1,0:T(8,128)(2,1)S(1)}, bf16[64,1024]{1,0:T(8,128)(2,1)S(1)}) custom-call(s32[2]{0:T(128)S(1)} %pad_add_fusion.place_ref, bf16[112,1024]{1,0:T(8,128)(2,1)S(1)} %collective-permute-done.6.a_ref, ...), custom_call_target="tpu_custom_call" | custom-call | flops 8000000000 | bytes 8000000 | tf_op jit(solution)/shard_map/pallas_call | solution.py:393
  73.6 0.1 collective-permute-start.10
  73.7 2.9 %collective-permute-start.11 = (bf16[64,1024]{1,0:T(8,128)(2,1)S(1)}, bf16[64,1024]{1,0:T(8,128)(2,1)S(1)}, u32[]{:S(2)}, u32[]{:S(2)}) collective-permute-start(bf16[64,1024]{1,0:T(8,128)(2,1)S(1)} %get-tuple-element.53), channel_id=1, source_target_pairs={{1,2},{2,1},{3,4},{4,3},{5,6},{6,5},{7,8},{8,7},{9,10},{10,9},{11,... | collective-permute-start | bytes 393224 | tf_op jit(solution)/shard_map/ppermute | solution.py:418
  76.6 3.3 %shard_map.94 = (bf16[128,1024]{1,0:T(8,128)(2,1)}, f32[128,1024]{1,0:T(8,128)S(1)}) custom-call(bf16[256,1024]{1,0:T(8,128)(2,1)S(1)} %get-tuple-element.39.x1_ref, bf16[192,1024]{1,0:T(8,128)(2,1)S(1)} %get-tuple-element.45.o_ref, bf16[192,1024]{1,0:T(8,128)(2,1)S(1)} %get-tuple-element.46.dq_ref, bf16[128,2048]{1,0:T(8,128)(2,1)S(1)} %get-tuple-element.47.dkv_ref, ...), custom_call_target="tpu_custom_call" | custom-call | flops 8000000000 | bytes 8000000 | tf_op jit(solution)/shard_map/pallas_call | solution.py:393
  79.9 0.0 collective-permute-done.10.a_ref
  79.9 2.8 %collective-permute-done.11.b_ref = bf16[64,1024]{1,0:T(8,128)(2,1)S(1)} collective-permute-done((bf16[64,1024]{1,0:T(8,128)(2,1)S(1)}, bf16[64,1024]{1,0:T(8,128)(2,1)S(1)}, u32[]{:S(2)}, u32[]{:S(2)}) %collective-permute-start.11) | collective-permute-done | bytes 131104 | tf_op jit(solution)/shard_map/ppermute | solution.py:418
  82.7 1.6 %shard_map.95 = bf16[128,1024]{1,0:T(8,128)(2,1)} custom-call(s32[2]{0:T(128)S(1)} %pad_add_fusion.place_ref, bf16[256,1024]{1,0:T(8,128)(2,1)S(1)} %get-tuple-element.39.x1_ref, bf16[128,1024]{1,0:T(8,128)(2,1)S(1)} %bitcast.11, f32[128,1024]{1,0:T(8,128)S(1)} %get-tuple-element.51.dn_ref, bf16[64,1024]{1,0:T(8,128)(2,1)S(1)} %collective-permute-done.10.a_ref, ...), custom_call_target="tpu_custom_call" | custom-call | tf_op jit(solution)/shard_map/pallas_call | solution.py:393
  (10 shorter events, 0.0 us)
Async XLA Ops:
  0.7 0.9 %copy-start.9 = (bf16[128,768]{1,0:T(8,128)(2,1)S(1)}, bf16[128,768]{1,0:T(8,128)(2,1)}, u32[]{:S(2)}) copy-start(bf16[128,768]{1,0:T(8,128)(2,1)} %patches_ref.1) | copy-start | bytes 589828
  1.6 0.7 copy-start.10
  3.0 14.1 %collective-permute-start = (bf16[96,896]{1,0:T(8,128)(2,1)S(1)}, bf16[96,896]{1,0:T(8,128)(2,1)S(1)}, u32[]{:S(2)}, u32[]{:S(2)}) collective-permute-start(bf16[96,896]{1,0:T(8,128)(2,1)S(1)} %get-tuple-element.29), channel_id=1, source_target_pairs={{0,128},{32,160},{64,192},{96,224},{128,0},{160,32},{192,64},{224,... | collective-permute-start | bytes 516104 | tf_op jit(solution)/shard_map/ppermute | solution.py:412
  10.3 2.2 %copy-start = (bf16[1024,2048]{1,0:T(8,128)(2,1)S(1)}, bf16[1024,2048]{1,0:T(8,128)(2,1)}, u32[]{:S(2)}) copy-start(bf16[1024,2048]{1,0:T(8,128)(2,1)} %wkv_ref.11) | copy-start | bytes 12582916
  12.5 1.6 %copy-start.2 = (bf16[1024,1024]{1,0:T(8,128)(2,1)S(1)}, bf16[1024,1024]{1,0:T(8,128)(2,1)}, u32[]{:S(2)}) copy-start(bf16[1024,1024]{1,0:T(8,128)(2,1)} %wq_ref.7) | copy-start | bytes 6291460
  14.1 1.6 %copy-start.4 = (bf16[1024,1024]{1,0:T(8,128)(2,1)S(1)}, bf16[1024,1024]{1,0:T(8,128)(2,1)}, u32[]{:S(2)}) copy-start(bf16[1024,1024]{1,0:T(8,128)(2,1)} %wo_ref.7) | copy-start | bytes 6291460
  15.7 1.4 %copy-start.6 = (bf16[768,1024]{1,0:T(8,128)(2,1)S(1)}, bf16[768,1024]{1,0:T(8,128)(2,1)}, u32[]{:S(2)}) copy-start(bf16[768,1024]{1,0:T(8,128)(2,1)} %we_ref.5) | copy-start | bytes 4718596
  17.1 4.2 %copy-start.8 = (bf16[16,8,1024]{2,1,0:T(8,128)(2,1)S(1)}, bf16[16,8,1024]{2,1,0:T(8,128)(2,1)}, u32[]{:S(2)}) copy-start(bf16[16,8,1024]{2,1,0:T(8,128)(2,1)} %param.13) | copy-start | bytes 786436
  17.1 22.4 %copy-start.3 = (bf16[1024,1024]{1,0:T(8,128)(2,1)S(1)}, bf16[1024,1024]{1,0:T(8,128)(2,1)}, u32[]{:S(2)}) copy-start(bf16[1024,1024]{1,0:T(8,128)(2,1)} %wq_ref.7) | copy-start | bytes 6291460
  17.1 22.4 %copy-start.7 = (bf16[768,1024]{1,0:T(8,128)(2,1)S(1)}, bf16[768,1024]{1,0:T(8,128)(2,1)}, u32[]{:S(2)}) copy-start(bf16[768,1024]{1,0:T(8,128)(2,1)} %we_ref.5) | copy-start | bytes 4718596
  17.7 15.5 %collective-permute-start.1 = (bf16[96,896]{1,0:T(8,128)(2,1)S(1)}, bf16[96,896]{1,0:T(8,128)(2,1)S(1)}, u32[]{:S(2)}, u32[]{:S(2)}) collective-permute-start(bf16[96,896]{1,0:T(8,128)(2,1)S(1)} %get-tuple-element.30), channel_id=1, source_target_pairs={{0,64},{32,96},{64,0},{96,32},{128,192},{160,224},{192,128},{224,1... | collective-permute-start | bytes 516104 | tf_op jit(solution)/shard_map/ppermute | solution.py:412
  19.0 14.2 %collective-permute-start.2 = (bf16[96,896]{1,0:T(8,128)(2,1)S(1)}, bf16[96,896]{1,0:T(8,128)(2,1)S(1)}, u32[]{:S(2)}, u32[]{:S(2)}) collective-permute-start(bf16[96,896]{1,0:T(8,128)(2,1)S(1)} %get-tuple-element.31), channel_id=1, source_target_pairs={{0,96},{32,64},{64,32},{96,0},{128,224},{160,192},{192,160},{224,1... | collective-permute-start | bytes 516104 | tf_op jit(solution)/shard_map/ppermute | solution.py:412
  21.2 12.0 %collective-permute-start.3 = (bf16[96,896]{1,0:T(8,128)(2,1)S(1)}, bf16[96,896]{1,0:T(8,128)(2,1)S(1)}, u32[]{:S(2)}, u32[]{:S(2)}) collective-permute-start(bf16[96,896]{1,0:T(8,128)(2,1)S(1)} %get-tuple-element.32), channel_id=1, source_target_pairs={{0,32},{32,0},{64,96},{96,64},{128,160},{160,128},{192,224},{224,1... | collective-permute-start | bytes 516104 | tf_op jit(solution)/shard_map/ppermute | solution.py:412
  21.3 35.5 %collective-permute-start.9 = (bf16[32,1024]{1,0:T(8,128)(2,1)S(1)}, bf16[32,1024]{1,0:T(8,128)(2,1)S(1)}, u32[]{:S(2)}, u32[]{:S(2)}) collective-permute-start(bf16[32,1024]{1,0:T(8,128)(2,1)S(1)} %get-tuple-element.54), channel_id=1, source_target_pairs={{32,0},{64,32},{96,64},{128,96},{160,128},{192,160},{224,192},{33,... | collective-permute-start | bytes 196616 | tf_op jit(solution)/shard_map/ppermute | solution.py:406
  25.2 31.7 %collective-permute-start.8 = (bf16[32,1024]{1,0:T(8,128)(2,1)S(1)}, bf16[32,1024]{1,0:T(8,128)(2,1)S(1)}, u32[]{:S(2)}, u32[]{:S(2)}) collective-permute-start(bf16[32,1024]{1,0:T(8,128)(2,1)S(1)} %get-tuple-element.55), channel_id=1, source_target_pairs={{0,32},{32,64},{64,96},{96,128},{128,160},{160,192},{192,224},{1,3... | collective-permute-start | bytes 196616 | tf_op jit(solution)/shard_map/ppermute | solution.py:406
  34.5 9.4 %collective-permute-start.4 = (bf16[144,768]{1,0:T(8,128)(2,1)S(1)}, bf16[144,768]{1,0:T(8,128)(2,1)S(1)}, u32[]{:S(2)}, u32[]{:S(2)}) collective-permute-start(bf16[144,768]{1,0:T(8,128)(2,1)S(1)} %get-tuple-element.33), channel_id=1, source_target_pairs={{0,1},{1,0},{2,3},{3,2},{4,5},{5,4},{6,7},{7,6},{8,9},{9,8},{10,11... | collective-permute-start | bytes 663560 | tf_op jit(solution)/shard_map/ppermute | solution.py:412
  34.6 11.6 %collective-permute-start.5 = (bf16[144,768]{1,0:T(8,128)(2,1)S(1)}, bf16[144,768]{1,0:T(8,128)(2,1)S(1)}, u32[]{:S(2)}, u32[]{:S(2)}) collective-permute-start(bf16[144,768]{1,0:T(8,128)(2,1)S(1)} %get-tuple-element.34), channel_id=1, source_target_pairs={{1,2},{2,1},{3,4},{4,3},{5,6},{6,5},{7,8},{8,7},{9,10},{10,9},{11,... | collective-permute-start | bytes 663560 | tf_op jit(solution)/shard_map/ppermute | solution.py:418
  39.5 6.6 %copy-start.1 = (bf16[1024,2048]{1,0:T(8,128)(2,1)S(1)}, bf16[1024,2048]{1,0:T(8,128)(2,1)}, u32[]{:S(2)}) copy-start(bf16[1024,2048]{1,0:T(8,128)(2,1)} %wkv_ref.11) | copy-start | bytes 12582916
  39.5 6.6 %copy-start.5 = (bf16[1024,1024]{1,0:T(8,128)(2,1)S(1)}, bf16[1024,1024]{1,0:T(8,128)(2,1)}, u32[]{:S(2)}) copy-start(bf16[1024,1024]{1,0:T(8,128)(2,1)} %wo_ref.7) | copy-start | bytes 6291460
  52.5 8.5 %collective-permute-start.6 = (bf16[112,1024]{1,0:T(8,128)(2,1)S(1)}, bf16[112,1024]{1,0:T(8,128)(2,1)S(1)}, u32[]{:S(2)}, u32[]{:S(2)}) collective-permute-start(bf16[112,1024]{1,0:T(8,128)(2,1)S(1)} %get-tuple-element.40), channel_id=1, source_target_pairs={{0,1},{1,0},{2,3},{3,2},{4,5},{5,4},{6,7},{7,6},{8,9},{9,8},{10,11... | collective-permute-start | bytes 688136 | tf_op jit(solution)/shard_map/ppermute | solution.py:412
  52.7 11.4 %collective-permute-start.7 = (bf16[112,1024]{1,0:T(8,128)(2,1)S(1)}, bf16[112,1024]{1,0:T(8,128)(2,1)S(1)}, u32[]{:S(2)}, u32[]{:S(2)}) collective-permute-start(bf16[112,1024]{1,0:T(8,128)(2,1)S(1)} %get-tuple-element.41), channel_id=1, source_target_pairs={{1,2},{2,1},{3,4},{4,3},{5,6},{6,5},{7,8},{8,7},{9,10},{10,9},{11,... | collective-permute-start | bytes 688136 | tf_op jit(solution)/shard_map/ppermute | solution.py:418
  73.6 6.3 %collective-permute-start.10 = (bf16[64,1024]{1,0:T(8,128)(2,1)S(1)}, bf16[64,1024]{1,0:T(8,128)(2,1)S(1)}, u32[]{:S(2)}, u32[]{:S(2)}) collective-permute-start(bf16[64,1024]{1,0:T(8,128)(2,1)S(1)} %get-tuple-element.52), channel_id=1, source_target_pairs={{0,1},{1,0},{2,3},{3,2},{4,5},{5,4},{6,7},{7,6},{8,9},{9,8},{10,11... | collective-permute-start | bytes 393224 | tf_op jit(solution)/shard_map/ppermute | solution.py:412
  73.7 9.0 %collective-permute-start.11 = (bf16[64,1024]{1,0:T(8,128)(2,1)S(1)}, bf16[64,1024]{1,0:T(8,128)(2,1)S(1)}, u32[]{:S(2)}, u32[]{:S(2)}) collective-permute-start(bf16[64,1024]{1,0:T(8,128)(2,1)S(1)} %get-tuple-element.53), channel_id=1, source_target_pairs={{1,2},{2,1},{3,4},{4,3},{5,6},{6,5},{7,8},{8,7},{9,10},{10,9},{11,... | collective-permute-start | bytes 393224 | tf_op jit(solution)/shard_map/ppermute | solution.py:418

commit v3 on v2

--- a/solution.py
+++ b/solution.py
@@ -61,53 +61,74 @@
     return jnp.where(lane < 2, low, high)
 
 
-def block_mask(first_row, col_index, grid_rows, grid_cols):
-    shape = (64, 256)
-    token, key = iota(shape, 0), iota(shape, 1)
-    query_row, query_col = token >> 3, token & 7
-    side = key - 128
+def key_places(key, first_row, col_index, grid_rows, grid_cols):
     right = (key < 192) == ((col_index & 1) == 0)
-    rim = side & 63
+    rim = key & 63
     key_row = jnp.where(key < 128, key >> 3, rim >> 2)
     rim_col = jnp.where(right, (rim & 3) + 8, (rim & 3) - 4)
     key_col = jnp.where(key < 128, key & 7, rim_col)
-    row_gap = key_row - query_row - 4
-    col_gap = key_col - query_col
-    near = (row_gap >= -3) & (row_gap <= 3) & (col_gap >= -3) & (col_gap <= 3)
     row = first_row + key_row
     col = col_index * 8 + key_col
     inside = (row >= 0) & (row < grid_rows) & (col >= 0) & (col < grid_cols)
-    mask = jnp.where(near & inside, 1.0, 0.0)
-    return jnp.concatenate([mask] * 4, axis=0)
-
-
-def softmax_parts(scores, mask):
+    return key_row, key_col, jnp.where(inside, 1.0, 0.0)
+
+
+def block_masks(axis, first_row, blocks, col_index, grid_rows, grid_cols):
+    shapes = (256, 1), (1, 256)
+    key, token = iota(shapes[axis], axis), iota(shapes[1 - axis], 1 - axis) & 63
+    for block in range(blocks):
+        key_row, key_col, inside = key_places(
+            key, first_row + 8 * block, col_index, grid_rows, grid_cols
+        )
+        if block == 0:
+            row_gap = key_row - (token >> 3) - 4
+            col_gap = key_col - (token & 7)
+            near = (row_gap >= -3) & (row_gap <= 3) & (col_gap >= -3) & (col_gap <= 3)
+            near = jnp.where(near, 1.0, 0.0)
+        yield near * inside
+
+
+def column_softmax(scores, mask):
     weight = jnp.exp(scores) * mask
-    total = jnp.sum(weight, axis=-1, keepdims=True)
-    return weight, 1.0 / jnp.where(total > 0, total, 1.0)
-
-
-def pack_kernel(place_ref, patches_ref, slot_ref, own_ref, far_ref, slot_s, wide_s, sems):
+    total = jnp.sum(weight, axis=0, keepdims=True)
+    return weight * (1.0 / jnp.where(total > 0, total, 1.0))
+
+
+def pack_kernel(
+    place_ref, patches_ref, slot_ref, cot_ref,
+    own_ref, far_ref, go_c_ref, go_d_ref, slot_s, wide_s, sems,
+):
     half = place_ref[0] >> 2
-    copies = [pltpu.make_async_copy(slot_ref, slot_s, sems.at[0])]
-    for i, (target, side) in enumerate(((own_ref, half), (far_ref, 1 - half))):
-        copies.append(
-            pltpu.make_async_copy(
-                patches_ref.at[pl.ds(pl.multiple_of(48 * side, 16), 80), :],
-                target.at[pl.ds(pl.multiple_of(16 - 16 * side, 16), 80), pl.ds(0, PIX)],
-                sems.at[i + 1],
-            )
-        )
+    odd = place_ref[0] & 1
+    own_rows = pl.ds(pl.multiple_of(16 - 16 * half, 16), 80)
+    own_source = pl.ds(pl.multiple_of(48 * half, 16), 80)
+    far_source = pl.ds(pl.multiple_of(48 - 48 * half, 16), 80)
+    c_rows = pl.ds(pl.multiple_of(96 - 96 * odd, 16), 32)
+    d_rows = pl.ds(pl.multiple_of(96 * odd, 16), 32)
+    lanes = pl.ds(0, PIX)
+    pairs = (
+        (slot_ref, slot_s),
+        (patches_ref.at[far_source, :], far_ref.at[:, lanes]),
+        (patches_ref.at[own_source, :], own_ref.at[own_rows, lanes]),
+        (cot_ref.at[c_rows, :], go_c_ref),
+        (cot_ref.at[d_rows, :], go_d_ref),
+    )
+    copies = [pltpu.make_async_copy(*pair, sems.at[i]) for i, pair in enumerate(pairs)]
     for copy in copies:
         copy.start()
     for copy in copies:
         copy.wait()
     wide_s[...] = jnp.broadcast_to(slot_s[...].astype(F32), (128, 128)).T.astype(BF)
-    for target, side in ((own_ref, half), (far_ref, 1 - half)):
-        target[pl.ds(pl.multiple_of(80 * side, 16), 16), :] = jnp.zeros((16, PIX + 128), BF)
-        target[pl.ds(pl.multiple_of(16 - 16 * side, 16), 80), PIX:] = wide_s[
-            pl.ds(pl.multiple_of(48 * side, 16), 80), :
-        ]
+    gap = pl.ds(pl.multiple_of(80 * half, 16), 16)
+    own_ref[gap, :] = jnp.zeros((16, PIX + 128), BF)
+    own_ref[own_rows, PIX:] = wide_s[own_source, :]
+    far_ref[:, PIX:] = wide_s[far_source, :]
+
+
+def far_window(place_ref, far_ref, wide_ref):
+    half = place_ref[0] >> 2
+    wide_ref[pl.ds(pl.multiple_of(80 * half, 16), 16), :] = jnp.zeros((16, PIX + 128), BF)
+    wide_ref[pl.ds(pl.multiple_of(16 - 16 * half, 16), 80), :] = far_ref[...]
 
 
 def windows(place_ref, own_ref, far_ref, step):
@@ -115,17 +136,23 @@
     return own_ref[pl.ds(start, 48), :], far_ref[pl.ds(start, 48), :]
 
 
-def spread_kernel(place_ref, own_ref, far_ref, touched_ref, *out_refs):
-    for step, out_ref in zip((2, 3, 1), out_refs):
-        near, far = windows(place_ref, own_ref, far_ref, step)
+def spread_kernel(
+    place_ref, own_ref, far_ref, mask_a_ref, mask_b_ref, *refs
+):
+    far_s = refs[3]
+    far_window(place_ref, far_ref, far_s)
+    for step, out_ref in zip((2, 3, 1), refs):
+        near, far = windows(place_ref, own_ref, far_s, step)
         out_ref[0:48, :] = near
         out_ref[48:96, :] = far
 
 
 def place_kernel(
-    place_ref, own_in_ref, far_in_ref, in2_ref, in3_ref, in1_ref, own_ref, go_a_ref, go_b_ref
-):
-    near, far = windows(place_ref, own_in_ref, far_in_ref, 0)
+    place_ref, touched_ref, own_in_ref, far_in_ref, in2_ref, in3_ref, in1_ref,
+    own_ref, go_a_ref, go_b_ref, far_s,
+):
+    far_window(place_ref, far_in_ref, far_s)
+    near, far = windows(place_ref, own_in_ref, far_s, 0)
     source = jnp.concatenate([near, far, in2_ref[...], in3_ref[...], in1_ref[...]], axis=0)
     slots = []
     for part in range(3):
@@ -146,10 +173,16 @@
     go_b_ref[...] = pick(edge + 4 * (1 - even))
 
 
-def touch_kernel(we_ref, wq_ref, wkv_ref, wo_ref, out_ref):
-    total = we_ref[0:16, 0:128].astype(F32) + wq_ref[0:16, 0:128].astype(F32)
-    total = total + wkv_ref[0:16, 0:128].astype(F32) + wo_ref[0:16, 0:128].astype(F32)
-    out_ref[...] = total
+def mask_kernel(grid_rows, grid_cols, place_ref, wkv_ref, first_ref, second_ref):
+    row, col = place_ref[0] * 16, place_ref[1]
+    for i, mask in enumerate(block_masks(1, row - 12, 4, col, grid_rows, grid_cols)):
+        first_ref[i] = mask
+    for i, mask in enumerate(block_masks(0, row - 8, 3, col, grid_rows, grid_cols)):
+        second_ref[i] = mask
+
+
+def touch_kernel(we_ref, wq_ref, send_ref, out_ref):
+    out_ref[...] = we_ref[0:16, 0:128].astype(F32) + wq_ref[0:16, 0:128].astype(F32)
 
 
 def own_first_kernel(own_ref, we_ref, wq_ref, wkv_ref, x0_ref, q_ref, kv_ref, x_s, n_s):
@@ -192,10 +225,9 @@
 
 
 def first_core_kernel(
-    grid_rows, grid_cols,
-    place_ref, a_ref, b_ref, we_ref, wkv_ref, wo_ref, x0_ref, q_ref, kv_ref,
+    place_ref, mask_ref, a_ref, b_ref, we_ref, wkv_ref, wo_ref, x0_ref, q_ref, kv_ref,
     x1_ref, go_a_ref, go_b_ref,
-    p_s, x_s, n_s, rim_s, o_s, mask_s,
+    p_s, x_s, n_s, rim_s, o_s,
 ):
     means = group_mean_matrix()
     p_s[0:144, :] = a_ref[...]
@@ -214,9 +246,6 @@
         value = dot(n_s[...], wkv_ref[:, cols(g + GROUPS)])
         rim_s[:, cols(g + GROUPS)] = padded_rim(value).astype(BF)
 
-    first_row = place_ref[0] * 16 - 12
-    for block in range(4):
-        mask_s[block] = block_mask(first_row + 8 * block, place_ref[1], grid_rows, grid_cols)
     masks = head_masks()
 
     for g in range(GROUPS):
@@ -224,8 +253,9 @@
             query = stack_heads(q_ref[64 * block : 64 * block + 64, cols(g)], masks)
             key = keys_of(kv_ref, rim_s, block, g)
             value = keys_of(kv_ref, rim_s, block, g + GROUPS)
-            weight, inverse = softmax_parts(dot(query, key, NT), mask_s[block])
-            mixed = dot(weight.astype(BF), value) * inverse
+            weight = jnp.exp(dot(query, key, NT)) * mask_ref[block]
+            total = jnp.sum(weight, axis=1, keepdims=True)
+            mixed = dot(weight.astype(BF), value) * (1.0 / jnp.where(total > 0, total, 1.0))
             o_s[64 * block : 64 * block + 64, cols(g)] = unstack_heads(mixed).astype(BF)
 
     n = iota((112, 256), 0)
@@ -244,16 +274,17 @@
 
 
 def own_second_kernel(
-    x1_ref, cot_ref, above_ref, below_ref, wq_ref, wkv_ref, wo_ref,
+    place_ref, x1_ref, cot_ref, c_ref, d_ref, wq_ref, wkv_ref, wo_ref,
     q_ref, kv_ref, do_ref, rsq_ref, rsk_ref,
     n_s, c_s,
 ):
     means = group_mean_matrix()
     residual = x1_ref[...].astype(F32)
     n_s[...] = (residual * row_scale(residual)).astype(BF)
-    c_s[0:32, :] = above_ref[...]
+    odd = place_ref[0] & 1
+    c_s[pl.ds(pl.multiple_of(160 - 160 * odd, 16), 32), :] = c_ref[...]
     c_s[32:160, :] = cot_ref[...]
-    c_s[160:192, :] = below_ref[...]
+    c_s[pl.ds(pl.multiple_of(160 * odd, 16), 32), :] = d_ref[...]
 
     for g in range(GROUPS):
         query = dot(n_s[32:224, :], wq_ref[:, cols(g)])
@@ -273,10 +304,9 @@
 
 
 def second_core_kernel(
-    grid_rows, grid_cols,
-    place_ref, a_ref, b_ref, wkv_ref, q_ref, kv_ref, do_ref,
+    mask_ref, a_ref, b_ref, wkv_ref, q_ref, kv_ref, do_ref,
     o_ref, dq_ref, dkv_ref, go_a_ref, go_b_ref,
-    n_s, rim_s, rs_s, db_s, mask_s,
+    n_s, rim_s, rs_s, db_s,
 ):
     means = group_mean_matrix()
     residual = jnp.concatenate([a_ref[...].astype(F32), b_ref[...].astype(F32)], axis=0)
@@ -291,9 +321,6 @@
         rs_s[64:128, cols(g)] = scale[160:224]
         rim_s[:, cols(g + GROUPS)] = dot(n_s[...], wkv_ref[:, cols(g + GROUPS)]).astype(BF)
 
-    first_row = place_ref[0] * 16 - 8
-    for block in range(3):
-        mask_s[block] = block_mask(first_row + 8 * block, place_ref[1], grid_rows, grid_cols)
     masks = head_masks()
 
     for g in range(GROUPS):
@@ -302,21 +329,20 @@
             query = stack_heads(q_ref[64 * block : 64 * block + 64, cols(g)], masks)
             key = keys_of(kv_ref, rim_s, block, g)
             value = keys_of(kv_ref, rim_s, block, g + GROUPS)
-            weight, inverse = softmax_parts(dot(query, key, NT), mask_s[block])
-            probs = weight * inverse
+            out_back = stack_heads(do_ref[64 * block : 64 * block + 64, cols(g)], masks)
+            probs = column_softmax(dot(key, query, NT), mask_ref[block])
             probs_low = probs.astype(BF)
-            out_back = stack_heads(do_ref[64 * block : 64 * block + 64, cols(g)], masks)
-            probs_back = dot(out_back, value, NT)
-            centre = jnp.sum(probs_back * probs, axis=-1, keepdims=True)
+            probs_back = dot(value, out_back, NT)
+            centre = jnp.sum(probs_back * probs, axis=0, keepdims=True)
             scores_back = (probs * (probs_back - centre)).astype(BF)
             o_ref[64 * block : 64 * block + 64, cols(g)] = unstack_heads(
-                dot(probs_low, value)
+                dot(probs_low, value, TN)
             ).astype(BF)
             dq_ref[64 * block : 64 * block + 64, cols(g)] = unstack_heads(
-                dot(scores_back, key)
+                dot(scores_back, key, TN)
             ).astype(BF)
-            key_backs.append(dot(scores_back, query, TN))
-            value_backs.append(dot(probs_low, out_back, TN))
+            key_backs.append(dot(scores_back, query))
+            value_backs.append(dot(probs_low, out_back))
 
         def fold(parts):
             def piece(start, half):
@@ -386,6 +412,8 @@
 def call(kernel, out_shapes, *operands, scratch=(), flops=0, moved=0, small=None, hbm=False):
     vmem = pl.BlockSpec(memory_space=pltpu.VMEM)
     in_specs = [pl.BlockSpec(memory_space=pltpu.HBM) if hbm else vmem] * len(operands)
+    if hbm:
+        operands = tuple(pltpu.with_memory_space_constraint(x, pltpu.HBM) for x in operands)
     if small is not None:
         operands = (small,) + operands
         in_specs = [pl.BlockSpec(memory_space=pltpu.SMEM)] + in_specs
@@ -401,22 +429,15 @@
     )(*operands)
 
 
-def shift(values, axis, step):
-    peers = lax.axis_size(axis)
-    return lax.ppermute(
-        values, axis, [(i, i + step) for i in range(peers) if 0 <= i + step < peers]
-    )
-
-
 def trade(values, axis, step):
     return lax.ppermute(values, axis, [(i, i ^ step) for i in range(lax.axis_size(axis))])
 
 
-def trade_sides(go_a, go_b):
-    peers = lax.axis_size("col")
+def trade_sides(go_a, go_b, axis):
+    peers = lax.axis_size(axis)
     across = [(i, ((i + 1) ^ 1) - 1) for i in range(peers)]
-    b = lax.ppermute(go_b, "col", [(i, j) for i, j in across if 0 <= j < peers])
-    return trade(go_a, "col", 1), b
+    b = lax.ppermute(go_b, axis, [(i, j) for i, j in across if 0 <= j < peers])
+    return trade(go_a, axis, 1), b
 
 
 def on_device(patches, tile_slot, w_embed, w_query, w_keyval, w_out, cotangent):
@@ -426,30 +447,37 @@
     cot = cotangent.reshape(128, D)
     window = ((96, PIX + 128), BF)
 
-    own, far = call(
-        pack_kernel, (window, window), patches, tile_slot.reshape(1, 128),
+    own, far, edge_c, edge_d = call(
+        pack_kernel,
+        (window, ((80, PIX + 128), BF), ((32, D), BF), ((32, D), BF)),
+        patches, tile_slot.reshape(1, 128), cot,
         small=place, hbm=True,
         scratch=(
-            ((1, 128), jnp.int32), ((128, 128), BF), (pltpu.SemaphoreType.DMA((3,)), None)
+            ((1, 128), jnp.int32), ((128, 128), BF), (pltpu.SemaphoreType.DMA((5,)), None)
         ),
     )
     far = trade(far, "row", 4)
-    (touched,) = call(
-        touch_kernel, (((16, 128), F32),), w_embed, w_query, w_keyval, w_out
-    )
-    sends = call(spread_kernel, (window, window, window), own, far, touched, small=place)
+    masks = call(
+        functools.partial(mask_kernel, grid_rows, grid_cols),
+        (((4, 256, 256), F32), ((3, 256, 256), F32)),
+        w_keyval,
+        small=place,
+    )
+    sends = call(
+        spread_kernel, (window, window, window), own, far, *masks,
+        small=place, scratch=(window,),
+    )
+    (touched,) = call(touch_kernel, (((16, 128), F32),), w_embed, w_query, sends[0])
     arrived = [trade(send, "row", step) for send, step in zip(sends, (2, 3, 1))]
-
-    above = shift(cot[96:], "row", 1)
-    below = shift(cot[:32], "row", -1)
-
+    edge_c, edge_d = trade_sides(edge_c, edge_d, "row")
     own, go_a, go_b = call(
         place_kernel,
         (((320, PIX), BF), ((144, PIX), BF), ((144, PIX), BF)),
-        own, far, *arrived,
+        touched, own, far, *arrived,
         small=place,
-    )
-    a, b = trade_sides(go_a, go_b)
+        scratch=(window,),
+    )
+    a, b = trade_sides(go_a, go_b, "col")
     x0, queries, keyval = call(
         own_first_kernel,
         (((256, D), BF), ((256, D), BF), ((320, 2 * D), BF)),
@@ -458,36 +486,34 @@
         flops=8 * 10**9, moved=8 * 10**6,
     )
     x1, go_a, go_b = call(
-        functools.partial(first_core_kernel, grid_rows, grid_cols),
+        first_core_kernel,
         (((256, D), BF), ((112, D), BF), ((112, D), BF)),
-        a, b, w_embed, w_keyval, w_out, x0, queries, keyval,
+        masks[0], a, b, w_embed, w_keyval, w_out, x0, queries, keyval,
         small=place,
         scratch=(
             ((288, PIX), BF), ((288, D), F32), ((288, D), BF), ((320, 2 * D), BF), ((256, D), BF),
-            ((4, 256, 256), F32),
         ),
         flops=8 * 10**9, moved=8 * 10**6,
     )
-    a, b = trade_sides(go_a, go_b)
+    a, b = trade_sides(go_a, go_b, "col")
     queries, keyval, out_back, query_scale, key_scale = call(
         own_second_kernel,
         (((192, D), BF), ((256, 2 * D), BF), ((192, D), BF), ((128, D), F32), ((128, D), F32)),
-        x1, cot, above, below, w_query, w_keyval, w_out,
+        x1, cot, edge_c, edge_d, w_query, w_keyval, w_out,
+        small=place,
         scratch=(((256, D), BF), ((192, D), BF)),
         flops=8 * 10**9, moved=8 * 10**6,
     )
     attended, dq, dkv, go_a, go_b = call(
-        functools.partial(second_core_kernel, grid_rows, grid_cols),
+        second_core_kernel,
         (((192, D), BF), ((192, D), BF), ((128, 2 * D), BF), ((64, D), BF), ((64, D), BF)),
-        a, b, w_keyval, queries, keyval, out_back,
-        small=place,
+        masks[1], a, b, w_keyval, queries, keyval, out_back,
         scratch=(
             ((256, D), BF), ((256, 2 * D), BF), ((128, D), F32), ((128, 2 * D), BF),
-            ((3, 256, 256), F32),
         ),
         flops=8 * 10**9, moved=8 * 10**6,
     )
-    a, b = trade_sides(go_a, go_b)
+    a, b = trade_sides(go_a, go_b, "col")
     final_tokens, back = call(
         own_back_kernel,
         (((128, D), BF), ((128, D), F32)),

time: 84.7 us -> 78.2 us (0.923)
  local copies, waits for them, and re-layouts: 8.39 us -> 2.21 us
  starting transfers between devices: 35 us -> 32.6 us
  waiting for transfers between devices: 8.14 us -> 9.42 us
  Pallas kernels: 31.8 us -> 32.8 us
    unnamed x22 -> x12, local copies, waits for them, and re-layouts: 8.38 us -> 2.21 us
    ppermute x5 -> x4, starting transfers between devices: 23.7 us -> 20.3 us  [trade_sides(): b = lax.ppermute(go_b, axis, [(i, j) for i, j in across if 0 <= j < peers])]
    ppermute x7 -> x8, starting transfers between devices: 11.3 us -> 12.3 us  [trade(): lax.ppermute(values, axis, [(i, i ^ step) for i in range(lax.axis_size(ax...]
    pallas_call x10 -> x11, Pallas kernels: 31.8 us -> 32.8 us  [call(): pl.pallas_call(kernel, out_shape=shapes, in_specs=in_specs, out_specs=tup...]
    ppermute x5 -> x4, waiting for transfers between devices: 8.12 us -> 8.72 us  [trade_sides(): b = lax.ppermute(go_b, axis, [(i, j) for i, j in across if 0 <= j < peers])]
  transfers between devices with their start and end apart: 12 -> 12, of which waited for: 3 -> 4; matrix products, arithmetic and copies ran while one was open for 0% -> 0% of each run, Pallas kernels for 23% -> 27%
where the time goes in v3:
time: 78.2 us; the launch traced here: 78 us
  Pallas kernels  32.8 us (42%)
  starting transfers between devices  32.6 us (42%)
  waiting for transfers between devices  9.42 us (12%)
  local copies, waits for them, and re-layouts  2.21 us (3%)
  between operations  0.87 us (1%)
    pallas_call x11, Pallas kernels, call(): pl.pallas_call(kernel, out_shape=shapes, in_specs=in_specs, out_specs=tup...  32.8 us
    ppermute x4, starting transfers between devices, trade_sides(): b = lax.ppermute(go_b, axis, [(i, j) for i, j in across if 0 <= j < peers])  20.3 us
    ppermute x8, starting transfers between devices, trade(): lax.ppermute(values, axis, [(i, i ^ step) for i in range(lax.axis_size(ax...  12.3 us
    ppermute x4, waiting for transfers between devices, trade_sides(): b = lax.ppermute(go_b, axis, [(i, j) for i, j in across if 0 <= j < peers])  8.72 us
    unnamed x12, local copies, waits for them, and re-layouts  2.21 us
  transfers between devices with their start and end apart: 12, of which 4 were waited for; matrix products, arithmetic and copies ran while one was open for 0% of the time, Pallas kernels for 27%

profile of v3, /device:TPU:30, one launch (start us, length us, event | category | flops | bytes accessed | tf_op | source)
XLA Modules:
  0.0 78.0 jit_solution(14135500931636593899)
XLA Ops:
  0.6 0.1 pad_add_fusion.place_ref
  0.7 1.7 %shard_map.87 = (bf16[96,896]{1,0:T(8,128)(2,1)S(1)}, bf16[80,896]{1,0:T(8,128)(2,1)S(1)}, bf16[32,1024]{1,0:T(8,128)(2,1)S(1)}, bf16[32,1024]{1,0:T(8,128)(2,1)S(1)}) custom-call(s32[2]{0:T(128)S(1)} %pad_add_fusion.place_ref, bf16[128,768]{1,0:T(8,128)(2,1)} %patches_ref.1, s32[1,128]{1,0:T(1,128)} %bitcast.10, bf16[128,1024]{1,0:T(8,128)(2,1)} %bitcast.6), custom_call_target="tpu_custom_call" | custom-call | tf_op jit(solution)/shard_map/pallas_call | solution.py:421
  2.4 7.3 %collective-permute-start = (bf16[80,896]{1,0:T(8,128)(2,1)S(1)}, bf16[80,896]{1,0:T(8,128)(2,1)S(1)}, u32[]{:S(2)}, u32[]{:S(2)}) collective-permute-start(bf16[80,896]{1,0:T(8,128)(2,1)S(1)} %get-tuple-element.34), channel_id=1, source_target_pairs={{0,128},{32,160},{64,192},{96,224},{128,0},{160,32},{192,64},{224,... | collective-permute-start | bytes 430088 | tf_op jit(solution)/shard_map/ppermute | solution.py:433
  9.7 0.0 copy-start
  9.7 2.2 %copy-done = bf16[1024,2048]{1,0:T(8,128)(2,1)S(1)} copy-done((bf16[1024,2048]{1,0:T(8,128)(2,1)S(1)}, bf16[1024,2048]{1,0:T(8,128)(2,1)}, u32[]{:S(2)}) %copy-start) | copy-done | bytes 4194328
  11.9 0.0 copy-start.3
  11.9 1.0 %shard_map.86 = (f32[4,256,256]{2,1,0:T(8,128)S(1)}, f32[3,256,256]{2,1,0:T(8,128)S(1)}) custom-call(s32[2]{0:T(128)S(1)} %pad_add_fusion.place_ref, bf16[1024,2048]{1,0:T(8,128)(2,1)S(1)} %copy-done), custom_call_target="tpu_custom_call" | custom-call | tf_op jit(solution)/shard_map/pallas_call | solution.py:421
  12.9 0.0 copy-start.2
  12.9 0.7 collective-permute-done.far_ref.far_in_ref
  13.6 0.6 shard_map.88
  14.2 0.3 collective-permute-start.2
  14.5 1.0 %collective-permute-start.3 = (bf16[96,896]{1,0:T(8,128)(2,1)S(1)}, bf16[96,896]{1,0:T(8,128)(2,1)S(1)}, u32[]{:S(2)}, u32[]{:S(2)}) collective-permute-start(bf16[96,896]{1,0:T(8,128)(2,1)S(1)} %get-tuple-element.38), channel_id=1, source_target_pairs={{0,32},{32,0},{64,96},{96,64},{128,160},{160,128},{192,224},{224,1... | collective-permute-start | bytes 516104 | tf_op jit(solution)/shard_map/ppermute | solution.py:433
  15.4 3.5 %collective-permute-start.1 = (bf16[96,896]{1,0:T(8,128)(2,1)S(1)}, bf16[96,896]{1,0:T(8,128)(2,1)S(1)}, u32[]{:S(2)}, u32[]{:S(2)}) collective-permute-start(bf16[96,896]{1,0:T(8,128)(2,1)S(1)} %get-tuple-element.36.send_ref), channel_id=1, source_target_pairs={{0,64},{32,96},{64,0},{96,32},{128,192},{160,224},{192,128},{224,1... | collective-permute-start | bytes 516104 | tf_op jit(solution)/shard_map/ppermute | solution.py:433
  18.9 0.0 collective-permute-start.8
  18.9 0.0 copy-start.1
  19.0 10.1 %collective-permute-start.9 = (bf16[32,1024]{1,0:T(8,128)(2,1)S(1)}, bf16[32,1024]{1,0:T(8,128)(2,1)S(1)}, u32[]{:S(2)}, u32[]{:S(2)}) collective-permute-start(bf16[32,1024]{1,0:T(8,128)(2,1)S(1)} %get-tuple-element.49), channel_id=1, source_target_pairs={{32,64},{64,32},{96,128},{128,96},{160,192},{192,160},{33,65},{65,... | collective-permute-start | bytes 196616 | tf_op jit(solution)/shard_map/ppermute | solution.py:439
  29.1 0.0 copy-done.3
  29.1 0.0 copy-done.2
  29.1 0.0 collective-permute-done.2.in3_ref
  29.1 0.0 collective-permute-done.3.in1_ref
  29.1 0.0 collective-permute-done.1.in2_ref
  29.1 1.2 %shard_map.90 = (bf16[320,768]{1,0:T(8,128)(2,1)S(1)}, bf16[144,768]{1,0:T(8,128)(2,1)S(1)}, bf16[144,768]{1,0:T(8,128)(2,1)S(1)}) custom-call(s32[2]{0:T(128)S(1)} %pad_add_fusion.place_ref, f32[16,128]{1,0:T(8,128)S(1)} %shard_map.89.touched_ref, bf16[96,896]{1,0:T(8,128)(2,1)S(1)} %get-tuple-element.33.own_ref.own_in_ref, ...), custom_call_target="tpu_custom_call" | custom-call | tf_op jit(solution)/shard_map/pallas_call | solution.py:421
  30.4 0.1 collective-permute-start.4
  30.5 3.1 %collective-permute-start.5 = (bf16[144,768]{1,0:T(8,128)(2,1)S(1)}, bf16[144,768]{1,0:T(8,128)(2,1)S(1)}, u32[]{:S(2)}, u32[]{:S(2)}) collective-permute-start(bf16[144,768]{1,0:T(8,128)(2,1)S(1)} %get-tuple-element.40), channel_id=1, source_target_pairs={{1,2},{2,1},{3,4},{4,3},{5,6},{6,5},{7,8},{8,7},{9,10},{10,9},{11,... | collective-permute-start | bytes 663560 | tf_op jit(solution)/shard_map/ppermute | solution.py:439
  33.6 0.0 copy-done.1
  33.6 0.0 copy-start.5
  33.6 4.3 %shard_map.91 = (bf16[256,1024]{1,0:T(8,128)(2,1)S(1)}, bf16[256,1024]{1,0:T(8,128)(2,1)S(1)}, bf16[320,2048]{1,0:T(8,128)(2,1)S(1)}) custom-call(bf16[320,768]{1,0:T(8,128)(2,1)S(1)} %get-tuple-element.41.own_ref, bf16[768,1024]{1,0:T(8,128)(2,1)S(1)} %copy-done.3, bf16[1024,1024]{1,0:T(8,128)(2,1)S(1)} %copy-done.2, bf16[1024,2048]{1,0:T(8,128)(2,1)S(1)} %copy-done.1), custom_call_target="tpu_custom_call" | custom-call | flops 8000000000 | bytes 8000000 | tf_op jit(solution)/shard_map/pallas_call | solution.py:421
  37.9 0.0 collective-permute-done.4.a_ref
  37.9 4.8 %collective-permute-done.5.b_ref = bf16[144,768]{1,0:T(8,128)(2,1)S(1)} collective-permute-done((bf16[144,768]{1,0:T(8,128)(2,1)S(1)}, bf16[144,768]{1,0:T(8,128)(2,1)S(1)}, u32[]{:S(2)}, u32[]{:S(2)}) %collective-permute-start.5) | collective-permute-done | bytes 221216 | tf_op jit(solution)/shard_map/ppermute | solution.py:439
  42.7 0.0 copy-done.5
  42.7 0.0 copy-start.4
  42.7 6.4 %shard_map.92 = (bf16[256,1024]{1,0:T(8,128)(2,1)S(1)}, bf16[112,1024]{1,0:T(8,128)(2,1)S(1)}, bf16[112,1024]{1,0:T(8,128)(2,1)S(1)}) custom-call(s32[2]{0:T(128)S(1)} %pad_add_fusion.place_ref, f32[4,256,256]{2,1,0:T(8,128)S(1)} %get-tuple-element.32.mask_a_ref.mask_ref, bf16[144,768]{1,0:T(8,128)(2,1)S(1)} %collective-permute-done.4.a_ref, ...), custom_call_target="tpu_custom_call" | custom-call | flops 8000000000 | bytes 8000000 | tf_op jit(solution)/shard_map/pallas_call | solution.py:421
  49.2 0.1 collective-permute-start.6
  49.3 3.0 %collective-permute-start.7 = (bf16[112,1024]{1,0:T(8,128)(2,1)S(1)}, bf16[112,1024]{1,0:T(8,128)(2,1)S(1)}, u32[]{:S(2)}, u32[]{:S(2)}) collective-permute-start(bf16[112,1024]{1,0:T(8,128)(2,1)S(1)} %get-tuple-element.47), channel_id=1, source_target_pairs={{1,2},{2,1},{3,4},{4,3},{5,6},{6,5},{7,8},{8,7},{9,10},{10,9},{11,... | collective-permute-start | bytes 688136 | tf_op jit(solution)/shard_map/ppermute | solution.py:439
  52.3 0.0 collective-permute-done.8.c_ref
  52.3 0.0 collective-permute-done.9.d_ref
  52.3 0.0 copy-done.4
  52.3 4.7 %shard_map.93 = (bf16[192,1024]{1,0:T(8,128)(2,1)S(1)}, bf16[256,2048]{1,0:T(8,128)(2,1)S(1)}, bf16[192,1024]{1,0:T(8,128)(2,1)S(1)}, f32[128,1024]{1,0:T(8,128)S(1)}, f32[128,1024]{1,0:T(8,128)S(1)}) custom-call(s32[2]{0:T(128)S(1)} %pad_add_fusion.place_ref, bf16[256,1024]{1,0:T(8,128)(2,1)S(1)} %get-tuple-element.45.x1_ref, ...), custom_call_target="tpu_custom_call" | custom-call | flops 8000000000 | bytes 8000000 | tf_op jit(solution)/shard_map/pallas_call | solution.py:421
  57.0 0.0 collective-permute-done.6.a_ref
  57.0 2.4 %collective-permute-done.7.b_ref = bf16[112,1024]{1,0:T(8,128)(2,1)S(1)} collective-permute-done((bf16[112,1024]{1,0:T(8,128)(2,1)S(1)}, bf16[112,1024]{1,0:T(8,128)(2,1)S(1)}, u32[]{:S(2)}, u32[]{:S(2)}) %collective-permute-start.7) | collective-permute-done | bytes 229408 | tf_op jit(solution)/shard_map/ppermute | solution.py:439
  59.4 7.9 %shard_map.94 = (bf16[192,1024]{1,0:T(8,128)(2,1)S(1)}, bf16[192,1024]{1,0:T(8,128)(2,1)S(1)}, bf16[128,2048]{1,0:T(8,128)(2,1)S(1)}, bf16[64,1024]{1,0:T(8,128)(2,1)S(1)}, bf16[64,1024]{1,0:T(8,128)(2,1)S(1)}) custom-call(f32[3,256,256]{2,1,0:T(8,128)S(1)} %get-tuple-element.35.mask_b_ref.mask_ref, bf16[112,1024]{1,0:T(8,128)(2,1)S(1)} %collective-permute-done.6.a_ref, ...), custom_call_target="tpu_custom_call" | custom-call | flops 8000000000 | bytes 8000000 | tf_op jit(solution)/shard_map/pallas_call | solution.py:421
  67.3 0.1 collective-permute-start.10
  67.4 4.1 %collective-permute-start.11 = (bf16[64,1024]{1,0:T(8,128)(2,1)S(1)}, bf16[64,1024]{1,0:T(8,128)(2,1)S(1)}, u32[]{:S(2)}, u32[]{:S(2)}) collective-permute-start(bf16[64,1024]{1,0:T(8,128)(2,1)S(1)} %get-tuple-element.61), channel_id=1, source_target_pairs={{1,2},{2,1},{3,4},{4,3},{5,6},{6,5},{7,8},{8,7},{9,10},{10,9},{11,... | collective-permute-start | bytes 393224 | tf_op jit(solution)/shard_map/ppermute | solution.py:439
  71.5 3.3 %shard_map.95 = (bf16[128,1024]{1,0:T(8,128)(2,1)}, f32[128,1024]{1,0:T(8,128)S(1)}) custom-call(bf16[256,1024]{1,0:T(8,128)(2,1)S(1)} %get-tuple-element.45.x1_ref, bf16[192,1024]{1,0:T(8,128)(2,1)S(1)} %get-tuple-element.53.o_ref, bf16[192,1024]{1,0:T(8,128)(2,1)S(1)} %get-tuple-element.54.dq_ref, bf16[128,2048]{1,0:T(8,128)(2,1)S(1)} %get-tuple-element.55.dkv_ref, ...), custom_call_target="tpu_custom_call" | custom-call | flops 8000000000 | bytes 8000000 | tf_op jit(solution)/shard_map/pallas_call | solution.py:421
  74.8 0.0 collective-permute-done.10.a_ref
  74.8 1.6 %collective-permute-done.11.b_ref = bf16[64,1024]{1,0:T(8,128)(2,1)S(1)} collective-permute-done((bf16[64,1024]{1,0:T(8,128)(2,1)S(1)}, bf16[64,1024]{1,0:T(8,128)(2,1)S(1)}, u32[]{:S(2)}, u32[]{:S(2)}) %collective-permute-start.11) | collective-permute-done | bytes 131104 | tf_op jit(solution)/shard_map/ppermute | solution.py:439
  76.4 1.6 %shard_map.96 = bf16[128,1024]{1,0:T(8,128)(2,1)} custom-call(s32[2]{0:T(128)S(1)} %pad_add_fusion.place_ref, bf16[256,1024]{1,0:T(8,128)(2,1)S(1)} %get-tuple-element.45.x1_ref, bf16[128,1024]{1,0:T(8,128)(2,1)S(1)} %bitcast.8, f32[128,1024]{1,0:T(8,128)S(1)} %get-tuple-element.59.dn_ref, bf16[64,1024]{1,0:T(8,128)(2,1)S(1)} %collective-permute-done.10.a_ref, ...), custom_call_target="tpu_custom_call" | custom-call | tf_op jit(solution)/shard_map/pallas_call | solution.py:421
  (1 shorter events, 0.0 us)
Async XLA Ops:
  2.4 11.1 %collective-permute-start = (bf16[80,896]{1,0:T(8,128)(2,1)S(1)}, bf16[80,896]{1,0:T(8,128)(2,1)S(1)}, u32[]{:S(2)}, u32[]{:S(2)}) collective-permute-start(bf16[80,896]{1,0:T(8,128)(2,1)S(1)} %get-tuple-element.34), channel_id=1, source_target_pairs={{0,128},{32,160},{64,192},{96,224},{128,0},{160,32},{192,64},{224,... | collective-permute-start | bytes 430088 | tf_op jit(solution)/shard_map/ppermute | solution.py:433
  9.7 2.2 %copy-start = (bf16[1024,2048]{1,0:T(8,128)(2,1)S(1)}, bf16[1024,2048]{1,0:T(8,128)(2,1)}, u32[]{:S(2)}) copy-start(bf16[1024,2048]{1,0:T(8,128)(2,1)} %wkv_ref.11) | copy-start | bytes 12582916
  11.9 17.2 %copy-start.3 = (bf16[768,1024]{1,0:T(8,128)(2,1)S(1)}, bf16[768,1024]{1,0:T(8,128)(2,1)}, u32[]{:S(2)}) copy-start(bf16[768,1024]{1,0:T(8,128)(2,1)} %we_ref.5) | copy-start | bytes 4718596
  12.9 16.2 %copy-start.2 = (bf16[1024,1024]{1,0:T(8,128)(2,1)S(1)}, bf16[1024,1024]{1,0:T(8,128)(2,1)}, u32[]{:S(2)}) copy-start(bf16[1024,1024]{1,0:T(8,128)(2,1)} %wq_ref.7) | copy-start | bytes 6291460
  14.2 14.9 %collective-permute-start.2 = (bf16[96,896]{1,0:T(8,128)(2,1)S(1)}, bf16[96,896]{1,0:T(8,128)(2,1)S(1)}, u32[]{:S(2)}, u32[]{:S(2)}) collective-permute-start(bf16[96,896]{1,0:T(8,128)(2,1)S(1)} %get-tuple-element.37), channel_id=1, source_target_pairs={{0,96},{32,64},{64,32},{96,0},{128,224},{160,192},{192,160},{224,1... | collective-permute-start | bytes 516104 | tf_op jit(solution)/shard_map/ppermute | solution.py:433
  14.5 14.6 %collective-permute-start.3 = (bf16[96,896]{1,0:T(8,128)(2,1)S(1)}, bf16[96,896]{1,0:T(8,128)(2,1)S(1)}, u32[]{:S(2)}, u32[]{:S(2)}) collective-permute-start(bf16[96,896]{1,0:T(8,128)(2,1)S(1)} %get-tuple-element.38), channel_id=1, source_target_pairs={{0,32},{32,0},{64,96},{96,64},{128,160},{160,128},{192,224},{224,1... | collective-permute-start | bytes 516104 | tf_op jit(solution)/shard_map/ppermute | solution.py:433
  15.4 13.7 %collective-permute-start.1 = (bf16[96,896]{1,0:T(8,128)(2,1)S(1)}, bf16[96,896]{1,0:T(8,128)(2,1)S(1)}, u32[]{:S(2)}, u32[]{:S(2)}) collective-permute-start(bf16[96,896]{1,0:T(8,128)(2,1)S(1)} %get-tuple-element.36.send_ref), channel_id=1, source_target_pairs={{0,64},{32,96},{64,0},{96,32},{128,192},{160,224},{192,128},{224,1... | collective-permute-start | bytes 516104 | tf_op jit(solution)/shard_map/ppermute | solution.py:433
  18.9 33.4 %collective-permute-start.8 = (bf16[32,1024]{1,0:T(8,128)(2,1)S(1)}, bf16[32,1024]{1,0:T(8,128)(2,1)S(1)}, u32[]{:S(2)}, u32[]{:S(2)}) collective-permute-start(bf16[32,1024]{1,0:T(8,128)(2,1)S(1)} %get-tuple-element.48), channel_id=1, source_target_pairs={{0,32},{32,0},{64,96},{96,64},{128,160},{160,128},{192,224},{224,1... | collective-permute-start | bytes 196616 | tf_op jit(solution)/shard_map/ppermute | solution.py:433
  18.9 14.6 %copy-start.1 = (bf16[1024,2048]{1,0:T(8,128)(2,1)S(1)}, bf16[1024,2048]{1,0:T(8,128)(2,1)}, u32[]{:S(2)}) copy-start(bf16[1024,2048]{1,0:T(8,128)(2,1)} %wkv_ref.11) | copy-start | bytes 12582916
  19.0 33.4 %collective-permute-start.9 = (bf16[32,1024]{1,0:T(8,128)(2,1)S(1)}, bf16[32,1024]{1,0:T(8,128)(2,1)S(1)}, u32[]{:S(2)}, u32[]{:S(2)}) collective-permute-start(bf16[32,1024]{1,0:T(8,128)(2,1)S(1)} %get-tuple-element.49), channel_id=1, source_target_pairs={{32,64},{64,32},{96,128},{128,96},{160,192},{192,160},{33,65},{65,... | collective-permute-start | bytes 196616 | tf_op jit(solution)/shard_map/ppermute | solution.py:439
  30.4 7.5 %collective-permute-start.4 = (bf16[144,768]{1,0:T(8,128)(2,1)S(1)}, bf16[144,768]{1,0:T(8,128)(2,1)S(1)}, u32[]{:S(2)}, u32[]{:S(2)}) collective-permute-start(bf16[144,768]{1,0:T(8,128)(2,1)S(1)} %get-tuple-element.39), channel_id=1, source_target_pairs={{0,1},{1,0},{2,3},{3,2},{4,5},{5,4},{6,7},{7,6},{8,9},{9,8},{10,11... | collective-permute-start | bytes 663560 | tf_op jit(solution)/shard_map/ppermute | solution.py:433
  30.5 12.2 %collective-permute-start.5 = (bf16[144,768]{1,0:T(8,128)(2,1)S(1)}, bf16[144,768]{1,0:T(8,128)(2,1)S(1)}, u32[]{:S(2)}, u32[]{:S(2)}) collective-permute-start(bf16[144,768]{1,0:T(8,128)(2,1)S(1)} %get-tuple-element.40), channel_id=1, source_target_pairs={{1,2},{2,1},{3,4},{4,3},{5,6},{6,5},{7,8},{8,7},{9,10},{10,9},{11,... | collective-permute-start | bytes 663560 | tf_op jit(solution)/shard_map/ppermute | solution.py:439
  33.6 9.1 %copy-start.5 = (bf16[1024,1024]{1,0:T(8,128)(2,1)S(1)}, bf16[1024,1024]{1,0:T(8,128)(2,1)}, u32[]{:S(2)}) copy-start(bf16[1024,1024]{1,0:T(8,128)(2,1)} %wo_ref.5) | copy-start | bytes 6291460
  42.7 9.6 %copy-start.4 = (bf16[16,8,1024]{2,1,0:T(8,128)(2,1)S(1)}, bf16[16,8,1024]{2,1,0:T(8,128)(2,1)}, u32[]{:S(2)}) copy-start(bf16[16,8,1024]{2,1,0:T(8,128)(2,1)} %param.13) | copy-start | bytes 786436
  49.2 7.9 %collective-permute-start.6 = (bf16[112,1024]{1,0:T(8,128)(2,1)S(1)}, bf16[112,1024]{1,0:T(8,128)(2,1)S(1)}, u32[]{:S(2)}, u32[]{:S(2)}) collective-permute-start(bf16[112,1024]{1,0:T(8,128)(2,1)S(1)} %get-tuple-element.46), channel_id=1, source_target_pairs={{0,1},{1,0},{2,3},{3,2},{4,5},{5,4},{6,7},{7,6},{8,9},{9,8},{10,11... | collective-permute-start | bytes 688136 | tf_op jit(solution)/shard_map/ppermute | solution.py:433
  49.3 10.1 %collective-permute-start.7 = (bf16[112,1024]{1,0:T(8,128)(2,1)S(1)}, bf16[112,1024]{1,0:T(8,128)(2,1)S(1)}, u32[]{:S(2)}, u32[]{:S(2)}) collective-permute-start(bf16[112,1024]{1,0:T(8,128)(2,1)S(1)} %get-tuple-element.47), channel_id=1, source_target_pairs={{1,2},{2,1},{3,4},{4,3},{5,6},{6,5},{7,8},{8,7},{9,10},{10,9},{11,... | collective-permute-start | bytes 688136 | tf_op jit(solution)/shard_map/ppermute | solution.py:439
  67.3 7.5 %collective-permute-start.10 = (bf16[64,1024]{1,0:T(8,128)(2,1)S(1)}, bf16[64,1024]{1,0:T(8,128)(2,1)S(1)}, u32[]{:S(2)}, u32[]{:S(2)}) collective-permute-start(bf16[64,1024]{1,0:T(8,128)(2,1)S(1)} %get-tuple-element.60), channel_id=1, source_target_pairs={{0,1},{1,0},{2,3},{3,2},{4,5},{5,4},{6,7},{7,6},{8,9},{9,8},{10,11... | collective-permute-start | bytes 393224 | tf_op jit(solution)/shard_map/ppermute | solution.py:433
  67.4 9.0 %collective-permute-start.11 = (bf16[64,1024]{1,0:T(8,128)(2,1)S(1)}, bf16[64,1024]{1,0:T(8,128)(2,1)S(1)}, u32[]{:S(2)}, u32[]{:S(2)}) collective-permute-start(bf16[64,1024]{1,0:T(8,128)(2,1)S(1)} %get-tuple-element.61), channel_id=1, source_target_pairs={{1,2},{2,1},{3,4},{4,3},{5,6},{6,5},{7,8},{8,7},{9,10},{10,9},{11,... | collective-permute-start | bytes 393224 | tf_op jit(solution)/shard_map/ppermute | solution.py:439

commit v4 on v3

--- a/solution.py
+++ b/solution.py
@@ -86,6 +86,22 @@
             near = (row_gap >= -3) & (row_gap <= 3) & (col_gap >= -3) & (col_gap <= 3)
             near = jnp.where(near, 1.0, 0.0)
         yield near * inside
+
+
+def third(n):
+    return (n * 171) >> 9
+
+
+def edge_token(n, right):
+    row = third(n)
+    return row * 8 + (n - 3 * row) + 5 * right
+
+
+def widen(shape, skipped, right):
+    m, n = iota(shape, 0), iota(shape, 1)
+    slot = (m & 3) - (1 - right)
+    match = (((m >> 2) - skipped) * 3 + slot == n) & (slot >= 0) & (slot <= 2)
+    return jnp.where(match, 1.0, 0.0).astype(BF)
 
 
 def column_softmax(scores, mask):
@@ -167,10 +183,9 @@
         return dot(hot, source).astype(BF)
 
     own_ref[...] = pick(iota((320, 384), 0) + 32)
-    n = iota((144, 384), 0)
-    edge = ((n >> 2) + 6) * 8 + (n & 3)
-    go_a_ref[...] = pick(edge + 4 * even)
-    go_b_ref[...] = pick(edge + 4 * (1 - even))
+    n = iota((112, 384), 0)
+    go_a_ref[...] = pick(edge_token(n, even) + 48)
+    go_b_ref[...] = pick(edge_token(n, 1 - even) + 48)
 
 
 def mask_kernel(grid_rows, grid_cols, place_ref, wkv_ref, first_ref, second_ref):
@@ -218,20 +233,15 @@
     )
 
 
-def padded_rim(values):
-    half = values.shape[0] // 2
-    pad = jnp.zeros((8, values.shape[1]), F32)
-    return jnp.concatenate([pad, values[:half], pad, pad, values[half:], pad], axis=0)
-
-
 def first_core_kernel(
     place_ref, mask_ref, a_ref, b_ref, we_ref, wkv_ref, wo_ref, x0_ref, q_ref, kv_ref,
     x1_ref, go_a_ref, go_b_ref,
     p_s, x_s, n_s, rim_s, o_s,
 ):
     means = group_mean_matrix()
-    p_s[0:144, :] = a_ref[...]
-    p_s[144:288, :] = b_ref[...]
+    even = 1 - (place_ref[1] & 1)
+    p_s[0:160, :] = dot(widen((160, 112), 2, even), a_ref[...]).astype(BF)
+    p_s[160:320, :] = dot(widen((160, 112), 2, 1 - even), b_ref[...]).astype(BF)
 
     for g in range(GROUPS):
         x_s[:, cols(g)] = dot(p_s[...], we_ref[:, cols(g)]).astype(BF).astype(F32)
@@ -242,9 +252,8 @@
     for g in range(GROUPS):
         key = dot(n_s[...], wkv_ref[:, cols(g)])
         key = key * lax.rsqrt(group_mean(key * key, means) + EPSILON)
-        rim_s[:, cols(g)] = padded_rim(key).astype(BF)
-        value = dot(n_s[...], wkv_ref[:, cols(g + GROUPS)])
-        rim_s[:, cols(g + GROUPS)] = padded_rim(value).astype(BF)
+        rim_s[:, cols(g)] = key.astype(BF)
+        rim_s[:, cols(g + GROUPS)] = dot(n_s[...], wkv_ref[:, cols(g + GROUPS)]).astype(BF)
 
     masks = head_masks()
 
@@ -258,12 +267,9 @@
             mixed = dot(weight.astype(BF), value) * (1.0 / jnp.where(total > 0, total, 1.0))
             o_s[64 * block : 64 * block + 64, cols(g)] = unstack_heads(mixed).astype(BF)
 
-    n = iota((112, 256), 0)
-    edge = ((n >> 2) + 2) * 8 + (n & 3)
-    source = iota((112, 256), 1)
-    even = 1 - (place_ref[1] & 1)
-    pick_a = jnp.where(edge + 4 * even == source, 1.0, 0.0).astype(BF)
-    pick_b = jnp.where(edge + 4 * (1 - even) == source, 1.0, 0.0).astype(BF)
+    n, source = iota((88, 256), 0), iota((88, 256), 1)
+    pick_a = jnp.where(edge_token(n, even) + 16 == source, 1.0, 0.0).astype(BF)
+    pick_b = jnp.where(edge_token(n, 1 - even) + 16 == source, 1.0, 0.0).astype(BF)
 
     for g in range(GROUPS):
         total = x0_ref[:, cols(g)].astype(F32) + dot(o_s[...], wo_ref[:, cols(g)])
@@ -282,9 +288,11 @@
     residual = x1_ref[...].astype(F32)
     n_s[...] = (residual * row_scale(residual)).astype(BF)
     odd = place_ref[0] & 1
-    c_s[pl.ds(pl.multiple_of(160 - 160 * odd, 16), 32), :] = c_ref[...]
+    c_above = jnp.full((32, D), odd, jnp.int32) == 1
+    c_edge, d_edge = c_ref[...].astype(F32), d_ref[...].astype(F32)
+    c_s[0:32, :] = jnp.where(c_above, c_edge, d_edge).astype(BF)
     c_s[32:160, :] = cot_ref[...]
-    c_s[pl.ds(pl.multiple_of(160 * odd, 16), 32), :] = d_ref[...]
+    c_s[160:192, :] = jnp.where(c_above, d_edge, c_edge).astype(BF)
 
     for g in range(GROUPS):
         query = dot(n_s[32:224, :], wq_ref[:, cols(g)])
@@ -304,13 +312,17 @@
 
 
 def second_core_kernel(
-    mask_ref, a_ref, b_ref, wkv_ref, q_ref, kv_ref, do_ref,
+    place_ref, mask_ref, a_ref, b_ref, wkv_ref, q_ref, kv_ref, do_ref,
     o_ref, dq_ref, dkv_ref, go_a_ref, go_b_ref,
-    n_s, rim_s, rs_s, db_s,
+    n_s, rim_s, rs_s, db_s, sent_s,
 ):
     means = group_mean_matrix()
-    residual = jnp.concatenate([a_ref[...].astype(F32), b_ref[...].astype(F32)], axis=0)
-    residual = padded_rim(residual)
+    even = 1 - (place_ref[1] & 1)
+    parts = [
+        dot(widen((128, 88), 2, right), ref[...])
+        for ref, right in ((a_ref, even), (b_ref, 1 - even))
+    ]
+    residual = jnp.concatenate(parts, axis=0)
     n_s[...] = (residual * row_scale(residual)).astype(BF)
 
     for g in range(GROUPS):
@@ -365,10 +377,18 @@
         dkv_ref[:, cols(g + GROUPS)] = own.astype(BF)
         db_s[:, cols(g + GROUPS)] = rim.astype(BF)
 
-    for g in range(GROUPS):
-        back = dot(db_s[...], wkv_ref[cols(g), :], NT).astype(BF)
-        go_a_ref[:, cols(g)] = back[:64]
-        go_b_ref[:, cols(g)] = back[64:]
+    narrow = []
+    for right in (even, 1 - even):
+        n, m = iota((48, 64), 0), iota((48, 64), 1)
+        row = third(n)
+        narrow.append(jnp.where(row * 4 + (n - 3 * row) + 1 - right == m, 1.0, 0.0).astype(BF))
+    for g in range(2 * GROUPS):
+        sent_s[0:48, cols(g)] = dot(narrow[0], db_s[0:64, cols(g)]).astype(BF)
+        sent_s[48:96, cols(g)] = dot(narrow[1], db_s[64:128, cols(g)]).astype(BF)
+    for g in range(GROUPS):
+        back = dot(sent_s[...], wkv_ref[cols(g), :], NT).astype(BF)
+        go_a_ref[:, cols(g)] = back[:48]
+        go_b_ref[:, cols(g)] = back[48:]
 
 
 def own_back_kernel(
@@ -395,10 +415,11 @@
 
 
 def last_kernel(place_ref, x1_ref, cot_ref, dn_ref, a_ref, b_ref, out_ref):
-    n, source = iota((128, 128), 0), iota((128, 128), 1)
-    right = (source < 64) == ((place_ref[1] & 1) == 0)
-    column = jnp.where(right, (source & 3) + 4, source & 3)
-    token = ((source & 63) >> 2) * 8 + column
+    n, source = iota((128, 96), 0), iota((128, 96), 1)
+    even = 1 - (place_ref[1] & 1)
+    from_a = source < 48
+    right = jnp.where(from_a, even, 1 - even)
+    token = edge_token(jnp.where(from_a, source, source - 48), right)
     pick = jnp.where(n == token, 1.0, 0.0).astype(BF)
     arrived = jnp.concatenate([a_ref[...], b_ref[...]], axis=0)
     back = dn_ref[...] + dot(pick, arrived)
@@ -409,17 +430,22 @@
     out_ref[...] = (cot_ref[...].astype(F32) + scale * (back - normed * mean)).astype(BF)
 
 
-def call(kernel, out_shapes, *operands, scratch=(), flops=0, moved=0, small=None, hbm=False):
+def placed(kernel):
+    def body(*refs):
+        kernel((lax.axis_index("row"), lax.axis_index("col")), *refs)
+
+    return body
+
+
+def call(kernel, out_shapes, *operands, scratch=(), flops=0, moved=0, small=False, hbm=False):
     vmem = pl.BlockSpec(memory_space=pltpu.VMEM)
     in_specs = [pl.BlockSpec(memory_space=pltpu.HBM) if hbm else vmem] * len(operands)
     if hbm:
         operands = tuple(pltpu.with_memory_space_constraint(x, pltpu.HBM) for x in operands)
-    if small is not None:
-        operands = (small,) + operands
-        in_specs = [pl.BlockSpec(memory_space=pltpu.SMEM)] + in_specs
+    body = placed(kernel) if small else kernel
     shapes = tuple(jax.ShapeDtypeStruct(s, d) for s, d in out_shapes)
     return pl.pallas_call(
-        kernel,
+        body,
         out_shape=shapes,
         in_specs=in_specs,
         out_specs=tuple(vmem for _ in shapes),
@@ -443,7 +469,6 @@
 def on_device(patches, tile_slot, w_embed, w_query, w_keyval, w_out, cotangent):
     rows, columns = lax.axis_size("row"), lax.axis_size("col")
     grid_rows, grid_cols = rows * 16, columns * 8
-    place = jnp.stack([lax.axis_index("row"), lax.axis_index("col")]).astype(jnp.int32)
     cot = cotangent.reshape(128, D)
     window = ((96, PIX + 128), BF)
 
@@ -451,7 +476,7 @@
         pack_kernel,
         (window, ((80, PIX + 128), BF), ((32, D), BF), ((32, D), BF)),
         patches, tile_slot.reshape(1, 128), cot,
-        small=place, hbm=True,
+        small=True, hbm=True,
         scratch=(
             ((1, 128), jnp.int32), ((128, 128), BF), (pltpu.SemaphoreType.DMA((5,)), None)
         ),
@@ -461,20 +486,20 @@
         functools.partial(mask_kernel, grid_rows, grid_cols),
         (((4, 256, 256), F32), ((3, 256, 256), F32)),
         w_keyval,
-        small=place,
+        small=True,
     )
     sends = call(
         spread_kernel, (window, window, window), own, far, *masks,
-        small=place, scratch=(window,),
+        small=True, scratch=(window,),
     )
     (touched,) = call(touch_kernel, (((16, 128), F32),), w_embed, w_query, sends[0])
     arrived = [trade(send, "row", step) for send, step in zip(sends, (2, 3, 1))]
     edge_c, edge_d = trade_sides(edge_c, edge_d, "row")
     own, go_a, go_b = call(
         place_kernel,
-        (((320, PIX), BF), ((144, PIX), BF), ((144, PIX), BF)),
+        (((320, PIX), BF), ((112, PIX), BF), ((112, PIX), BF)),
         touched, own, far, *arrived,
-        small=place,
+        small=True,
         scratch=(window,),
     )
     a, b = trade_sides(go_a, go_b, "col")
@@ -487,11 +512,11 @@
     )
     x1, go_a, go_b = call(
         first_core_kernel,
-        (((256, D), BF), ((112, D), BF), ((112, D), BF)),
+        (((256, D), BF), ((88, D), BF), ((88, D), BF)),
         masks[0], a, b, w_embed, w_keyval, w_out, x0, queries, keyval,
-        small=place,
+        small=True,
         scratch=(
-            ((288, PIX), BF), ((288, D), F32), ((288, D), BF), ((320, 2 * D), BF), ((256, D), BF),
+            ((320, PIX), BF), ((320, D), F32), ((320, D), BF), ((320, 2 * D), BF), ((256, D), BF),
         ),
         flops=8 * 10**9, moved=8 * 10**6,
     )
@@ -500,16 +525,18 @@
         own_second_kernel,
         (((192, D), BF), ((256, 2 * D), BF), ((192, D), BF), ((128, D), F32), ((128, D), F32)),
         x1, cot, edge_c, edge_d, w_query, w_keyval, w_out,
-        small=place,
+        small=True,
         scratch=(((256, D), BF), ((192, D), BF)),
         flops=8 * 10**9, moved=8 * 10**6,
     )
     attended, dq, dkv, go_a, go_b = call(
         second_core_kernel,
-        (((192, D), BF), ((192, D), BF), ((128, 2 * D), BF), ((64, D), BF), ((64, D), BF)),
+        (((192, D), BF), ((192, D), BF), ((128, 2 * D), BF), ((48, D), BF), ((48, D), BF)),
         masks[1], a, b, w_keyval, queries, keyval, out_back,
+        small=True,
         scratch=(
             ((256, D), BF), ((256, 2 * D), BF), ((128, D), F32), ((128, 2 * D), BF),
+            ((96, 2 * D), BF),
         ),
         flops=8 * 10**9, moved=8 * 10**6,
     )
@@ -521,7 +548,7 @@
         scratch=(((128, D), BF), ((128, 2 * D), BF)),
         flops=8 * 10**9, moved=8 * 10**6,
     )
-    (input_grad,) = call(last_kernel, (((128, D), BF),), x1, cot, back, a, b, small=place)
+    (input_grad,) = call(last_kernel, (((128, D), BF),), x1, cot, back, a, b, small=True)
     return final_tokens.reshape(16, 8, D), input_grad.reshape(16, 8, D)
 
 

time: 78.2 us -> 74.1 us (0.948)
  Pallas kernels: 32.8 us -> 29.6 us
    pallas_call x11, Pallas kernels: 32.8 us -> 29.6 us  [call(): pl.pallas_call(body, out_shape=shapes, in_specs=in_specs, out_specs=tuple...]
    ppermute x4, waiting for transfers between devices: 8.72 us -> 7.71 us  [trade_sides(): b = lax.ppermute(go_b, axis, [(i, j) for i, j in across if 0 <= j < peers])]
  transfers between devices with their start and end apart: 12 -> 12, of which waited for: 4 -> 4; matrix products, arithmetic and copies ran while one was open for 0% -> 0% of each run, Pallas kernels for 27% -> 26%
where the time goes in v4:
time: 74.1 us; the launch traced here: 73.9 us
  starting transfers between devices  32.2 us (43%)
  Pallas kernels  29.6 us (40%)
  waiting for transfers between devices  8.95 us (12%)
  local copies, waits for them, and re-layouts  2.21 us (3%)
  between operations  0.86 us (1%)
    pallas_call x11, Pallas kernels, call(): pl.pallas_call(body, out_shape=shapes, in_specs=in_specs, out_specs=tuple...  29.6 us
    ppermute x4, starting transfers between devices, trade_sides(): b = lax.ppermute(go_b, axis, [(i, j) for i, j in across if 0 <= j < peers])  19.9 us
    ppermute x8, starting transfers between devices, trade(): lax.ppermute(values, axis, [(i, i ^ step) for i in range(lax.axis_size(ax...  12.3 us
    ppermute x4, waiting for transfers between devices, trade_sides(): b = lax.ppermute(go_b, axis, [(i, j) for i, j in across if 0 <= j < peers])  7.71 us
    unnamed x12, local copies, waits for them, and re-layouts  2.21 us
  transfers between devices with their start and end apart: 12, of which 4 were waited for; matrix products, arithmetic and copies ran while one was open for 0% of the time, Pallas kernels for 26%

profile of v4, /device:TPU:30, one launch (start us, length us, event | category | flops | bytes accessed | tf_op | source)
XLA Modules:
  0.0 73.9 jit_solution(5273880406815495169)
XLA Ops:
  0.6 1.2 %shard_map.87 = (bf16[96,896]{1,0:T(8,128)(2,1)S(1)}, bf16[80,896]{1,0:T(8,128)(2,1)S(1)}, bf16[32,1024]{1,0:T(8,128)(2,1)S(1)}, bf16[32,1024]{1,0:T(8,128)(2,1)S(1)}) custom-call(bf16[128,768]{1,0:T(8,128)(2,1)} %refs_0_.3, s32[1,128]{1,0:T(1,128)} %bitcast.8, bf16[128,1024]{1,0:T(8,128)(2,1)} %bitcast.4), custom_call_target="tpu_custom_call" | custom-call | tf_op jit(solution)/shard_map/pallas_call | solution.py:447
  1.8 7.3 %collective-permute-start = (bf16[80,896]{1,0:T(8,128)(2,1)S(1)}, bf16[80,896]{1,0:T(8,128)(2,1)S(1)}, u32[]{:S(2)}, u32[]{:S(2)}) collective-permute-start(bf16[80,896]{1,0:T(8,128)(2,1)S(1)} %get-tuple-element.34), channel_id=1, source_target_pairs={{0,128},{32,160},{64,192},{96,224},{128,0},{160,32},{192,64},{224,... | collective-permute-start | bytes 430088 | tf_op jit(solution)/shard_map/ppermute | solution.py:459
  9.1 0.0 copy-start
  9.1 2.2 %copy-done = bf16[1024,2048]{1,0:T(8,128)(2,1)S(1)} copy-done((bf16[1024,2048]{1,0:T(8,128)(2,1)S(1)}, bf16[1024,2048]{1,0:T(8,128)(2,1)}, u32[]{:S(2)}) %copy-start) | copy-done | bytes 4194328
  11.3 0.0 copy-start.3
  11.3 0.4 shard_map.86
  11.7 0.0 copy-start.2
  11.7 1.2 %collective-permute-done.refs_1_.refs_2_ = bf16[80,896]{1,0:T(8,128)(2,1)S(1)} collective-permute-done((bf16[80,896]{1,0:T(8,128)(2,1)S(1)}, bf16[80,896]{1,0:T(8,128)(2,1)S(1)}, u32[]{:S(2)}, u32[]{:S(2)}) %collective-permute-start) | collective-permute-done | bytes 143392 | tf_op jit(solution)/shard_map/ppermute | solution.py:459
  12.9 0.1 shard_map.88
  13.0 0.3 collective-permute-start.2
  13.3 1.0 %collective-permute-start.3 = (bf16[96,896]{1,0:T(8,128)(2,1)S(1)}, bf16[96,896]{1,0:T(8,128)(2,1)S(1)}, u32[]{:S(2)}, u32[]{:S(2)}) collective-permute-start(bf16[96,896]{1,0:T(8,128)(2,1)S(1)} %get-tuple-element.38), channel_id=1, source_target_pairs={{0,32},{32,0},{64,96},{96,64},{128,160},{160,128},{192,224},{224,1... | collective-permute-start | bytes 516104 | tf_op jit(solution)/shard_map/ppermute | solution.py:459
  14.3 3.5 %collective-permute-start.1 = (bf16[96,896]{1,0:T(8,128)(2,1)S(1)}, bf16[96,896]{1,0:T(8,128)(2,1)S(1)}, u32[]{:S(2)}, u32[]{:S(2)}) collective-permute-start(bf16[96,896]{1,0:T(8,128)(2,1)S(1)} %get-tuple-element.36.send_ref), channel_id=1, source_target_pairs={{0,64},{32,96},{64,0},{96,32},{128,192},{160,224},{192,128},{224,1... | collective-permute-start | bytes 516104 | tf_op jit(solution)/shard_map/ppermute | solution.py:459
  17.8 0.0 collective-permute-start.8
  17.8 0.0 copy-start.1
  17.8 10.1 %collective-permute-start.9 = (bf16[32,1024]{1,0:T(8,128)(2,1)S(1)}, bf16[32,1024]{1,0:T(8,128)(2,1)S(1)}, u32[]{:S(2)}, u32[]{:S(2)}) collective-permute-start(bf16[32,1024]{1,0:T(8,128)(2,1)S(1)} %get-tuple-element.49), channel_id=1, source_target_pairs={{32,64},{64,32},{96,128},{128,96},{160,192},{192,160},{33,65},{65,... | collective-permute-start | bytes 196616 | tf_op jit(solution)/shard_map/ppermute | solution.py:465
  27.9 0.0 copy-done.3
  27.9 0.0 copy-done.2
  27.9 0.0 collective-permute-done.2.refs_4_
  28.0 0.0 collective-permute-done.3.refs_5_
  28.0 0.0 collective-permute-done.1.refs_3_
  28.0 0.7 shard_map.90
  28.7 0.1 collective-permute-start.4
  28.8 3.1 %collective-permute-start.5 = (bf16[112,768]{1,0:T(8,128)(2,1)S(1)}, bf16[112,768]{1,0:T(8,128)(2,1)S(1)}, u32[]{:S(2)}, u32[]{:S(2)}) collective-permute-start(bf16[112,768]{1,0:T(8,128)(2,1)S(1)} %get-tuple-element.40), channel_id=1, source_target_pairs={{1,2},{2,1},{3,4},{4,3},{5,6},{6,5},{7,8},{8,7},{9,10},{10,9},{11,... | collective-permute-start | bytes 516104 | tf_op jit(solution)/shard_map/ppermute | solution.py:465
  31.8 0.0 copy-done.1
  31.9 0.0 copy-start.5
  31.9 4.3 %shard_map.91 = (bf16[256,1024]{1,0:T(8,128)(2,1)S(1)}, bf16[256,1024]{1,0:T(8,128)(2,1)S(1)}, bf16[320,2048]{1,0:T(8,128)(2,1)S(1)}) custom-call(bf16[320,768]{1,0:T(8,128)(2,1)S(1)} %get-tuple-element.41.own_ref, bf16[768,1024]{1,0:T(8,128)(2,1)S(1)} %copy-done.3, bf16[1024,1024]{1,0:T(8,128)(2,1)S(1)} %copy-done.2, bf16[1024,2048]{1,0:T(8,128)(2,1)S(1)} %copy-done.1), custom_call_target="tpu_custom_call" | custom-call | flops 8000000000 | bytes 8000000 | tf_op jit(solution)/shard_map/pallas_call | solution.py:447
  36.2 0.0 collective-permute-done.4.refs_1_
  36.2 3.7 %collective-permute-done.5.refs_2_ = bf16[112,768]{1,0:T(8,128)(2,1)S(1)} collective-permute-done((bf16[112,768]{1,0:T(8,128)(2,1)S(1)}, bf16[112,768]{1,0:T(8,128)(2,1)S(1)}, u32[]{:S(2)}, u32[]{:S(2)}) %collective-permute-start.5) | collective-permute-done | bytes 172064 | tf_op jit(solution)/shard_map/ppermute | solution.py:465
  39.9 0.0 copy-done.5
  39.9 0.0 copy-start.4
  39.9 6.1 %shard_map.92 = (bf16[256,1024]{1,0:T(8,128)(2,1)S(1)}, bf16[88,1024]{1,0:T(8,128)(2,1)S(1)}, bf16[88,1024]{1,0:T(8,128)(2,1)S(1)}) custom-call(f32[4,256,256]{2,1,0:T(8,128)S(1)} %get-tuple-element.32.refs_2_.refs_0_, bf16[112,768]{1,0:T(8,128)(2,1)S(1)} %collective-permute-done.4.refs_1_, bf16[112,768]{1,0:T(8,128)(2,1)S(1)} %collective-permute-done.5.refs_2_, ...), custom_call_target="tpu_custom_call" | custom-call | flops 8000000000 | bytes 8000000 | tf_op jit(solution)/shard_map/pallas_call | solution.py:447
  46.0 0.1 collective-permute-start.6
  46.1 3.1 %collective-permute-start.7 = (bf16[88,1024]{1,0:T(8,128)(2,1)S(1)}, bf16[88,1024]{1,0:T(8,128)(2,1)S(1)}, u32[]{:S(2)}, u32[]{:S(2)}) collective-permute-start(bf16[88,1024]{1,0:T(8,128)(2,1)S(1)} %get-tuple-element.47), channel_id=1, source_target_pairs={{1,2},{2,1},{3,4},{4,3},{5,6},{6,5},{7,8},{8,7},{9,10},{10,9},{11,... | collective-permute-start | bytes 540680 | tf_op jit(solution)/shard_map/ppermute | solution.py:465
  49.2 0.0 collective-permute-done.8.refs_2_
  49.2 0.0 collective-permute-done.9.refs_3_
  49.2 0.0 copy-done.4
  49.2 4.2 %shard_map.93 = (bf16[192,1024]{1,0:T(8,128)(2,1)S(1)}, bf16[256,2048]{1,0:T(8,128)(2,1)S(1)}, bf16[192,1024]{1,0:T(8,128)(2,1)S(1)}, f32[128,1024]{1,0:T(8,128)S(1)}, f32[128,1024]{1,0:T(8,128)S(1)}) custom-call(bf16[256,1024]{1,0:T(8,128)(2,1)S(1)} %get-tuple-element.45.refs_0_.x1_ref, bf16[128,1024]{1,0:T(8,128)(2,1)S(1)} %bitcast.5, ...), custom_call_target="tpu_custom_call" | custom-call | flops 8000000000 | bytes 8000000 | tf_op jit(solution)/shard_map/pallas_call | solution.py:447
  53.4 0.0 collective-permute-done.6.refs_1_
  53.4 2.2 %collective-permute-done.7.refs_2_ = bf16[88,1024]{1,0:T(8,128)(2,1)S(1)} collective-permute-done((bf16[88,1024]{1,0:T(8,128)(2,1)S(1)}, bf16[88,1024]{1,0:T(8,128)(2,1)S(1)}, u32[]{:S(2)}, u32[]{:S(2)}) %collective-permute-start.7) | collective-permute-done | bytes 180256 | tf_op jit(solution)/shard_map/ppermute | solution.py:465
  55.6 8.5 %shard_map.94 = (bf16[192,1024]{1,0:T(8,128)(2,1)S(1)}, bf16[192,1024]{1,0:T(8,128)(2,1)S(1)}, bf16[128,2048]{1,0:T(8,128)(2,1)S(1)}, bf16[48,1024]{1,0:T(8,128)(2,1)S(1)}, bf16[48,1024]{1,0:T(8,128)(2,1)S(1)}) custom-call(f32[3,256,256]{2,1,0:T(8,128)S(1)} %get-tuple-element.35.refs_3_.refs_0_, bf16[88,1024]{1,0:T(8,128)(2,1)S(1)} %collective-permute-done.6.refs_1_, ...), custom_call_target="tpu_custom_call" | custom-call | flops 8000000000 | bytes 8000000 | tf_op jit(solution)/shard_map/pallas_call | solution.py:447
  64.1 0.1 collective-permute-start.10
  64.2 3.6 %collective-permute-start.11 = (bf16[48,1024]{1,0:T(8,128)(2,1)S(1)}, bf16[48,1024]{1,0:T(8,128)(2,1)S(1)}, u32[]{:S(2)}, u32[]{:S(2)}) collective-permute-start(bf16[48,1024]{1,0:T(8,128)(2,1)S(1)} %get-tuple-element.61), channel_id=1, source_target_pairs={{1,2},{2,1},{3,4},{4,3},{5,6},{6,5},{7,8},{8,7},{9,10},{10,9},{11,... | collective-permute-start | bytes 294920 | tf_op jit(solution)/shard_map/ppermute | solution.py:465
  67.8 3.3 %shard_map.95 = (bf16[128,1024]{1,0:T(8,128)(2,1)}, f32[128,1024]{1,0:T(8,128)S(1)}) custom-call(bf16[256,1024]{1,0:T(8,128)(2,1)S(1)} %get-tuple-element.45.refs_0_.x1_ref, bf16[192,1024]{1,0:T(8,128)(2,1)S(1)} %get-tuple-element.53.o_ref, bf16[192,1024]{1,0:T(8,128)(2,1)S(1)} %get-tuple-element.54.dq_ref, bf16[128,2048]{1,0:T(8,128)(2,1)S(1)} %get-tuple-element.55.dkv_ref, ...), custom_call_target="tpu_custom_call" | custom-call | flops 8000000000 | bytes 8000000 | tf_op jit(solution)/shard_map/pallas_call | solution.py:447
  71.1 0.0 collective-permute-done.10.refs_3_
  71.1 1.7 %collective-permute-done.11.refs_4_ = bf16[48,1024]{1,0:T(8,128)(2,1)S(1)} collective-permute-done((bf16[48,1024]{1,0:T(8,128)(2,1)S(1)}, bf16[48,1024]{1,0:T(8,128)(2,1)S(1)}, u32[]{:S(2)}, u32[]{:S(2)}) %collective-permute-start.11) | collective-permute-done | bytes 98336 | tf_op jit(solution)/shard_map/ppermute | solution.py:465
  72.8 1.1 %shard_map.96 = bf16[128,1024]{1,0:T(8,128)(2,1)} custom-call(bf16[256,1024]{1,0:T(8,128)(2,1)S(1)} %get-tuple-element.45.refs_0_.x1_ref, bf16[128,1024]{1,0:T(8,128)(2,1)S(1)} %bitcast.6, f32[128,1024]{1,0:T(8,128)S(1)} %get-tuple-element.59.refs_2_, bf16[48,1024]{1,0:T(8,128)(2,1)S(1)} %collective-permute-done.10.refs_3_, ...), custom_call_target="tpu_custom_call" | custom-call | tf_op jit(solution)/shard_map/pallas_call | solution.py:447
  (1 shorter events, 0.0 us)
Async XLA Ops:
  1.8 11.1 %collective-permute-start = (bf16[80,896]{1,0:T(8,128)(2,1)S(1)}, bf16[80,896]{1,0:T(8,128)(2,1)S(1)}, u32[]{:S(2)}, u32[]{:S(2)}) collective-permute-start(bf16[80,896]{1,0:T(8,128)(2,1)S(1)} %get-tuple-element.34), channel_id=1, source_target_pairs={{0,128},{32,160},{64,192},{96,224},{128,0},{160,32},{192,64},{224,... | collective-permute-start | bytes 430088 | tf_op jit(solution)/shard_map/ppermute | solution.py:459
  9.1 2.2 %copy-start = (bf16[1024,2048]{1,0:T(8,128)(2,1)S(1)}, bf16[1024,2048]{1,0:T(8,128)(2,1)}, u32[]{:S(2)}) copy-start(bf16[1024,2048]{1,0:T(8,128)(2,1)} %wkv_ref.3) | copy-start | bytes 12582916
  11.3 16.6 %copy-start.3 = (bf16[768,1024]{1,0:T(8,128)(2,1)S(1)}, bf16[768,1024]{1,0:T(8,128)(2,1)}, u32[]{:S(2)}) copy-start(bf16[768,1024]{1,0:T(8,128)(2,1)} %refs_3_.2) | copy-start | bytes 4718596
  11.7 16.2 %copy-start.2 = (bf16[1024,1024]{1,0:T(8,128)(2,1)S(1)}, bf16[1024,1024]{1,0:T(8,128)(2,1)}, u32[]{:S(2)}) copy-start(bf16[1024,1024]{1,0:T(8,128)(2,1)} %wq_ref.5) | copy-start | bytes 6291460
  13.0 14.9 %collective-permute-start.2 = (bf16[96,896]{1,0:T(8,128)(2,1)S(1)}, bf16[96,896]{1,0:T(8,128)(2,1)S(1)}, u32[]{:S(2)}, u32[]{:S(2)}) collective-permute-start(bf16[96,896]{1,0:T(8,128)(2,1)S(1)} %get-tuple-element.37), channel_id=1, source_target_pairs={{0,96},{32,64},{64,32},{96,0},{128,224},{160,192},{192,160},{224,1... | collective-permute-start | bytes 516104 | tf_op jit(solution)/shard_map/ppermute | solution.py:459
  13.3 14.6 %collective-permute-start.3 = (bf16[96,896]{1,0:T(8,128)(2,1)S(1)}, bf16[96,896]{1,0:T(8,128)(2,1)S(1)}, u32[]{:S(2)}, u32[]{:S(2)}) collective-permute-start(bf16[96,896]{1,0:T(8,128)(2,1)S(1)} %get-tuple-element.38), channel_id=1, source_target_pairs={{0,32},{32,0},{64,96},{96,64},{128,160},{160,128},{192,224},{224,1... | collective-permute-start | bytes 516104 | tf_op jit(solution)/shard_map/ppermute | solution.py:459
  14.3 13.7 %collective-permute-start.1 = (bf16[96,896]{1,0:T(8,128)(2,1)S(1)}, bf16[96,896]{1,0:T(8,128)(2,1)S(1)}, u32[]{:S(2)}, u32[]{:S(2)}) collective-permute-start(bf16[96,896]{1,0:T(8,128)(2,1)S(1)} %get-tuple-element.36.send_ref), channel_id=1, source_target_pairs={{0,64},{32,96},{64,0},{96,32},{128,192},{160,224},{192,128},{224,1... | collective-permute-start | bytes 516104 | tf_op jit(solution)/shard_map/ppermute | solution.py:459
  17.8 31.4 %collective-permute-start.8 = (bf16[32,1024]{1,0:T(8,128)(2,1)S(1)}, bf16[32,1024]{1,0:T(8,128)(2,1)S(1)}, u32[]{:S(2)}, u32[]{:S(2)}) collective-permute-start(bf16[32,1024]{1,0:T(8,128)(2,1)S(1)} %get-tuple-element.48), channel_id=1, source_target_pairs={{0,32},{32,0},{64,96},{96,64},{128,160},{160,128},{192,224},{224,1... | collective-permute-start | bytes 196616 | tf_op jit(solution)/shard_map/ppermute | solution.py:459
  17.8 14.0 %copy-start.1 = (bf16[1024,2048]{1,0:T(8,128)(2,1)S(1)}, bf16[1024,2048]{1,0:T(8,128)(2,1)}, u32[]{:S(2)}) copy-start(bf16[1024,2048]{1,0:T(8,128)(2,1)} %wkv_ref.3) | copy-start | bytes 12582916
  17.8 31.4 %collective-permute-start.9 = (bf16[32,1024]{1,0:T(8,128)(2,1)S(1)}, bf16[32,1024]{1,0:T(8,128)(2,1)S(1)}, u32[]{:S(2)}, u32[]{:S(2)}) collective-permute-start(bf16[32,1024]{1,0:T(8,128)(2,1)S(1)} %get-tuple-element.49), channel_id=1, source_target_pairs={{32,64},{64,32},{96,128},{128,96},{160,192},{192,160},{33,65},{65,... | collective-permute-start | bytes 196616 | tf_op jit(solution)/shard_map/ppermute | solution.py:465
  28.7 7.5 %collective-permute-start.4 = (bf16[112,768]{1,0:T(8,128)(2,1)S(1)}, bf16[112,768]{1,0:T(8,128)(2,1)S(1)}, u32[]{:S(2)}, u32[]{:S(2)}) collective-permute-start(bf16[112,768]{1,0:T(8,128)(2,1)S(1)} %get-tuple-element.39), channel_id=1, source_target_pairs={{0,1},{1,0},{2,3},{3,2},{4,5},{5,4},{6,7},{7,6},{8,9},{9,8},{10,11... | collective-permute-start | bytes 516104 | tf_op jit(solution)/shard_map/ppermute | solution.py:459
  28.8 11.2 %collective-permute-start.5 = (bf16[112,768]{1,0:T(8,128)(2,1)S(1)}, bf16[112,768]{1,0:T(8,128)(2,1)S(1)}, u32[]{:S(2)}, u32[]{:S(2)}) collective-permute-start(bf16[112,768]{1,0:T(8,128)(2,1)S(1)} %get-tuple-element.40), channel_id=1, source_target_pairs={{1,2},{2,1},{3,4},{4,3},{5,6},{6,5},{7,8},{8,7},{9,10},{10,9},{11,... | collective-permute-start | bytes 516104 | tf_op jit(solution)/shard_map/ppermute | solution.py:465
  31.9 8.1 %copy-start.5 = (bf16[1024,1024]{1,0:T(8,128)(2,1)S(1)}, bf16[1024,1024]{1,0:T(8,128)(2,1)}, u32[]{:S(2)}) copy-start(bf16[1024,1024]{1,0:T(8,128)(2,1)} %wo_ref.1) | copy-start | bytes 6291460
  39.9 9.3 %copy-start.4 = (bf16[16,8,1024]{2,1,0:T(8,128)(2,1)S(1)}, bf16[16,8,1024]{2,1,0:T(8,128)(2,1)}, u32[]{:S(2)}) copy-start(bf16[16,8,1024]{2,1,0:T(8,128)(2,1)} %param.13) | copy-start | bytes 786436
  46.0 7.4 %collective-permute-start.6 = (bf16[88,1024]{1,0:T(8,128)(2,1)S(1)}, bf16[88,1024]{1,0:T(8,128)(2,1)S(1)}, u32[]{:S(2)}, u32[]{:S(2)}) collective-permute-start(bf16[88,1024]{1,0:T(8,128)(2,1)S(1)} %get-tuple-element.46), channel_id=1, source_target_pairs={{0,1},{1,0},{2,3},{3,2},{4,5},{5,4},{6,7},{7,6},{8,9},{9,8},{10,11... | collective-permute-start | bytes 540680 | tf_op jit(solution)/shard_map/ppermute | solution.py:459
  46.1 9.5 %collective-permute-start.7 = (bf16[88,1024]{1,0:T(8,128)(2,1)S(1)}, bf16[88,1024]{1,0:T(8,128)(2,1)S(1)}, u32[]{:S(2)}, u32[]{:S(2)}) collective-permute-start(bf16[88,1024]{1,0:T(8,128)(2,1)S(1)} %get-tuple-element.47), channel_id=1, source_target_pairs={{1,2},{2,1},{3,4},{4,3},{5,6},{6,5},{7,8},{8,7},{9,10},{10,9},{11,... | collective-permute-start | bytes 540680 | tf_op jit(solution)/shard_map/ppermute | solution.py:465
  64.1 7.0 %collective-permute-start.10 = (bf16[48,1024]{1,0:T(8,128)(2,1)S(1)}, bf16[48,1024]{1,0:T(8,128)(2,1)S(1)}, u32[]{:S(2)}, u32[]{:S(2)}) collective-permute-start(bf16[48,1024]{1,0:T(8,128)(2,1)S(1)} %get-tuple-element.60), channel_id=1, source_target_pairs={{0,1},{1,0},{2,3},{3,2},{4,5},{5,4},{6,7},{7,6},{8,9},{9,8},{10,11... | collective-permute-start | bytes 294920 | tf_op jit(solution)/shard_map/ppermute | solution.py:459
  64.2 8.6 %collective-permute-start.11 = (bf16[48,1024]{1,0:T(8,128)(2,1)S(1)}, bf16[48,1024]{1,0:T(8,128)(2,1)S(1)}, u32[]{:S(2)}, u32[]{:S(2)}) collective-permute-start(bf16[48,1024]{1,0:T(8,128)(2,1)S(1)} %get-tuple-element.61), channel_id=1, source_target_pairs={{1,2},{2,1},{3,4},{4,3},{5,6},{6,5},{7,8},{8,7},{9,10},{10,9},{11,... | collective-permute-start | bytes 294920 | tf_op jit(solution)/shard_map/ppermute | solution.py:465

commit v5 on v4

--- a/solution.py
+++ b/solution.py
@@ -62,7 +62,7 @@
 
 
 def key_places(key, first_row, col_index, grid_rows, grid_cols):
-    right = (key < 192) == ((col_index & 1) == 0)
+    right = (key < 192) == ((col_index & 1) == 1)
     rim = key & 63
     key_row = jnp.where(key < 128, key >> 3, rim >> 2)
     rim_col = jnp.where(right, (rim & 3) + 8, (rim & 3) - 4)
@@ -176,7 +176,7 @@
     tile = lax.rem(iota((8, 384), 1) >> 4, 3)
     slot = jnp.concatenate(slots, axis=1) + 128.0 * tile.astype(F32)
     source = source[:, :PIX]
-    even = 1 - (place_ref[1] & 1)
+    a_right = place_ref[1] & 1
 
     def pick(position):
         hot = jnp.where(position.astype(F32) == slot[:1], 1.0, 0.0).astype(BF)
@@ -184,8 +184,8 @@
 
     own_ref[...] = pick(iota((320, 384), 0) + 32)
     n = iota((112, 384), 0)
-    go_a_ref[...] = pick(edge_token(n, even) + 48)
-    go_b_ref[...] = pick(edge_token(n, 1 - even) + 48)
+    go_a_ref[...] = pick(edge_token(n, a_right) + 48)
+    go_b_ref[...] = pick(edge_token(n, 1 - a_right) + 48)
 
 
 def mask_kernel(grid_rows, grid_cols, place_ref, wkv_ref, first_ref, second_ref):
@@ -239,9 +239,9 @@
     p_s, x_s, n_s, rim_s, o_s,
 ):
     means = group_mean_matrix()
-    even = 1 - (place_ref[1] & 1)
-    p_s[0:160, :] = dot(widen((160, 112), 2, even), a_ref[...]).astype(BF)
-    p_s[160:320, :] = dot(widen((160, 112), 2, 1 - even), b_ref[...]).astype(BF)
+    a_right = place_ref[1] & 1
+    p_s[0:160, :] = dot(widen((160, 112), 2, a_right), a_ref[...]).astype(BF)
+    p_s[160:320, :] = dot(widen((160, 112), 2, 1 - a_right), b_ref[...]).astype(BF)
 
     for g in range(GROUPS):
         x_s[:, cols(g)] = dot(p_s[...], we_ref[:, cols(g)]).astype(BF).astype(F32)
@@ -268,8 +268,8 @@
             o_s[64 * block : 64 * block + 64, cols(g)] = unstack_heads(mixed).astype(BF)
 
     n, source = iota((88, 256), 0), iota((88, 256), 1)
-    pick_a = jnp.where(edge_token(n, even) + 16 == source, 1.0, 0.0).astype(BF)
-    pick_b = jnp.where(edge_token(n, 1 - even) + 16 == source, 1.0, 0.0).astype(BF)
+    pick_a = jnp.where(edge_token(n, a_right) + 16 == source, 1.0, 0.0).astype(BF)
+    pick_b = jnp.where(edge_token(n, 1 - a_right) + 16 == source, 1.0, 0.0).astype(BF)
 
     for g in range(GROUPS):
         total = x0_ref[:, cols(g)].astype(F32) + dot(o_s[...], wo_ref[:, cols(g)])
@@ -317,10 +317,10 @@
     n_s, rim_s, rs_s, db_s, sent_s,
 ):
     means = group_mean_matrix()
-    even = 1 - (place_ref[1] & 1)
+    a_right = place_ref[1] & 1
     parts = [
         dot(widen((128, 88), 2, right), ref[...])
-        for ref, right in ((a_ref, even), (b_ref, 1 - even))
+        for ref, right in ((a_ref, a_right), (b_ref, 1 - a_right))
     ]
     residual = jnp.concatenate(parts, axis=0)
     n_s[...] = (residual * row_scale(residual)).astype(BF)
@@ -378,7 +378,7 @@
         db_s[:, cols(g + GROUPS)] = rim.astype(BF)
 
     narrow = []
-    for right in (even, 1 - even):
+    for right in (a_right, 1 - a_right):
         n, m = iota((48, 64), 0), iota((48, 64), 1)
         row = third(n)
         narrow.append(jnp.where(row * 4 + (n - 3 * row) + 1 - right == m, 1.0, 0.0).astype(BF))
@@ -416,9 +416,9 @@
 
 def last_kernel(place_ref, x1_ref, cot_ref, dn_ref, a_ref, b_ref, out_ref):
     n, source = iota((128, 96), 0), iota((128, 96), 1)
-    even = 1 - (place_ref[1] & 1)
+    a_right = place_ref[1] & 1
     from_a = source < 48
-    right = jnp.where(from_a, even, 1 - even)
+    right = jnp.where(from_a, a_right, 1 - a_right)
     token = edge_token(jnp.where(from_a, source, source - 48), right)
     pick = jnp.where(n == token, 1.0, 0.0).astype(BF)
     arrived = jnp.concatenate([a_ref[...], b_ref[...]], axis=0)
@@ -459,11 +459,14 @@
     return lax.ppermute(values, axis, [(i, i ^ step) for i in range(lax.axis_size(axis))])
 
 
-def trade_sides(go_a, go_b, axis):
+def trade_across(values, axis):
     peers = lax.axis_size(axis)
-    across = [(i, ((i + 1) ^ 1) - 1) for i in range(peers)]
-    b = lax.ppermute(go_b, axis, [(i, j) for i, j in across if 0 <= j < peers])
-    return trade(go_a, axis, 1), b
+    pairs = [(i, ((i + 1) ^ 1) - 1) for i in range(peers)]
+    return lax.ppermute(values, axis, [(i, j) for i, j in pairs if 0 <= j < peers])
+
+
+def trade_sides(go_a, go_b):
+    return trade_across(go_a, "col"), trade(go_b, "col", 1)
 
 
 def on_device(patches, tile_slot, w_embed, w_query, w_keyval, w_out, cotangent):
@@ -494,7 +497,7 @@
     )
     (touched,) = call(touch_kernel, (((16, 128), F32),), w_embed, w_query, sends[0])
     arrived = [trade(send, "row", step) for send, step in zip(sends, (2, 3, 1))]
-    edge_c, edge_d = trade_sides(edge_c, edge_d, "row")
+    edge_c, edge_d = trade(edge_c, "row", 1), trade_across(edge_d, "row")
     own, go_a, go_b = call(
         place_kernel,
         (((320, PIX), BF), ((112, PIX), BF), ((112, PIX), BF)),
@@ -502,7 +505,7 @@
         small=True,
         scratch=(window,),
     )
-    a, b = trade_sides(go_a, go_b, "col")
+    a, b = trade_sides(go_a, go_b)
     x0, queries, keyval = call(
         own_first_kernel,
         (((256, D), BF), ((256, D), BF), ((320, 2 * D), BF)),
@@ -520,7 +523,7 @@
         ),
         flops=8 * 10**9, moved=8 * 10**6,
     )
-    a, b = trade_sides(go_a, go_b, "col")
+    a, b = trade_sides(go_a, go_b)
     queries, keyval, out_back, query_scale, key_scale = call(
         own_second_kernel,
         (((192, D), BF), ((256, 2 * D), BF), ((192, D), BF), ((128, D), F32), ((128, D), F32)),
@@ -540,7 +543,7 @@
         ),
         flops=8 * 10**9, moved=8 * 10**6,
     )
-    a, b = trade_sides(go_a, go_b, "col")
+    a, b = trade_sides(go_a, go_b)
     final_tokens, back = call(
         own_back_kernel,
         (((128, D), BF), ((128, D), F32)),

time: 74.1 us -> 72.2 us (0.974)
  waiting for transfers between devices: 8.95 us -> 5.94 us
  starting transfers between devices: 32.2 us -> 33.3 us
    ppermute x4, waiting for transfers between devices: 7.71 us -> 4.7 us  [trade_across(): lax.ppermute(values, axis, [(i, j) for i, j in pairs if 0 <= j < peers])]
    ppermute x8, starting transfers between devices: 12.3 us -> 14.6 us  [trade(): lax.ppermute(values, axis, [(i, i ^ step) for i in range(lax.axis_size(ax...]
    ppermute x4, starting transfers between devices: 19.9 us -> 18.8 us  [trade_across(): lax.ppermute(values, axis, [(i, j) for i, j in pairs if 0 <= j < peers])]
where the time goes in v5:
time: 72.2 us; the launch traced here: 72 us
  starting transfers between devices  33.3 us (46%)
  Pallas kernels  29.6 us (41%)
  waiting for transfers between devices  5.94 us (8%)
  local copies, waits for them, and re-layouts  2.21 us (3%)
  between operations  0.83 us (1%)
    pallas_call x11, Pallas kernels, call(): pl.pallas_call(body, out_shape=shapes, in_specs=in_specs, out_specs=tuple...  29.6 us
    ppermute x4, starting transfers between devices, trade_across(): lax.ppermute(values, axis, [(i, j) for i, j in pairs if 0 <= j < peers])  18.8 us
    ppermute x8, starting transfers between devices, trade(): lax.ppermute(values, axis, [(i, i ^ step) for i in range(lax.axis_size(ax...  14.6 us
    ppermute x4, waiting for transfers between devices, trade_across(): lax.ppermute(values, axis, [(i, j) for i, j in pairs if 0 <= j < peers])  4.7 us
    unnamed x12, local copies, waits for them, and re-layouts  2.21 us
  transfers between devices with their start and end apart: 12, of which 4 were waited for; matrix products, arithmetic and copies ran while one was open for 0% of the time, Pallas kernels for 26%

profile of v5, /device:TPU:30, one launch (start us, length us, event | category | flops | bytes accessed | tf_op | source)
XLA Modules:
  0.0 72.0 jit_solution(7864223551086145178)
XLA Ops:
  0.6 1.2 %shard_map.87 = (bf16[96,896]{1,0:T(8,128)(2,1)S(1)}, bf16[80,896]{1,0:T(8,128)(2,1)S(1)}, bf16[32,1024]{1,0:T(8,128)(2,1)S(1)}, bf16[32,1024]{1,0:T(8,128)(2,1)S(1)}) custom-call(bf16[128,768]{1,0:T(8,128)(2,1)} %refs_0_.3, s32[1,128]{1,0:T(1,128)} %bitcast.8, bf16[128,1024]{1,0:T(8,128)(2,1)} %bitcast.4), custom_call_target="tpu_custom_call" | custom-call | tf_op jit(solution)/shard_map/pallas_call | solution.py:447
  1.8 7.3 %collective-permute-start = (bf16[80,896]{1,0:T(8,128)(2,1)S(1)}, bf16[80,896]{1,0:T(8,128)(2,1)S(1)}, u32[]{:S(2)}, u32[]{:S(2)}) collective-permute-start(bf16[80,896]{1,0:T(8,128)(2,1)S(1)} %get-tuple-element.34), channel_id=1, source_target_pairs={{0,128},{32,160},{64,192},{96,224},{128,0},{160,32},{192,64},{224,... | collective-permute-start | bytes 430088 | tf_op jit(solution)/shard_map/ppermute | solution.py:459
  9.1 0.0 copy-start
  9.1 2.2 %copy-done = bf16[1024,2048]{1,0:T(8,128)(2,1)S(1)} copy-done((bf16[1024,2048]{1,0:T(8,128)(2,1)S(1)}, bf16[1024,2048]{1,0:T(8,128)(2,1)}, u32[]{:S(2)}) %copy-start) | copy-done | bytes 4194328
  11.3 0.0 copy-start.3
  11.3 0.4 shard_map.86
  11.7 0.0 copy-start.2
  11.7 1.2 %collective-permute-done.refs_1_.refs_2_ = bf16[80,896]{1,0:T(8,128)(2,1)S(1)} collective-permute-done((bf16[80,896]{1,0:T(8,128)(2,1)S(1)}, bf16[80,896]{1,0:T(8,128)(2,1)S(1)}, u32[]{:S(2)}, u32[]{:S(2)}) %collective-permute-start) | collective-permute-done | bytes 143392 | tf_op jit(solution)/shard_map/ppermute | solution.py:459
  12.9 0.1 shard_map.88
  13.0 0.3 collective-permute-start.2
  13.3 1.0 %collective-permute-start.3 = (bf16[96,896]{1,0:T(8,128)(2,1)S(1)}, bf16[96,896]{1,0:T(8,128)(2,1)S(1)}, u32[]{:S(2)}, u32[]{:S(2)}) collective-permute-start(bf16[96,896]{1,0:T(8,128)(2,1)S(1)} %get-tuple-element.38), channel_id=1, source_target_pairs={{0,32},{32,0},{64,96},{96,64},{128,160},{160,128},{192,224},{224,1... | collective-permute-start | bytes 516104 | tf_op jit(solution)/shard_map/ppermute | solution.py:459
  14.3 3.5 %collective-permute-start.1 = (bf16[96,896]{1,0:T(8,128)(2,1)S(1)}, bf16[96,896]{1,0:T(8,128)(2,1)S(1)}, u32[]{:S(2)}, u32[]{:S(2)}) collective-permute-start(bf16[96,896]{1,0:T(8,128)(2,1)S(1)} %get-tuple-element.36.send_ref), channel_id=1, source_target_pairs={{0,64},{32,96},{64,0},{96,32},{128,192},{160,224},{192,128},{224,1... | collective-permute-start | bytes 516104 | tf_op jit(solution)/shard_map/ppermute | solution.py:459
  17.8 0.0 collective-permute-start.8
  17.8 0.0 copy-start.1
  17.8 10.1 %collective-permute-start.9 = (bf16[32,1024]{1,0:T(8,128)(2,1)S(1)}, bf16[32,1024]{1,0:T(8,128)(2,1)S(1)}, u32[]{:S(2)}, u32[]{:S(2)}) collective-permute-start(bf16[32,1024]{1,0:T(8,128)(2,1)S(1)} %get-tuple-element.49), channel_id=1, source_target_pairs={{32,64},{64,32},{96,128},{128,96},{160,192},{192,160},{33,65},{65,... | collective-permute-start | bytes 196616 | tf_op jit(solution)/shard_map/ppermute | solution.py:465
  27.9 0.0 copy-done.3
  27.9 0.0 copy-done.2
  27.9 0.0 collective-permute-done.2.refs_4_
  28.0 0.0 collective-permute-done.3.refs_5_
  28.0 0.0 collective-permute-done.1.refs_3_
  28.0 0.7 shard_map.90
  28.7 1.9 %collective-permute-start.4 = (bf16[112,768]{1,0:T(8,128)(2,1)S(1)}, bf16[112,768]{1,0:T(8,128)(2,1)S(1)}, u32[]{:S(2)}, u32[]{:S(2)}) collective-permute-start(bf16[112,768]{1,0:T(8,128)(2,1)S(1)} %get-tuple-element.39), channel_id=1, source_target_pairs={{1,2},{2,1},{3,4},{4,3},{5,6},{6,5},{7,8},{8,7},{9,10},{10,9},{11,... | collective-permute-start | bytes 516104 | tf_op jit(solution)/shard_map/ppermute | solution.py:465
  30.6 2.1 %collective-permute-start.5 = (bf16[112,768]{1,0:T(8,128)(2,1)S(1)}, bf16[112,768]{1,0:T(8,128)(2,1)S(1)}, u32[]{:S(2)}, u32[]{:S(2)}) collective-permute-start(bf16[112,768]{1,0:T(8,128)(2,1)S(1)} %get-tuple-element.40), channel_id=1, source_target_pairs={{0,1},{1,0},{2,3},{3,2},{4,5},{5,4},{6,7},{7,6},{8,9},{9,8},{10,11... | collective-permute-start | bytes 516104 | tf_op jit(solution)/shard_map/ppermute | solution.py:459
  32.7 0.0 copy-done.1
  32.7 0.0 copy-start.5
  32.7 4.3 %shard_map.91 = (bf16[256,1024]{1,0:T(8,128)(2,1)S(1)}, bf16[256,1024]{1,0:T(8,128)(2,1)S(1)}, bf16[320,2048]{1,0:T(8,128)(2,1)S(1)}) custom-call(bf16[320,768]{1,0:T(8,128)(2,1)S(1)} %get-tuple-element.41.own_ref, bf16[768,1024]{1,0:T(8,128)(2,1)S(1)} %copy-done.3, bf16[1024,1024]{1,0:T(8,128)(2,1)S(1)} %copy-done.2, bf16[1024,2048]{1,0:T(8,128)(2,1)S(1)} %copy-done.1), custom_call_target="tpu_custom_call" | custom-call | flops 8000000000 | bytes 8000000 | tf_op jit(solution)/shard_map/pallas_call | solution.py:447
  37.0 1.2 %collective-permute-done.4.refs_1_ = bf16[112,768]{1,0:T(8,128)(2,1)S(1)} collective-permute-done((bf16[112,768]{1,0:T(8,128)(2,1)S(1)}, bf16[112,768]{1,0:T(8,128)(2,1)S(1)}, u32[]{:S(2)}, u32[]{:S(2)}) %collective-permute-start.4) | collective-permute-done | bytes 172064 | tf_op jit(solution)/shard_map/ppermute | solution.py:465
  38.2 0.0 collective-permute-done.5.refs_2_
  38.2 0.0 copy-done.5
  38.2 0.0 copy-start.4
  38.2 6.1 %shard_map.92 = (bf16[256,1024]{1,0:T(8,128)(2,1)S(1)}, bf16[88,1024]{1,0:T(8,128)(2,1)S(1)}, bf16[88,1024]{1,0:T(8,128)(2,1)S(1)}) custom-call(f32[4,256,256]{2,1,0:T(8,128)S(1)} %get-tuple-element.32.refs_2_.refs_0_, bf16[112,768]{1,0:T(8,128)(2,1)S(1)} %collective-permute-done.4.refs_1_, bf16[112,768]{1,0:T(8,128)(2,1)S(1)} %collective-permute-done.5.refs_2_, ...), custom_call_target="tpu_custom_call" | custom-call | flops 8000000000 | bytes 8000000 | tf_op jit(solution)/shard_map/pallas_call | solution.py:447
  44.3 3.4 %collective-permute-start.6 = (bf16[88,1024]{1,0:T(8,128)(2,1)S(1)}, bf16[88,1024]{1,0:T(8,128)(2,1)S(1)}, u32[]{:S(2)}, u32[]{:S(2)}) collective-permute-start(bf16[88,1024]{1,0:T(8,128)(2,1)S(1)} %get-tuple-element.46), channel_id=1, source_target_pairs={{1,2},{2,1},{3,4},{4,3},{5,6},{6,5},{7,8},{8,7},{9,10},{10,9},{11,... | collective-permute-start | bytes 540680 | tf_op jit(solution)/shard_map/ppermute | solution.py:465
  47.7 0.3 collective-permute-start.7
  48.0 0.0 collective-permute-done.8.refs_2_
  48.0 0.0 collective-permute-done.9.refs_3_
  48.0 0.0 copy-done.4
  48.0 4.2 %shard_map.93 = (bf16[192,1024]{1,0:T(8,128)(2,1)S(1)}, bf16[256,2048]{1,0:T(8,128)(2,1)S(1)}, bf16[192,1024]{1,0:T(8,128)(2,1)S(1)}, f32[128,1024]{1,0:T(8,128)S(1)}, f32[128,1024]{1,0:T(8,128)S(1)}) custom-call(bf16[256,1024]{1,0:T(8,128)(2,1)S(1)} %get-tuple-element.45.refs_0_.x1_ref, bf16[128,1024]{1,0:T(8,128)(2,1)S(1)} %bitcast.5, ...), custom_call_target="tpu_custom_call" | custom-call | flops 8000000000 | bytes 8000000 | tf_op jit(solution)/shard_map/pallas_call | solution.py:447
  52.2 1.6 %collective-permute-done.6.refs_1_ = bf16[88,1024]{1,0:T(8,128)(2,1)S(1)} collective-permute-done((bf16[88,1024]{1,0:T(8,128)(2,1)S(1)}, bf16[88,1024]{1,0:T(8,128)(2,1)S(1)}, u32[]{:S(2)}, u32[]{:S(2)}) %collective-permute-start.6) | collective-permute-done | bytes 180256 | tf_op jit(solution)/shard_map/ppermute | solution.py:465
  53.8 0.0 collective-permute-done.7.refs_2_
  53.8 8.5 %shard_map.94 = (bf16[192,1024]{1,0:T(8,128)(2,1)S(1)}, bf16[192,1024]{1,0:T(8,128)(2,1)S(1)}, bf16[128,2048]{1,0:T(8,128)(2,1)S(1)}, bf16[48,1024]{1,0:T(8,128)(2,1)S(1)}, bf16[48,1024]{1,0:T(8,128)(2,1)S(1)}) custom-call(f32[3,256,256]{2,1,0:T(8,128)S(1)} %get-tuple-element.35.refs_3_.refs_0_, bf16[88,1024]{1,0:T(8,128)(2,1)S(1)} %collective-permute-done.6.refs_1_, ...), custom_call_target="tpu_custom_call" | custom-call | flops 8000000000 | bytes 8000000 | tf_op jit(solution)/shard_map/pallas_call | solution.py:447
  62.3 3.4 %collective-permute-start.10 = (bf16[48,1024]{1,0:T(8,128)(2,1)S(1)}, bf16[48,1024]{1,0:T(8,128)(2,1)S(1)}, u32[]{:S(2)}, u32[]{:S(2)}) collective-permute-start(bf16[48,1024]{1,0:T(8,128)(2,1)S(1)} %get-tuple-element.60), channel_id=1, source_target_pairs={{1,2},{2,1},{3,4},{4,3},{5,6},{6,5},{7,8},{8,7},{9,10},{10,9},{11,... | collective-permute-start | bytes 294920 | tf_op jit(solution)/shard_map/ppermute | solution.py:465
  65.6 0.1 collective-permute-start.11
  65.7 3.3 %shard_map.95 = (bf16[128,1024]{1,0:T(8,128)(2,1)}, f32[128,1024]{1,0:T(8,128)S(1)}) custom-call(bf16[256,1024]{1,0:T(8,128)(2,1)S(1)} %get-tuple-element.45.refs_0_.x1_ref, bf16[192,1024]{1,0:T(8,128)(2,1)S(1)} %get-tuple-element.53.o_ref, bf16[192,1024]{1,0:T(8,128)(2,1)S(1)} %get-tuple-element.54.dq_ref, bf16[128,2048]{1,0:T(8,128)(2,1)S(1)} %get-tuple-element.55.dkv_ref, ...), custom_call_target="tpu_custom_call" | custom-call | flops 8000000000 | bytes 8000000 | tf_op jit(solution)/shard_map/pallas_call | solution.py:447
  69.0 1.9 %collective-permute-done.10.refs_3_ = bf16[48,1024]{1,0:T(8,128)(2,1)S(1)} collective-permute-done((bf16[48,1024]{1,0:T(8,128)(2,1)S(1)}, bf16[48,1024]{1,0:T(8,128)(2,1)S(1)}, u32[]{:S(2)}, u32[]{:S(2)}) %collective-permute-start.10) | collective-permute-done | bytes 98336 | tf_op jit(solution)/shard_map/ppermute | solution.py:465
  70.9 0.0 collective-permute-done.11.refs_4_
  70.9 1.1 %shard_map.96 = bf16[128,1024]{1,0:T(8,128)(2,1)} custom-call(bf16[256,1024]{1,0:T(8,128)(2,1)S(1)} %get-tuple-element.45.refs_0_.x1_ref, bf16[128,1024]{1,0:T(8,128)(2,1)S(1)} %bitcast.6, f32[128,1024]{1,0:T(8,128)S(1)} %get-tuple-element.59.refs_2_, bf16[48,1024]{1,0:T(8,128)(2,1)S(1)} %collective-permute-done.10.refs_3_, ...), custom_call_target="tpu_custom_call" | custom-call | tf_op jit(solution)/shard_map/pallas_call | solution.py:447
  (1 shorter events, 0.0 us)
Async XLA Ops:
  1.8 11.1 %collective-permute-start = (bf16[80,896]{1,0:T(8,128)(2,1)S(1)}, bf16[80,896]{1,0:T(8,128)(2,1)S(1)}, u32[]{:S(2)}, u32[]{:S(2)}) collective-permute-start(bf16[80,896]{1,0:T(8,128)(2,1)S(1)} %get-tuple-element.34), channel_id=1, source_target_pairs={{0,128},{32,160},{64,192},{96,224},{128,0},{160,32},{192,64},{224,... | collective-permute-start | bytes 430088 | tf_op jit(solution)/shard_map/ppermute | solution.py:459
  9.1 2.2 %copy-start = (bf16[1024,2048]{1,0:T(8,128)(2,1)S(1)}, bf16[1024,2048]{1,0:T(8,128)(2,1)}, u32[]{:S(2)}) copy-start(bf16[1024,2048]{1,0:T(8,128)(2,1)} %wkv_ref.3) | copy-start | bytes 12582916
  11.3 16.6 %copy-start.3 = (bf16[768,1024]{1,0:T(8,128)(2,1)S(1)}, bf16[768,1024]{1,0:T(8,128)(2,1)}, u32[]{:S(2)}) copy-start(bf16[768,1024]{1,0:T(8,128)(2,1)} %refs_3_.2) | copy-start | bytes 4718596
  11.7 16.2 %copy-start.2 = (bf16[1024,1024]{1,0:T(8,128)(2,1)S(1)}, bf16[1024,1024]{1,0:T(8,128)(2,1)}, u32[]{:S(2)}) copy-start(bf16[1024,1024]{1,0:T(8,128)(2,1)} %wq_ref.5) | copy-start | bytes 6291460
  13.0 14.9 %collective-permute-start.2 = (bf16[96,896]{1,0:T(8,128)(2,1)S(1)}, bf16[96,896]{1,0:T(8,128)(2,1)S(1)}, u32[]{:S(2)}, u32[]{:S(2)}) collective-permute-start(bf16[96,896]{1,0:T(8,128)(2,1)S(1)} %get-tuple-element.37), channel_id=1, source_target_pairs={{0,96},{32,64},{64,32},{96,0},{128,224},{160,192},{192,160},{224,1... | collective-permute-start | bytes 516104 | tf_op jit(solution)/shard_map/ppermute | solution.py:459
  13.3 14.6 %collective-permute-start.3 = (bf16[96,896]{1,0:T(8,128)(2,1)S(1)}, bf16[96,896]{1,0:T(8,128)(2,1)S(1)}, u32[]{:S(2)}, u32[]{:S(2)}) collective-permute-start(bf16[96,896]{1,0:T(8,128)(2,1)S(1)} %get-tuple-element.38), channel_id=1, source_target_pairs={{0,32},{32,0},{64,96},{96,64},{128,160},{160,128},{192,224},{224,1... | collective-permute-start | bytes 516104 | tf_op jit(solution)/shard_map/ppermute | solution.py:459
  14.3 13.7 %collective-permute-start.1 = (bf16[96,896]{1,0:T(8,128)(2,1)S(1)}, bf16[96,896]{1,0:T(8,128)(2,1)S(1)}, u32[]{:S(2)}, u32[]{:S(2)}) collective-permute-start(bf16[96,896]{1,0:T(8,128)(2,1)S(1)} %get-tuple-element.36.send_ref), channel_id=1, source_target_pairs={{0,64},{32,96},{64,0},{96,32},{128,192},{160,224},{192,128},{224,1... | collective-permute-start | bytes 516104 | tf_op jit(solution)/shard_map/ppermute | solution.py:459
  17.8 30.2 %collective-permute-start.8 = (bf16[32,1024]{1,0:T(8,128)(2,1)S(1)}, bf16[32,1024]{1,0:T(8,128)(2,1)S(1)}, u32[]{:S(2)}, u32[]{:S(2)}) collective-permute-start(bf16[32,1024]{1,0:T(8,128)(2,1)S(1)} %get-tuple-element.48), channel_id=1, source_target_pairs={{0,32},{32,0},{64,96},{96,64},{128,160},{160,128},{192,224},{224,1... | collective-permute-start | bytes 196616 | tf_op jit(solution)/shard_map/ppermute | solution.py:459
  17.8 14.9 %copy-start.1 = (bf16[1024,2048]{1,0:T(8,128)(2,1)S(1)}, bf16[1024,2048]{1,0:T(8,128)(2,1)}, u32[]{:S(2)}) copy-start(bf16[1024,2048]{1,0:T(8,128)(2,1)} %wkv_ref.3) | copy-start | bytes 12582916
  17.8 30.2 %collective-permute-start.9 = (bf16[32,1024]{1,0:T(8,128)(2,1)S(1)}, bf16[32,1024]{1,0:T(8,128)(2,1)S(1)}, u32[]{:S(2)}, u32[]{:S(2)}) collective-permute-start(bf16[32,1024]{1,0:T(8,128)(2,1)S(1)} %get-tuple-element.49), channel_id=1, source_target_pairs={{32,64},{64,32},{96,128},{128,96},{160,192},{192,160},{33,65},{65,... | collective-permute-start | bytes 196616 | tf_op jit(solution)/shard_map/ppermute | solution.py:465
  28.7 9.5 %collective-permute-start.4 = (bf16[112,768]{1,0:T(8,128)(2,1)S(1)}, bf16[112,768]{1,0:T(8,128)(2,1)S(1)}, u32[]{:S(2)}, u32[]{:S(2)}) collective-permute-start(bf16[112,768]{1,0:T(8,128)(2,1)S(1)} %get-tuple-element.39), channel_id=1, source_target_pairs={{1,2},{2,1},{3,4},{4,3},{5,6},{6,5},{7,8},{8,7},{9,10},{10,9},{11,... | collective-permute-start | bytes 516104 | tf_op jit(solution)/shard_map/ppermute | solution.py:465
  30.6 7.6 %collective-permute-start.5 = (bf16[112,768]{1,0:T(8,128)(2,1)S(1)}, bf16[112,768]{1,0:T(8,128)(2,1)S(1)}, u32[]{:S(2)}, u32[]{:S(2)}) collective-permute-start(bf16[112,768]{1,0:T(8,128)(2,1)S(1)} %get-tuple-element.40), channel_id=1, source_target_pairs={{0,1},{1,0},{2,3},{3,2},{4,5},{5,4},{6,7},{7,6},{8,9},{9,8},{10,11... | collective-permute-start | bytes 516104 | tf_op jit(solution)/shard_map/ppermute | solution.py:459
  32.7 5.5 %copy-start.5 = (bf16[1024,1024]{1,0:T(8,128)(2,1)S(1)}, bf16[1024,1024]{1,0:T(8,128)(2,1)}, u32[]{:S(2)}) copy-start(bf16[1024,1024]{1,0:T(8,128)(2,1)} %wo_ref.1) | copy-start | bytes 6291460
  38.2 9.8 %copy-start.4 = (bf16[16,8,1024]{2,1,0:T(8,128)(2,1)S(1)}, bf16[16,8,1024]{2,1,0:T(8,128)(2,1)}, u32[]{:S(2)}) copy-start(bf16[16,8,1024]{2,1,0:T(8,128)(2,1)} %param.13) | copy-start | bytes 786436
  44.3 9.5 %collective-permute-start.6 = (bf16[88,1024]{1,0:T(8,128)(2,1)S(1)}, bf16[88,1024]{1,0:T(8,128)(2,1)S(1)}, u32[]{:S(2)}, u32[]{:S(2)}) collective-permute-start(bf16[88,1024]{1,0:T(8,128)(2,1)S(1)} %get-tuple-element.46), channel_id=1, source_target_pairs={{1,2},{2,1},{3,4},{4,3},{5,6},{6,5},{7,8},{8,7},{9,10},{10,9},{11,... | collective-permute-start | bytes 540680 | tf_op jit(solution)/shard_map/ppermute | solution.py:465
  47.7 6.1 %collective-permute-start.7 = (bf16[88,1024]{1,0:T(8,128)(2,1)S(1)}, bf16[88,1024]{1,0:T(8,128)(2,1)S(1)}, u32[]{:S(2)}, u32[]{:S(2)}) collective-permute-start(bf16[88,1024]{1,0:T(8,128)(2,1)S(1)} %get-tuple-element.47), channel_id=1, source_target_pairs={{0,1},{1,0},{2,3},{3,2},{4,5},{5,4},{6,7},{7,6},{8,9},{9,8},{10,11... | collective-permute-start | bytes 540680 | tf_op jit(solution)/shard_map/ppermute | solution.py:459
  62.3 8.6 %collective-permute-start.10 = (bf16[48,1024]{1,0:T(8,128)(2,1)S(1)}, bf16[48,1024]{1,0:T(8,128)(2,1)S(1)}, u32[]{:S(2)}, u32[]{:S(2)}) collective-permute-start(bf16[48,1024]{1,0:T(8,128)(2,1)S(1)} %get-tuple-element.60), channel_id=1, source_target_pairs={{1,2},{2,1},{3,4},{4,3},{5,6},{6,5},{7,8},{8,7},{9,10},{10,9},{11,... | collective-permute-start | bytes 294920 | tf_op jit(solution)/shard_map/ppermute | solution.py:465
  65.6 5.2 %collective-permute-start.11 = (bf16[48,1024]{1,0:T(8,128)(2,1)S(1)}, bf16[48,1024]{1,0:T(8,128)(2,1)S(1)}, u32[]{:S(2)}, u32[]{:S(2)}) collective-permute-start(bf16[48,1024]{1,0:T(8,128)(2,1)S(1)} %get-tuple-element.61), channel_id=1, source_target_pairs={{0,1},{1,0},{2,3},{3,2},{4,5},{5,4},{6,7},{7,6},{8,9},{9,8},{10,11... | collective-permute-start | bytes 294920 | tf_op jit(solution)/shard_map/ppermute | solution.py:459
